TPU v7x, 32 devices: a whole 2x2x4 slice. The times are simulated.
32 devices in a mesh: req: 4 (over y, x), hid: 8 (over z, core).
Axes of the slice: x: 2, y: 2, z: 4, core: 2. Of those that a mesh axis runs over, the one named last changes fastest.
Arguments:
- tokens: bfloat16 [1024, 7168], P(('req', 'hid')), may hold values from -90 to 90
- gain_in: float32 [7168], replicated, may hold values from 0.25 to 1.75
- w_qkv: bfloat16 [7168, 3, 1792], P(None, None, 'hid'), may hold values from -0.0625 to 0.0625
- adapt_down: bfloat16 [7168, 128], replicated, may hold values from -0.0625 to 0.0625
- adapt_up: bfloat16 [128, 1792], P(None, 'hid'), may hold values from -0.5 to 0.5
- w_out: bfloat16 [1792, 3584], P('hid'), may hold values from -0.125 to 0.125
- gain_ff: float32 [3584], replicated, may hold values from 0.25 to 1.75
- w_gate_up: bfloat16 [3584, 2, 14336], P(None, None, 'hid'), may hold values from -0.09375 to 0.09375
- w_down: bfloat16 [14336, 3584], P('hid'), may hold values from -0.046875 to 0.046875
- prefix_cache: bfloat16 [4, 512, 2, 1792], P('req', 'hid'), may hold values from -330 to 330
- prefix_owner: int32 [3], replicated, may hold values from 0 to 3, as said below
- group_prefix: int32 [4], replicated, may hold values from 0 to 2, as said below
- lengths: int32 [4, 6], P('req'), may hold values from 1 to 128, 256 in all within a row
Outputs:
- attn_out: bfloat16 [1024, 3584], P(('req', 'hid'))
- block_out: bfloat16 [1024, 3584], P(('req', 'hid'))
Inputs may be any that keep to these rules, and one draw needn't show every extreme that they name: `prefix_owner`: the 3 prefixes have different owners. `group_prefix`: every prefix is extended by at least one group. Each group's 6 lengths sum to 256, and the longest of each group is exactly 128.
All inputs are finite; a program needn't handle non-finite values.
Results may differ from a plain program's by a relative error of at most 0.035.
Values may be sent and summed in bfloat16 or wider, within the bound.
No kernel may reach another device: no remote copies, remote signals or barrier semaphores. Data moves between devices by JAX's collectives and lax.ppermute only.
A program may use at most 128 MiB of HBM per device.

v0:
```python
import jax
import jax.numpy as jnp
from jax import lax
from jax.sharding import PartitionSpec as P

HD = 224


EPS = 1e-05


def rms_scale(matrix, gain_vec):
    return matrix * lax.rsqrt(jnp.mean(matrix * matrix, axis=-1, keepdims=True) + EPS) * gain_vec


def prefix_part(queries, kv_block):
    span_len = kv_block.shape[0]
    head_count = queries.shape[1]
    head_size = queries.shape[2]
    cached_k = kv_block[:, 0].reshape(span_len, head_count, head_size)
    cached_v = kv_block[:, 1].reshape(span_len, head_count, head_size)
    scores = jnp.einsum(
        "thd,phd->htp", queries, cached_k, preferred_element_type=jnp.float32
    ) * head_size ** (-0.5)
    row_max = jnp.max(scores, axis=-1)
    expos = jnp.exp(scores - row_max[..., None])
    row_sum = jnp.sum(expos, axis=-1)
    weighted = jnp.einsum(
        "htp,phd->htd", expos.astype(jnp.bfloat16), cached_v, preferred_element_type=jnp.float32
    )
    return (row_max, row_sum, weighted)


def suffix_part(queries, suffix_keys, suffix_vals, allowed):
    head_size = queries.shape[2]
    scores = jnp.einsum(
        "thd,shd->hts", queries, suffix_keys, preferred_element_type=jnp.float32
    ) * head_size ** (-0.5)
    scores = jnp.where(allowed[None], scores, -jnp.inf)
    row_max = jnp.max(scores, axis=-1)
    expos = jnp.exp(scores - row_max[..., None])
    row_sum = jnp.sum(expos, axis=-1)
    weighted = jnp.einsum(
        "hts,shd->htd", expos.astype(jnp.bfloat16), suffix_vals, preferred_element_type=jnp.float32
    )
    return (row_max, row_sum, weighted)


def combine(first_part, second_part):
    joint_max = jnp.maximum(first_part[0], second_part[0])
    first_factor = jnp.exp(first_part[0] - joint_max)
    second_factor = jnp.exp(second_part[0] - joint_max)
    joint_sum = first_part[1] * first_factor + second_part[1] * second_factor
    joint_acc = first_part[2] * first_factor[..., None] + second_part[2] * second_factor[..., None]
    return (joint_max, joint_sum, joint_acc)


def per_device(
    tokens,
    gain_in,
    w_qkv,
    adapt_down,
    adapt_up,
    w_out,
    gain_ff,
    w_gate_up,
    w_down,
    prefix_cache,
    prefix_owner,
    group_prefix,
    lengths,
):
    tok_dev = tokens.shape[0]
    width_in = tokens.shape[1]
    head_cols = w_qkv.shape[2]
    head_count = head_cols // HD
    model_width = w_out.shape[1]
    normed = rms_scale(tokens.astype(jnp.float32), gain_in).astype(jnp.bfloat16)
    latent = jnp.dot(normed, adapt_down, preferred_element_type=jnp.float32).astype(jnp.bfloat16)
    row_block = jnp.concatenate([normed, latent], axis=1)
    joint_weight = w_qkv.reshape(width_in, 3 * head_cols)
    shard_rows = lax.all_gather(row_block, "hid", axis=0, tiled=True)
    joint = jnp.dot(shard_rows[:, :width_in], joint_weight, preferred_element_type=jnp.float32)
    query_part = joint[:, :head_cols] + jnp.dot(
        shard_rows[:, width_in:], adapt_up, preferred_element_type=jnp.float32
    )
    projected = jnp.concatenate([query_part, joint[:, head_cols:]], axis=1).astype(jnp.bfloat16)
    tok_grp = projected.shape[0]
    queries = projected[:, :head_cols].reshape(tok_grp, head_count, HD)
    suffix_keys = projected[:, head_cols : 2 * head_cols].reshape(tok_grp, head_count, HD)
    suffix_vals = projected[:, 2 * head_cols :].reshape(tok_grp, head_count, HD)
    request_ends = jnp.cumsum(lengths[0])
    position = jnp.arange(tok_grp, dtype=jnp.int32)
    request = jnp.sum((position[:, None] >= request_ends[None, :]).astype(jnp.int32), axis=1)
    allowed = jnp.logical_and(
        request[:, None] == request[None, :], position[None, :] <= position[:, None]
    )
    partial_value = suffix_part(queries, suffix_keys, suffix_vals, allowed)
    group_index = lax.axis_index("req")
    target = prefix_owner[group_prefix[group_index]]
    heads_cache = lax.all_to_all(prefix_cache[0], "hid", split_axis=2, concat_axis=0, tiled=True)
    span_len = heads_cache.shape[0]
    shard_rows = lax.all_gather(heads_cache, "req", axis=0, tiled=True)
    slot_count = shard_rows.shape[0] // span_len
    inside = jnp.logical_and(target >= 0, target < slot_count)
    chosen = lax.dynamic_slice_in_dim(
        shard_rows, jnp.clip(target, 0, slot_count - 1) * span_len, span_len, 0
    )
    partial_value = lax.cond(
        inside,
        lambda kept: combine(kept, prefix_part(queries, chosen)),
        lambda kept: kept,
        partial_value,
    )
    heads_out = (partial_value[2] / partial_value[1][..., None]).astype(jnp.bfloat16)
    out_weight = w_out.reshape(head_count, HD, model_width)
    projected_out = jnp.einsum(
        "htd,hdm->tm", heads_out, out_weight, preferred_element_type=jnp.float32
    )
    summed = lax.psum(projected_out.astype(jnp.bfloat16), "hid").astype(jnp.float32)
    hid_index = lax.axis_index("hid")
    attn_out = lax.dynamic_slice_in_dim(summed, hid_index * tok_dev, tok_dev, 0).astype(
        jnp.bfloat16
    )
    ff_in = rms_scale(summed, gain_ff).astype(jnp.bfloat16)
    unit_count = w_gate_up.shape[2]
    gate_up = jnp.dot(
        ff_in, w_gate_up.reshape(model_width, 2 * unit_count), preferred_element_type=jnp.float32
    )
    hidden = (jax.nn.silu(gate_up[:, :unit_count]) * gate_up[:, unit_count:]).astype(jnp.bfloat16)
    block_out = lax.psum_scatter(
        jnp.dot(hidden, w_down, preferred_element_type=jnp.float32).astype(jnp.bfloat16),
        "hid",
        scatter_dimension=0,
        tiled=True,
    )
    return (attn_out, block_out)


def solution(mesh):
    placed = (
        P(("req", "hid"), None),
        P(),
        P(None, None, "hid"),
        P(),
        P(None, "hid"),
        P("hid", None),
        P(),
        P(None, None, "hid"),
        P("hid", None),
        P("req", "hid", None, None),
        P(),
        P(),
        P("req", None),
    )
    return jax.shard_map(
        per_device,
        mesh=mesh,
        in_specs=placed,
        out_specs=(P(("req", "hid"), None), P(("req", "hid"), None)),
        check_vma=False,
    )
```

profile of v0, /device:TPU:0, one launch (start us, length us, event | category | flops | bytes accessed | tf_op | source)
XLA Modules:
  0.0 235.9 jit_solution(2696729063100563315)
XLA Ops:
  7.2 0.0 copy-start
  7.2 0.0 all-gather.3.cloned.1.call-start
  7.2 1.3 fusion.19
  8.6 0.0 copy-start.3
  8.6 1.3 fusion.21
  9.9 0.4 convolution_convert_fusion.2
  10.3 0.8 pad_maximum_fusion
  11.1 0.0 all-gather.3.cloned.1.call-update
  11.1 0.0 all-gather.5.cloned.1.call-start
  11.2 1.3 copy.30
  12.5 0.7 bitcast_bitcast_fusion
  13.2 0.6 reshape.147
  13.8 0.0 copy-start.6
  13.8 0.0 copy-start.7
  13.8 0.0 copy-start.8
  13.8 31.0 %all_to_all.18 = bf16[8,2,14336]{2,1,0:T(2,128)(2,1)S(1)} all-to-all(bf16[8,2,14336]{2,1,0:T(2,128)(2,1)S(1)} %reshape.147), channel_id=1, replica_groups=mesh['req'=4,'hid'=8] {'hid'}, dimensions={0} | all-to-all | bytes 917504 | tf_op jit(solution)/shard_map/all_to_all | solution.py:101
  44.8 0.6 reshape.148
  45.4 2.0 copy.31
  47.4 0.0 all-gather.5.cloned.1.call-update
  47.5 0.0 all-reduce.2.cloned.1.call-start
  47.5 0.6 dynamic_slice.17
  50.1 0.6 dynamic_slice.18
  52.0 0.2 reduce-window.8
  52.1 0.1 convert_reduce_fusion
  52.2 13.7 %all-gather.3.cloned.1.call-done = bf16[256,7296]{1,0:T(8,128)(2,1)} async-done(((bf16[32,7296]{1,0:T(8,128)(2,1)}), bf16[256,7296]{1,0:T(8,128)(2,1)}) %all-gather.3.cloned.1.call-update) | async-done | bytes 3735568 | tf_op jit(solution)/shard_map/all_gather | solution.py:82
  65.9 6.4 %fusion.37 = (bf16[256,672]{0,1:T(8,128)(2,1)S(1)}, f32[256,672]{0,1:T(8,128)S(1)}) fusion(bf16[7168,672]{0,1:T(8,128)(2,1)} %bitcast.57, bf16[256,7296]{1,0:T(8,128)(2,1)} %all-gather.3.cloned.1.call-done), kind=kOutput, calls=%fused_computation.61 | convolution fusion | flops 2466422784 | bytes 14336000 | tf_op jit(solution)/shard_map/dot_general | solution.py:83
  72.4 1.0 fusion.18
  73.4 0.2 fusion.38
  73.7 0.1 fusion.26
  73.7 0.2 convolution_bitcast_fusion
  73.9 27.9 %all-gather.5.cloned.1.call-done = bf16[2048,2,224]{2,0,1:T(8,128)(2,1)} async-done(((bf16[512,2,224]{2,0,1:T(8,128)(2,1)}), bf16[2048,2,224]{2,0,1:T(8,128)(2,1)}) %all-gather.5.cloned.1.call-update) | async-done | bytes 1835024 | tf_op jit(solution)/shard_map/all_gather | solution.py:103
  101.8 7.4 %conditional.1 = ((f32[1,256]{1,0:T(1,128)S(1)}, f32[1,256,224]{1,2,0:T(8,128)S(1)})) conditional(s32[]{:T(128)} %convert_element_type.48, (f32[1,256]{1,0:T(1,128)S(1)}, f32[1,256,224]{1,2,0:T(8,128)S(1)}) %tuple.49, (s32[]{:T(128)}, bf16[2048,2,224]{2,0,1:T(8,128)(2,1)}, bf16[256,224]{0,1:T(8,128)(2,1)S(1)}, f32[256]{0:T(256)S(1)}, ...), branch_computations={%region_5.6_spmd, %region_6.9_spmd} | conditional | flops 118400008 | bytes 6291574 | solution.py:109
  102.6 3.9 %copy.32 = bf16[2048,2,224]{0,2,1:T(8,128)(2,1)} copy(bf16[2048,2,224]{2,0,1:T(8,128)(2,1)} %get-tuple-element.113) | data formatting | bytes 3670016 | tf_op jit(solution)/shard_map
  106.6 1.2 fusion.36
  107.8 0.1 fusion.3
  107.9 1.3 fusion.1
  109.3 1.9 convolution_convert_fusion.1
  111.2 0.0 all-reduce.2.cloned.1.call-update
  111.2 0.2 reduce-scatter.2.cloned.1.call-start
  111.5 23.9 %copy.35 = bf16[448,8,2,1792]{3,1,2,0:T(8,128)(2,1)} copy(bf16[448,8,2,1792]{3,2,1,0:T(2,128)(2,1)} %bitcast.46) | data formatting | bytes 51380224
  135.3 39.2 %all-reduce.2.cloned.1.call-done = bf16[256,3584]{1,0:T(8,128)(2,1)} async-done(((bf16[256,3584]{1,0:T(8,128)(2,1)}), bf16[256,3584]{1,0:T(8,128)(2,1)}) %all-reduce.2.cloned.1.call-update) | async-done | bytes 1835024 | tf_op jit(solution)/shard_map/psum | solution.py:120
  174.6 2.1 multiply_reduce_fusion
  176.7 0.0 slice-start.1
  176.7 12.5 %fusion.12 = f32[256,3584]{1,0:T(8,128)S(1)} fusion(bf16[3584,3584]{1,0:T(8,128)(2,1)} %bitcast.47, f32[3584]{0:T(1024)S(1)} %copy-done.5, f32[256]{0:T(256)S(1)} %add_rsqrt_fusion, bf16[256,3584]{1,0:T(8,128)(2,1)} %all-reduce.2.cloned.1.call-done), kind=kOutput, calls=%fused_computation.23 | convolution fusion | flops 6580338688 | bytes 31210496 | tf_op jit(solution)/shard_map/dot_general | solution.py:127
  189.4 5.3 %convolution_convert_fusion = bf16[256,3584]{1,0:T(8,128)(2,1)} fusion(bf16[1792,3584]{1,0:T(8,128)(2,1)S(1)} %bitcast.56, f32[256,3584]{1,0:T(8,128)S(1)} %fusion.12), kind=kOutput, calls=%fused_computation.17 | convolution fusion | flops 3292004352 | bytes 18350080 | tf_op jit(solution)/shard_map/dot_general | solution.py:132
  194.6 0.0 reduce-scatter.2.cloned.1.call-update
  194.7 1.6 dynamic-slice_convert_fusion
  196.3 33.0 %reduce-scatter.2.cloned.1.call-done = bf16[32,3584]{1,0:T(8,128)(2,1)} async-done(((bf16[256,3584]{1,0:T(8,128)(2,1)}), bf16[32,3584]{1,0:T(8,128)(2,1)}) %reduce-scatter.2.cloned.1.call-update) | async-done | bytes 229392 | tf_op jit(solution)/shard_map/reduce_scatter | solution.py:131
  (25 shorter events, 0.1 us)
Async XLA Ops:
  7.2 2.7 %copy-start = (bf16[7168,128]{1,0:T(8,128)(2,1)S(1)}, bf16[7168,128]{1,0:T(8,128)(2,1)}, u32[]{:S(2)}) copy-start(bf16[7168,128]{1,0:T(8,128)(2,1)} %param.18) | copy-start | bytes 5505028
  7.2 58.7 %all-gather.3.cloned.1.call-start = ((), (), s32[]{:S(2)}) async-start(), calls=%async_computation.2 | async-start | bytes 4202496 | tf_op jit(solution)/shard_map/all_gather | solution.py:82
  8.6 2.6 %copy-start.3 = (bf16[1,64,2,1792]{3,2,1,0:T(2,128)(2,1)S(1)}, bf16[1,64,2,1792]{3,2,1,0:T(2,128)(2,1)}, u32[]{:S(2)}) copy-start(bf16[1,64,2,1792]{3,2,1,0:T(2,128)(2,1)} %param.24) | copy-start | bytes 1376260
  11.1 90.7 %all-gather.5.cloned.1.call-start = ((), (), s32[]{:S(2)}) async-start(), calls=%async_computation.3 | async-start | bytes 2621440 | tf_op jit(solution)/shard_map/all_gather | solution.py:103
  13.8 33.7 %copy-start.6 = (s32[4]{0:T(128)S(1)}, s32[4]{0:T(128)}, u32[]{:S(2)}) copy-start(s32[4]{0:T(128)} %param.26) | copy-start | bytes 52
  13.8 36.2 %copy-start.7 = (s32[3]{0:T(128)S(1)}, s32[3]{0:T(128)}, u32[]{:S(2)}) copy-start(s32[3]{0:T(128)} %param.25) | copy-start | bytes 40
  13.8 38.1 %copy-start.8 = (s32[1,6]{1,0:T(1,128)S(1)}, s32[1,6]{1,0:T(1,128)}, u32[]{:S(2)}) copy-start(s32[1,6]{1,0:T(1,128)} %param.27) | copy-start | bytes 76
  47.5 127.1 %all-reduce.2.cloned.1.call-start = ((), (), s32[]{:S(2)}) async-start(), calls=%async_computation.4 | async-start | bytes 3670016 | tf_op jit(solution)/shard_map/psum | solution.py:120
  65.9 6.4 %copy-start.4 = (bf16[128,224]{0,1:T(8,128)(2,1)S(1)}, bf16[128,224]{0,1:T(8,128)(2,1)}, u32[]{:S(2)}) copy-start(bf16[128,224]{0,1:T(8,128)(2,1)} %param.19) | copy-start | bytes 172036
  101.8 7.4 %copy-start.2 = (bf16[224,3584]{1,0:T(8,128)(2,1)S(1)}, bf16[224,3584]{1,0:T(8,128)(2,1)}, u32[]{:S(2)}) copy-start(bf16[224,3584]{1,0:T(8,128)(2,1)} %param.20) | copy-start | bytes 4816900
  111.2 118.1 %reduce-scatter.2.cloned.1.call-start = ((), (), s32[]{:S(2)}) async-start(), calls=%async_computation.5 | async-start | bytes 2064384 | tf_op jit(solution)/shard_map/reduce_scatter | solution.py:131
  111.4 65.3 %copy-start.5 = (f32[3584]{0:T(1024)S(1)}, f32[3584]{0:T(1024)}, u32[]{:S(2)}) copy-start(f32[3584]{0:T(1024)} %param.21) | copy-start | bytes 43012
  174.6 14.7 %slice-start = ((s8[12845056]{0:T(1024)(128)(4,1)}), s8[4194304]{0:T(1024)(128)(4,1)S(1)}, s32[]{:S(2)}) async-start(s8[12845056]{0:T(1024)(128)(4,1)} %bitcast.55), calls=%async_computation.6 | async-start | bytes 8388608
  176.7 12.6 %slice-start.1 = ((s8[12845056]{0:T(1024)(128)(4,1)}), s8[4194304]{0:T(1024)(128)(4,1)S(1)}, s32[]{:S(2)}) async-start(s8[12845056]{0:T(1024)(128)(4,1)} %bitcast.55), calls=%async_computation.7 | async-start | bytes 8388608
  176.7 12.6 %slice-start.2 = ((s8[12845056]{0:T(1024)(128)(4,1)}), s8[4194304]{0:T(1024)(128)(4,1)S(1)}, s32[]{:S(2)}) async-start(s8[12845056]{0:T(1024)(128)(4,1)} %bitcast.55), calls=%async_computation.8 | async-start | bytes 8388608
  176.7 12.6 %slice-start.3 = ((s8[12845056]{0:T(1024)(128)(4,1)}), s8[262144]{0:T(1024)(128)(4,1)S(1)}, s32[]{:S(2)}) async-start(s8[12845056]{0:T(1024)(128)(4,1)} %bitcast.55), calls=%async_computation.9 | async-start | bytes 524288
  189.3 40.0 %copy-start.1 = (bf16[7168,128]{1,0:T(8,128)(2,1)S(1)}, bf16[7168,128]{1,0:T(8,128)(2,1)}, u32[]{:S(2)}) copy-start(bf16[7168,128]{1,0:T(8,128)(2,1)} %param.18) | copy-start | bytes 5505028
Sparse Core Ops, SparseCore 0:
  11.3 54.6 all-gather.2
  67.8 34.0 all-gather.4
  111.3 63.2 all-reduce.1
  194.8 34.5 reduce-scatter.1
where the time goes:
time: 237 us; the launch traced here: 236 us
  waiting for transfers between devices  114 us (48%)
  local copies, waits for them, and re-layouts  35.9 us (15%)
  blocking collectives  31 us (13%)
  matrix products  30.6 us (13%)
  between operations  17.3 us (7%)
  other arithmetic  6.02 us (3%)
    psum x1, waiting for transfers between devices, per_device(): lax.psum(projected_out.astype(jnp.bfloat16), 'hid').astype(jnp.float32)  39.2 us
    reduce_scatter x1, waiting for transfers between devices, per_device(): lax.psum_scatter(jnp.dot(hidden, w_down, preferred_element_type=jnp.float...  33 us
    all_to_all x1, blocking collectives, per_device(): lax.all_to_all(prefix_cache[0], 'hid', split_axis=2, concat_axis=0, tiled...  31 us
    all_gather x1, waiting for transfers between devices, per_device(): shard_rows = lax.all_gather(heads_cache, 'req', axis=0, tiled=True)  27.9 us
    unnamed x31, local copies, waits for them, and re-layouts  27.1 us
    all_gather x1, waiting for transfers between devices, per_device(): shard_rows = lax.all_gather(row_block, 'hid', axis=0, tiled=True)  13.7 us
    dot_general x1, matrix products, per_device(): jnp.dot(ff_in, w_gate_up.reshape(model_width, 2 * unit_count), preferred_...  12.5 us
    dot_general x1, matrix products, per_device(): jnp.dot(shard_rows[:, :width_in], joint_weight, preferred_element_type=jn...  6.43 us
  transfers between devices with their start and end apart: 4, of which 4 were waited for; matrix products, arithmetic and copies ran while one was open for 17% of the time, Pallas kernels for 0%

commit v1 on v0

v1 whole, which is shorter than its diff:
```python
import jax
import jax.numpy as jnp
from jax import lax
from jax.sharding import PartitionSpec as P

HD = 224
EPS = 1e-05
F32 = jnp.float32
BF16 = jnp.bfloat16


def ring_order(n):
    half = n // 2
    return [2 * q for q in range(half)] + [2 * (n - 1 - q) + 1 for q in range(half, n)]


def ring_steps(n):
    order = ring_order(n)
    fwd = [(order[i], order[(i + 1) % n]) for i in range(n)]
    bwd = [(order[i], order[(i - 1) % n]) for i in range(n)]
    return fwd, bwd


def split_cols(block, count):
    width = block.shape[1] // count
    return [block[:, i * width : (i + 1) * width] for i in range(count)]


def ring_gather(block, n, count):
    fwd, bwd = ring_steps(n)
    own = split_cols(block, count)
    slots = [None] * n
    slots[0] = own
    ahead, behind = list(own), list(own)
    for step in range(1, n // 2 + 1):
        ahead = [lax.ppermute(v, "hid", fwd) for v in ahead]
        slots[step] = list(ahead)
        if step < n // 2:
            behind = [lax.ppermute(v, "hid", bwd) for v in behind]
            slots[n - step] = list(behind)
    return jnp.concatenate([jnp.concatenate(s, axis=1) for s in slots], axis=0)


def ring_scatter(partial, n, count):
    fwd, bwd = ring_steps(n)
    rows = partial.shape[0] // n
    out = []
    for part in split_cols(partial, count):
        slot = lambda k: part[(k % n) * rows : (k % n + 1) * rows]
        ahead = slot(n // 2)
        for k in range(n // 2 + 1, n + 1):
            ahead = lax.ppermute(ahead.astype(BF16), "hid", fwd).astype(F32)
            if k < n:
                ahead = ahead + slot(k)
        behind = slot(n // 2 - 1)
        for k in range(n // 2 - 2, -1, -1):
            behind = lax.ppermute(behind.astype(BF16), "hid", bwd).astype(F32)
            if k > 0:
                behind = behind + slot(k)
        out.append(ahead + behind + slot(0))
    return jnp.concatenate(out, axis=1)


def rms_scale(matrix, gain_vec):
    return matrix * lax.rsqrt(jnp.mean(matrix * matrix, axis=-1, keepdims=True) + EPS) * gain_vec


def make(mesh):
    n = mesh.shape["hid"]
    n_req = mesh.shape["req"]
    half = n // 2

    def per_device(tokens, gain_in, w_qkv, adapt_down, adapt_up, w_out, gain_ff, w_gate_up, w_down,
                   prefix_cache, prefix_owner, group_prefix, lengths):
        tok_dev, width_in = tokens.shape
        cols = w_qkv.shape[2]
        model_width = w_out.shape[1]
        hid = lax.axis_index("hid")
        core = hid % 2
        chip = hid // 2
        place = jnp.where(core == 0, chip, n - 1 - chip)

        cache = prefix_cache[0].reshape(-1, 2, half, 2, cols)
        mine = lax.dynamic_index_in_dim(cache, core, 3, keepdims=False)
        other = lax.dynamic_index_in_dim(cache, 1 - core, 3, keepdims=False)
        both = [(h, h ^ 1) for h in range(n)]
        got = lax.ppermute(other, "hid", both)
        cache = jnp.concatenate([mine, got], axis=0)
        blocks = [lax.dynamic_index_in_dim(cache, chip, 2, keepdims=False)]
        for k in range(1, half):
            block = lax.dynamic_index_in_dim(cache, chip ^ k, 2, keepdims=False)
            blocks.append(lax.ppermute(block, "hid", [(h, h ^ (2 * k)) for h in range(n)]))
        heads_cache = jnp.concatenate(blocks, axis=0)

        normed = rms_scale(tokens.astype(F32), gain_in).astype(BF16)
        rows_in = ring_gather(normed, n, 2)

        req = lax.axis_index("req")
        target = prefix_owner[group_prefix[req]]
        away = target ^ req
        chosen = heads_cache
        for k in range(1, n_req):
            seen = lax.ppermute(heads_cache, "req", [(r, r ^ k) for r in range(n_req)])
            chosen = jnp.where(away == k, seen, chosen)

        latent = jnp.dot(rows_in, adapt_down, preferred_element_type=F32).astype(BF16)
        joint = jnp.dot(rows_in, w_qkv.reshape(width_in, 3 * cols), preferred_element_type=F32)
        queries = (joint[:, :cols] + jnp.dot(latent, adapt_up, preferred_element_type=F32)).astype(BF16)
        keys = joint[:, cols : 2 * cols].astype(BF16)
        vals = joint[:, 2 * cols :].astype(BF16)
        tok_grp = rows_in.shape[0]
        spot = (place - jnp.arange(n, dtype=jnp.int32)) % n
        owner = jnp.where(spot < half, 2 * spot, 2 * (n - 1 - spot) + 1)
        position = (owner[:, None] * tok_dev + jnp.arange(tok_dev, dtype=jnp.int32)[None, :]).reshape(-1)
        ends = jnp.cumsum(lengths[0])
        request = jnp.sum((position[:, None] >= ends[None, :]).astype(jnp.int32), axis=1)
        allowed = jnp.logical_and(request[:, None] == request[None, :], position[None, :] <= position[:, None])
        nt = (((1,), (1,)), ((), ()))
        scale = HD ** (-0.5)
        pre = lax.dot_general(queries, chosen[:, 0], nt, preferred_element_type=F32) * scale
        suf = lax.dot_general(queries, keys, nt, preferred_element_type=F32) * scale
        suf = jnp.where(allowed, suf, -jnp.inf)
        top = jnp.maximum(jnp.max(pre, axis=1), jnp.max(suf, axis=1))[:, None]
        pre = jnp.exp(pre - top)
        suf = jnp.exp(suf - top)
        total = jnp.sum(pre, axis=1) + jnp.sum(suf, axis=1)
        weighted = jnp.dot(pre.astype(BF16), chosen[:, 1], preferred_element_type=F32) + jnp.dot(
            suf.astype(BF16), vals, preferred_element_type=F32
        )
        heads_out = (weighted / total[:, None]).astype(BF16)
        partial = jnp.dot(heads_out, w_out, preferred_element_type=F32)
        attn_own = ring_scatter(partial, n, 2).astype(BF16)
        summed = ring_gather(attn_own, n, 2).astype(F32)

        ff_in = rms_scale(summed, gain_ff).astype(BF16)
        units = w_gate_up.shape[2]
        gate_up = jnp.dot(ff_in, w_gate_up.reshape(model_width, 2 * units), preferred_element_type=F32)
        hidden = (jax.nn.silu(gate_up[:, :units]) * gate_up[:, units:]).astype(BF16)
        down = jnp.dot(hidden, w_down, preferred_element_type=F32)
        block_own = ring_scatter(down, n, 2).astype(BF16)
        return attn_own, block_own

    return per_device


def solution(mesh):
    placed = (
        P(("req", "hid"), None),
        P(),
        P(None, None, "hid"),
        P(),
        P(None, "hid"),
        P("hid", None),
        P(),
        P(None, None, "hid"),
        P("hid", None),
        P("req", "hid", None, None),
        P(),
        P(),
        P("req", None),
    )
    return jax.shard_map(
        make(mesh),
        mesh=mesh,
        in_specs=placed,
        out_specs=(P(("req", "hid"), None), P(("req", "hid"), None)),
        check_vma=False,
    )
```

time: 237 us -> 217 us (0.916)
  starting transfers between devices: 0.35 us -> 74.3 us
  waiting for transfers between devices: 114 us -> 56 us
  blocking collectives: 31 us -> 0 us
  other arithmetic: 6.02 us -> 20.2 us
  between operations: 17.3 us -> 3.48 us
  local copies, waits for them, and re-layouts: 35.9 us -> 30.7 us
    ppermute x0 -> x63, starting transfers between devices: none -> 74.3 us  [the longest x16 37.2 us: ring_gather(): ahead = [lax.ppermute(v, 'hid', fwd) for v in ahead]]
    ppermute x0 -> x63, waiting for transfers between devices: none -> 56 us  [the longest x16 19.2 us: ring_scatter(): ahead = lax.ppermute(ahead.astype(BF16), 'hid', fwd).astype(F32)]
    all_gather x2 -> x0, waiting for transfers between devices: 41.6 us -> none  [the longest x1 27.9 us: per_device(): shard_rows = lax.all_gather(heads_cache, 'req', axis=0, tiled=True)]
    psum x1 -> x0, waiting for transfers between devices: 39.2 us -> none  [per_device(): lax.psum(projected_out.astype(jnp.bfloat16), 'hid').astype(jnp.float32)]
    reduce_scatter x1 -> x0, waiting for transfers between devices: 33 us -> none  [per_device(): lax.psum_scatter(jnp.dot(hidden, w_down, preferred_element_type=jnp.float...]
    all_to_all x1 -> x0, blocking collectives: 31 us -> none  [per_device(): lax.all_to_all(prefix_cache[0], 'hid', split_axis=2, concat_axis=0, tiled...]
    unnamed x1 -> x15, other arithmetic: 0.01 us -> 9.63 us
    unnamed x31 -> x23, local copies, waits for them, and re-layouts: 27.1 us -> 23.9 us
  transfers between devices with their start and end apart: 4 -> 63, of which waited for: 4 -> 26; matrix products, arithmetic and copies ran while one was open for 17% -> 17% of each run, Pallas kernels for 0% -> 0%
where the time goes in v1:
time: 217 us; the launch traced here: 216 us
  starting transfers between devices  74.3 us (34%)
  waiting for transfers between devices  56 us (26%)
  matrix products  31.3 us (14%)
  local copies, waits for them, and re-layouts  30.7 us (14%)
  other arithmetic  20.2 us (9%)
  between operations  3.48 us (2%)
    ppermute x16, starting transfers between devices, ring_gather(): ahead = [lax.ppermute(v, 'hid', fwd) for v in ahead]  37.2 us
    ppermute x16, starting transfers between devices, ring_scatter(): ahead = lax.ppermute(ahead.astype(BF16), 'hid', fwd).astype(F32)  26.9 us
    unnamed x23, local copies, waits for them, and re-layouts  23.9 us
    ppermute x16, waiting for transfers between devices, ring_scatter(): ahead = lax.ppermute(ahead.astype(BF16), 'hid', fwd).astype(F32)  19.2 us
    ppermute x3, waiting for transfers between devices, per_device(): seen = lax.ppermute(heads_cache, 'req', [(r, r ^ k) for r in range(n_req)])  12.5 us
    dot_general x1, matrix products, per_device(): jnp.dot(ff_in, w_gate_up.reshape(model_width, 2 * units), preferred_eleme...  12.1 us
    ppermute x12, waiting for transfers between devices, ring_scatter(): behind = lax.ppermute(behind.astype(BF16), 'hid', bwd).astype(F32)  10.1 us
    unnamed x15, other arithmetic  9.63 us
  transfers between devices with their start and end apart: 63, of which 26 were waited for; matrix products, arithmetic and copies ran while one was open for 17% of the time, Pallas kernels for 0%

profile of v1, /device:TPU:0, one launch (start us, length us, event | category | flops | bytes accessed | tf_op | source)
XLA Modules:
  0.0 216.1 jit_solution(2274266180970210986)
XLA Ops:
  2.0 2.0 constant_dynamic-update-slice_fusion
  5.3 2.6 %collective-permute-start = (bf16[32,3584]{1,0:T(8,128)(2,1)}, bf16[32,3584]{1,0:T(8,128)(2,1)}, u32[]{:S(2)}, u32[]{:S(2)}) collective-permute-start(bf16[32,3584]{1,0:T(8,128)(2,1)} %get-tuple-element.44), channel_id=1, source_target_pairs={{0,2},{2,4},{4,6},{6,7},{7,5},{5,3},{3,1},{1,0},{8,10},{10,12},{12... | collective-permute-start | bytes 688136 | tf_op jit(solution)/shard_map/ppermute | solution.py:36
  7.9 2.0 collective-permute-start.1
  9.9 1.8 reshape.118
  17.6 2.8 %collective-permute-start.17 = (bf16[128,2,224]{0,2,1:T(8,128)(2,1)S(1)}, bf16[128,2,224]{0,2,1:T(8,128)(2,1)S(1)}, u32[]{:S(2)}, u32[]{:S(2)}) collective-permute-start(bf16[128,2,224]{0,2,1:T(8,128)(2,1)S(1)} %bitcast.46), channel_id=1, source_target_pairs={{0,6},{1,7},{2,4},{3,5},{4,2},{5,3},{6,0},{7,1},{8,14},{9,15},{10,... | collective-permute-start | bytes 344072 | tf_op jit(solution)/shard_map/ppermute | solution.py:92
  24.8 1.8 maximum_dynamic-update-slice_fusion.6
  26.8 5.6 %collective-permute-done.16 = bf16[128,2,224]{0,2,1:T(8,128)(2,1)S(1)} collective-permute-done((bf16[128,2,224]{0,2,1:T(8,128)(2,1)S(1)}, bf16[128,2,224]{0,2,1:T(8,128)(2,1)S(1)}, u32[]{:S(2)}, u32[]{:S(2)}) %collective-permute-start.16) | collective-permute-done | bytes 114720 | tf_op jit(solution)/shard_map/ppermute | solution.py:92
  34.1 2.7 %collective-permute-start.4 = (bf16[32,3584]{1,0:T(8,128)(2,1)S(1)}, bf16[32,3584]{1,0:T(8,128)(2,1)S(1)}, u32[]{:S(2)}, u32[]{:S(2)}) collective-permute-start(bf16[32,3584]{1,0:T(8,128)(2,1)S(1)} %collective-permute-done.2), channel_id=1, source_target_pairs={{0,2},{2,4},{4,6},{6,7},{7,5},{5,3},{3,1},{1,0},{8,10},{10,12},{12... | collective-permute-start | bytes 688136 | tf_op jit(solution)/shard_map/ppermute | solution.py:36
  36.8 4.8 %collective-permute-start.5 = (bf16[32,3584]{1,0:T(8,128)(2,1)}, bf16[32,3584]{1,0:T(8,128)(2,1)S(1)}, u32[]{:S(2)}, u32[]{:S(2)}) collective-permute-start(bf16[32,3584]{1,0:T(8,128)(2,1)} %collective-permute-done.3), channel_id=1, source_target_pairs={{0,2},{2,4},{4,6},{6,7},{7,5},{5,3},{3,1},{1,0},{8,10},{10,12},{12... | collective-permute-start | bytes 688136 | tf_op jit(solution)/shard_map/ppermute | solution.py:36
  41.6 1.8 maximum_dynamic-update-slice_fusion.5
  47.2 2.5 %collective-permute-start.6 = (bf16[32,3584]{1,0:T(8,128)(2,1)S(1)}, bf16[32,3584]{1,0:T(8,128)(2,1)S(1)}, u32[]{:S(2)}, u32[]{:S(2)}) collective-permute-start(bf16[32,3584]{1,0:T(8,128)(2,1)S(1)} %collective-permute-done.4), channel_id=1, source_target_pairs={{0,2},{2,4},{4,6},{6,7},{7,5},{5,3},{3,1},{1,0},{8,10},{10,12},{12... | collective-permute-start | bytes 688136 | tf_op jit(solution)/shard_map/ppermute | solution.py:36
  49.7 12.5 %collective-permute-done.19 = bf16[512,2,224]{0,2,1:T(8,128)(2,1)S(1)} collective-permute-done((bf16[512,2,224]{0,2,1:T(8,128)(2,1)S(1)}, bf16[512,2,224]{0,2,1:T(8,128)(2,1)S(1)}, u32[]{:S(2)}, u32[]{:S(2)}) %collective-permute-start.19) | collective-permute-done | bytes 458784 | tf_op jit(solution)/shard_map/ppermute | solution.py:103
  62.2 2.9 %collective-permute-start.7 = (bf16[32,3584]{1,0:T(8,128)(2,1)S(1)}, bf16[32,3584]{1,0:T(8,128)(2,1)S(1)}, u32[]{:S(2)}, u32[]{:S(2)}) collective-permute-start(bf16[32,3584]{1,0:T(8,128)(2,1)S(1)} %collective-permute-done.5), channel_id=1, source_target_pairs={{0,2},{2,4},{4,6},{6,7},{7,5},{5,3},{3,1},{1,0},{8,10},{10,12},{12... | collective-permute-start | bytes 688136 | tf_op jit(solution)/shard_map/ppermute | solution.py:36
  65.3 3.3 %collective-permute-done.7 = bf16[32,3584]{1,0:T(8,128)(2,1)S(1)} collective-permute-done((bf16[32,3584]{1,0:T(8,128)(2,1)S(1)}, bf16[32,3584]{1,0:T(8,128)(2,1)S(1)}, u32[]{:S(2)}, u32[]{:S(2)}) %collective-permute-start.7) | collective-permute-done | bytes 229408 | tf_op jit(solution)/shard_map/ppermute | solution.py:36
  71.0 1.8 maximum_dynamic-update-slice_fusion
  72.8 6.4 %fusion.69 = (bf16[256,672]{0,1:T(8,128)(2,1)S(1)}, f32[256,672]{0,1:T(8,128)S(1)}) fusion(bf16[256,7168]{1,0:T(8,128)(2,1)} %maximum_dynamic-update-slice_fusion, bf16[7168,672]{0,1:T(8,128)(2,1)} %bitcast.50), kind=kOutput, calls=%fused_computation.140 | convolution fusion | flops 2466422784 | bytes 14336000 | tf_op jit(solution)/shard_map/dot_general | solution.py:107
  79.2 3.4 %fusion.51 = bf16[256,224]{0,1:T(8,128)(2,1)S(1)} fusion(f32[256,672]{0,1:T(8,128)S(1)} %get-tuple-element.47, bf16[128,224]{0,1:T(8,128)(2,1)S(1)} %copy-done.2, bf16[256,7168]{1,0:T(8,128)(2,1)} %maximum_dynamic-update-slice_fusion, bf16[7168,128]{1,0:T(8,128)(2,1)S(1)} %copy-done), kind=kOutput, calls=%fused_computation.103 | convolution fusion | flops 484589568 | bytes 5906432 | tf_op jit(solution)/shard_map/dot_general | solution.py:108
  83.7 5.1 %fusion.72 = (bf16[256,3584]{1,0:T(8,128)(2,1)}, f32[256,3584]{1,0:T(8,128)}) fusion(bf16[224,3584]{1,0:T(8,128)(2,1)} %param.18, f32[256,224]{0,1:T(8,128)S(1)} %fusion.52, f32[256,512]{1,0:T(8,128)S(1)} %get-tuple-element.49, f32[256]{0:T(256)S(1)} %max.7, bf16[512,2,224]{0,2,1:T(8,128)(2,1)S(1)} %select_select_fusion, f32[256]{0:T(256)S(1)} %add.215), kind=kOutput, calls=%fused_computation.143 | convolution fusion | flops 471113728 | bytes 8095744 | tf_op jit(solution)/shard_map/dot_general | solution.py:131
  89.9 2.5 %collective-permute-start.21 = (bf16[32,1792]{1,0:T(8,128)(2,1)S(1)}, bf16[32,1792]{1,0:T(8,128)(2,1)S(1)}, u32[]{:S(2)}, u32[]{:S(2)}) collective-permute-start(bf16[32,1792]{1,0:T(8,128)(2,1)S(1)} %get-tuple-element.34), channel_id=1, source_target_pairs={{0,2},{2,4},{4,6},{6,7},{7,5},{5,3},{3,1},{1,0},{8,10},{10,12},{12... | collective-permute-start | bytes 344072 | tf_op jit(solution)/shard_map/ppermute | solution.py:52
  94.1 1.8 collective-permute-done.21
  95.9 2.3 %collective-permute-done.28 = bf16[32,1792]{1,0:T(8,128)(2,1)S(1)} collective-permute-done((bf16[32,1792]{1,0:T(8,128)(2,1)S(1)}, bf16[32,1792]{1,0:T(8,128)(2,1)S(1)}, u32[]{:S(2)}, u32[]{:S(2)}) %collective-permute-start.28) | collective-permute-done | bytes 114720 | tf_op jit(solution)/shard_map/ppermute | solution.py:52
  99.3 2.5 %collective-permute-start.22 = (bf16[32,1792]{1,0:T(8,128)(2,1)S(1)}, bf16[32,1792]{1,0:T(8,128)(2,1)S(1)}, u32[]{:S(2)}, u32[]{:S(2)}) collective-permute-start(bf16[32,1792]{1,0:T(8,128)(2,1)S(1)} %get-tuple-element.28), channel_id=1, source_target_pairs={{0,2},{2,4},{4,6},{6,7},{7,5},{5,3},{3,1},{1,0},{8,10},{10,12},{12... | collective-permute-start | bytes 344072 | tf_op jit(solution)/shard_map/ppermute | solution.py:52
  101.8 2.3 %collective-permute-done.22 = bf16[32,1792]{1,0:T(8,128)(2,1)S(1)} collective-permute-done((bf16[32,1792]{1,0:T(8,128)(2,1)S(1)}, bf16[32,1792]{1,0:T(8,128)(2,1)S(1)}, u32[]{:S(2)}, u32[]{:S(2)}) %collective-permute-start.22) | collective-permute-done | bytes 114720 | tf_op jit(solution)/shard_map/ppermute | solution.py:52
  106.7 2.5 %collective-permute-start.23 = (bf16[32,1792]{1,0:T(8,128)(2,1)S(1)}, bf16[32,1792]{1,0:T(8,128)(2,1)S(1)}, u32[]{:S(2)}, u32[]{:S(2)}) collective-permute-start(bf16[32,1792]{1,0:T(8,128)(2,1)S(1)} %get-tuple-element.24), channel_id=1, source_target_pairs={{0,2},{2,4},{4,6},{6,7},{7,5},{5,3},{3,1},{1,0},{8,10},{10,12},{12... | collective-permute-start | bytes 344072 | tf_op jit(solution)/shard_map/ppermute | solution.py:52
  109.2 2.0 collective-permute-start.30
  114.0 2.0 collective-permute-done.26
  117.9 1.8 collective-permute-start.31
  119.7 23.9 %copy.38 = bf16[448,8,2,1792]{3,1,2,0:T(8,128)(2,1)} copy(bf16[448,8,2,1792]{3,2,1,0:T(2,128)(2,1)} %bitcast.38) | data formatting | bytes 51380224
  144.7 2.0 collective-permute-start.35
  146.8 2.0 collective-permute-start.36
  150.5 2.0 collective-permute-start.37
  153.0 2.0 collective-permute-start.38
  156.1 2.1 collective-permute-start.39
  158.6 2.1 collective-permute-start.40
  160.7 2.3 %collective-permute-start.41 = (bf16[32,1792]{1,0:T(8,128)(2,1)S(1)}, bf16[32,1792]{1,0:T(8,128)(2,1)S(1)}, u32[]{:S(2)}, u32[]{:S(2)}) collective-permute-start(bf16[32,1792]{1,0:T(8,128)(2,1)S(1)} %collective-permute-done.39), channel_id=1, source_target_pairs={{0,2},{2,4},{4,6},{6,7},{7,5},{5,3},{3,1},{1,0},{8,10},{10,12},{12... | collective-permute-start | bytes 344072 | tf_op jit(solution)/shard_map/ppermute | solution.py:36
  163.1 2.4 %collective-permute-start.42 = (bf16[32,1792]{1,0:T(8,128)(2,1)S(1)}, bf16[32,1792]{1,0:T(8,128)(2,1)S(1)}, u32[]{:S(2)}, u32[]{:S(2)}) collective-permute-start(bf16[32,1792]{1,0:T(8,128)(2,1)S(1)} %collective-permute-done.40), channel_id=1, source_target_pairs={{0,2},{2,4},{4,6},{6,7},{7,5},{5,3},{3,1},{1,0},{8,10},{10,12},{12... | collective-permute-start | bytes 344072 | tf_op jit(solution)/shard_map/ppermute | solution.py:36
  165.5 2.3 %collective-permute-done.42 = bf16[32,1792]{1,0:T(8,128)(2,1)S(1)} collective-permute-done((bf16[32,1792]{1,0:T(8,128)(2,1)S(1)}, bf16[32,1792]{1,0:T(8,128)(2,1)S(1)}, u32[]{:S(2)}, u32[]{:S(2)}) %collective-permute-start.42) | collective-permute-done | bytes 114720 | tf_op jit(solution)/shard_map/ppermute | solution.py:36
  168.5 12.1 %fusion.3 = f32[256,3584]{1,0:T(8,128)S(1)} fusion(bf16[3584,3584]{1,0:T(8,128)(2,1)} %bitcast.39, bf16[256,3584]{1,0:T(8,128)(2,1)S(1)} %maximum_dynamic-update-slice_fusion.7, f32[3584]{0:T(1024)S(1)} %copy-done.3, f32[256]{0:T(256)S(1)} %add_rsqrt_fusion), kind=kOutput, calls=%fused_computation.5 | convolution fusion | flops 6580338688 | bytes 31210496 | tf_op jit(solution)/shard_map/dot_general | solution.py:137
  180.6 3.6 %fusion.75 = (bf16[256,3584]{1,0:T(8,128)(2,1)S(1)}, f32[256,3584]{1,0:T(8,128)S(1)}) fusion(bf16[1792,3584]{1,0:T(8,128)(2,1)S(1)} %bitcast.49, f32[256,3584]{1,0:T(8,128)S(1)} %fusion.3), kind=kOutput, calls=%fused_computation.144 | convolution fusion | flops 3292004352 | bytes 22020096 | tf_op jit(solution)/shard_map/dot_general | solution.py:139
  184.3 2.4 %collective-permute-start.49 = (bf16[32,1792]{1,0:T(8,128)(2,1)S(1)}, bf16[32,1792]{1,0:T(8,128)(2,1)S(1)}, u32[]{:S(2)}, u32[]{:S(2)}) collective-permute-start(bf16[32,1792]{1,0:T(8,128)(2,1)S(1)} %get-tuple-element.30), channel_id=1, source_target_pairs={{0,2},{2,4},{4,6},{6,7},{7,5},{5,3},{3,1},{1,0},{8,10},{10,12},{12... | collective-permute-start | bytes 344072 | tf_op jit(solution)/shard_map/ppermute | solution.py:52
  186.7 2.0 collective-permute-start.56
  190.3 2.3 %collective-permute-done.56 = bf16[32,1792]{1,0:T(8,128)(2,1)S(1)} collective-permute-done((bf16[32,1792]{1,0:T(8,128)(2,1)S(1)}, bf16[32,1792]{1,0:T(8,128)(2,1)S(1)}, u32[]{:S(2)}, u32[]{:S(2)}) %collective-permute-start.56) | collective-permute-done | bytes 114720 | tf_op jit(solution)/shard_map/ppermute | solution.py:52
  192.6 2.5 %collective-permute-start.50 = (bf16[32,1792]{1,0:T(8,128)(2,1)S(1)}, bf16[32,1792]{1,0:T(8,128)(2,1)S(1)}, u32[]{:S(2)}, u32[]{:S(2)}) collective-permute-start(bf16[32,1792]{1,0:T(8,128)(2,1)S(1)} %get-tuple-element.16), channel_id=1, source_target_pairs={{0,2},{2,4},{4,6},{6,7},{7,5},{5,3},{3,1},{1,0},{8,10},{10,12},{12... | collective-permute-start | bytes 344072 | tf_op jit(solution)/shard_map/ppermute | solution.py:52
  195.2 2.3 %collective-permute-done.50 = bf16[32,1792]{1,0:T(8,128)(2,1)S(1)} collective-permute-done((bf16[32,1792]{1,0:T(8,128)(2,1)S(1)}, bf16[32,1792]{1,0:T(8,128)(2,1)S(1)}, u32[]{:S(2)}, u32[]{:S(2)}) %collective-permute-start.50) | collective-permute-done | bytes 114720 | tf_op jit(solution)/shard_map/ppermute | solution.py:52
  198.7 2.5 %collective-permute-start.51 = (bf16[32,1792]{1,0:T(8,128)(2,1)S(1)}, bf16[32,1792]{1,0:T(8,128)(2,1)S(1)}, u32[]{:S(2)}, u32[]{:S(2)}) collective-permute-start(bf16[32,1792]{1,0:T(8,128)(2,1)S(1)} %get-tuple-element.12), channel_id=1, source_target_pairs={{0,2},{2,4},{4,6},{6,7},{7,5},{5,3},{3,1},{1,0},{8,10},{10,12},{12... | collective-permute-start | bytes 344072 | tf_op jit(solution)/shard_map/ppermute | solution.py:52
  201.2 2.0 collective-permute-start.58
  206.0 2.1 collective-permute-done.54
  211.9 1.9 collective-permute-done.62
  (164 shorter events, 48.3 us)
Async XLA Ops:
  4.8 15.5 %collective-permute-start.8 = (bf16[32,3584]{1,0:T(8,128)(2,1)}, bf16[32,3584]{1,0:T(8,128)(2,1)S(1)}, u32[]{:S(2)}, u32[]{:S(2)}) collective-permute-start(bf16[32,3584]{1,0:T(8,128)(2,1)} %get-tuple-element.44), channel_id=1, source_target_pairs={{0,1},{2,0},{4,2},{6,4},{7,6},{5,7},{3,5},{1,3},{8,9},{10,8},{12,1... | collective-permute-start | bytes 688136 | tf_op jit(solution)/shard_map/ppermute | solution.py:39
  5.3 15.9 %collective-permute-start = (bf16[32,3584]{1,0:T(8,128)(2,1)}, bf16[32,3584]{1,0:T(8,128)(2,1)}, u32[]{:S(2)}, u32[]{:S(2)}) collective-permute-start(bf16[32,3584]{1,0:T(8,128)(2,1)} %get-tuple-element.44), channel_id=1, source_target_pairs={{0,2},{2,4},{4,6},{6,7},{7,5},{5,3},{3,1},{1,0},{8,10},{10,12},{12... | collective-permute-start | bytes 688136 | tf_op jit(solution)/shard_map/ppermute | solution.py:36
  7.9 14.2 %collective-permute-start.11 = (bf16[32,3584]{1,0:T(8,128)(2,1)}, bf16[32,3584]{1,0:T(8,128)(2,1)}, u32[]{:S(2)}, u32[]{:S(2)}) collective-permute-start(bf16[32,3584]{1,0:T(8,128)(2,1)} %get-tuple-element.45), channel_id=1, source_target_pairs={{0,1},{2,0},{4,2},{6,4},{7,6},{5,7},{3,5},{1,3},{8,9},{10,8},{12,1... | collective-permute-start | bytes 688136 | tf_op jit(solution)/shard_map/ppermute | solution.py:39
  7.9 15.3 %collective-permute-start.1 = (bf16[32,3584]{1,0:T(8,128)(2,1)}, bf16[32,3584]{1,0:T(8,128)(2,1)}, u32[]{:S(2)}, u32[]{:S(2)}) collective-permute-start(bf16[32,3584]{1,0:T(8,128)(2,1)} %get-tuple-element.45), channel_id=1, source_target_pairs={{0,2},{2,4},{4,6},{6,7},{7,5},{5,3},{3,1},{1,0},{8,10},{10,12},{12... | collective-permute-start | bytes 688136 | tf_op jit(solution)/shard_map/ppermute | solution.py:36
  17.6 9.1 %collective-permute-start.17 = (bf16[128,2,224]{0,2,1:T(8,128)(2,1)S(1)}, bf16[128,2,224]{0,2,1:T(8,128)(2,1)S(1)}, u32[]{:S(2)}, u32[]{:S(2)}) collective-permute-start(bf16[128,2,224]{0,2,1:T(8,128)(2,1)S(1)} %bitcast.46), channel_id=1, source_target_pairs={{0,6},{1,7},{2,4},{3,5},{4,2},{5,3},{6,0},{7,1},{8,14},{9,15},{10,... | collective-permute-start | bytes 344072 | tf_op jit(solution)/shard_map/ppermute | solution.py:92
  20.4 12.0 %collective-permute-start.16 = (bf16[128,2,224]{0,2,1:T(8,128)(2,1)S(1)}, bf16[128,2,224]{0,2,1:T(8,128)(2,1)S(1)}, u32[]{:S(2)}, u32[]{:S(2)}) collective-permute-start(bf16[128,2,224]{0,2,1:T(8,128)(2,1)S(1)} %bitcast.45), channel_id=1, source_target_pairs={{0,4},{1,5},{2,6},{3,7},{4,0},{5,1},{6,2},{7,3},{8,12},{9,13},{10,... | collective-permute-start | bytes 344072 | tf_op jit(solution)/shard_map/ppermute | solution.py:92
  21.1 11.2 %collective-permute-start.15 = (bf16[128,2,224]{0,2,1:T(8,128)(2,1)S(1)}, bf16[128,2,224]{0,2,1:T(8,128)(2,1)S(1)}, u32[]{:S(2)}, u32[]{:S(2)}) collective-permute-start(bf16[128,2,224]{0,2,1:T(8,128)(2,1)S(1)} %bitcast.44), channel_id=1, source_target_pairs={{0,2},{1,3},{2,0},{3,1},{4,6},{5,7},{6,4},{7,5},{8,10},{9,11},{10,... | collective-permute-start | bytes 344072 | tf_op jit(solution)/shard_map/ppermute | solution.py:92
  22.0 12.0 %collective-permute-start.2 = (bf16[32,3584]{1,0:T(8,128)(2,1)}, bf16[32,3584]{1,0:T(8,128)(2,1)S(1)}, u32[]{:S(2)}, u32[]{:S(2)}) collective-permute-start(bf16[32,3584]{1,0:T(8,128)(2,1)} %collective-permute-done), channel_id=1, source_target_pairs={{0,2},{2,4},{4,6},{6,7},{7,5},{5,3},{3,1},{1,0},{8,10},{10,12},{12... | collective-permute-start | bytes 688136 | tf_op jit(solution)/shard_map/ppermute | solution.py:36
  23.2 13.6 %collective-permute-start.3 = (bf16[32,3584]{1,0:T(8,128)(2,1)}, bf16[32,3584]{1,0:T(8,128)(2,1)}, u32[]{:S(2)}, u32[]{:S(2)}) collective-permute-start(bf16[32,3584]{1,0:T(8,128)(2,1)} %collective-permute-done.1), channel_id=1, source_target_pairs={{0,2},{2,4},{4,6},{6,7},{7,5},{5,3},{3,1},{1,0},{8,10},{10,12},{12... | collective-permute-start | bytes 688136 | tf_op jit(solution)/shard_map/ppermute | solution.py:36
  26.7 16.7 %collective-permute-start.9 = (bf16[32,3584]{1,0:T(8,128)(2,1)S(1)}, bf16[32,3584]{1,0:T(8,128)(2,1)S(1)}, u32[]{:S(2)}, u32[]{:S(2)}) collective-permute-start(bf16[32,3584]{1,0:T(8,128)(2,1)S(1)} %collective-permute-done.8), channel_id=1, source_target_pairs={{0,1},{2,0},{4,2},{6,4},{7,6},{5,7},{3,5},{1,3},{8,9},{10,8},{12,1... | collective-permute-start | bytes 688136 | tf_op jit(solution)/shard_map/ppermute | solution.py:39
  32.4 12.5 %collective-permute-start.12 = (bf16[32,3584]{1,0:T(8,128)(2,1)}, bf16[32,3584]{1,0:T(8,128)(2,1)S(1)}, u32[]{:S(2)}, u32[]{:S(2)}) collective-permute-start(bf16[32,3584]{1,0:T(8,128)(2,1)} %collective-permute-done.11), channel_id=1, source_target_pairs={{0,1},{2,0},{4,2},{6,4},{7,6},{5,7},{3,5},{1,3},{8,9},{10,8},{12,1... | collective-permute-start | bytes 688136 | tf_op jit(solution)/shard_map/ppermute | solution.py:39
  32.4 14.8 %collective-permute-start.20 = (bf16[512,2,224]{0,2,1:T(8,128)(2,1)S(1)}, bf16[512,2,224]{0,2,1:T(8,128)(2,1)S(1)}, u32[]{:S(2)}, u32[]{:S(2)}) collective-permute-start(bf16[512,2,224]{0,2,1:T(8,128)(2,1)S(1)} %pad_maximum_fusion), channel_id=1, source_target_pairs={{0,8},{8,0},{16,24},{24,16},{1,9},{9,1},{17,25},{25,17},{2,10},{10... | collective-permute-start | bytes 1376264 | tf_op jit(solution)/shard_map/ppermute | solution.py:103
  34.1 12.3 %collective-permute-start.4 = (bf16[32,3584]{1,0:T(8,128)(2,1)S(1)}, bf16[32,3584]{1,0:T(8,128)(2,1)S(1)}, u32[]{:S(2)}, u32[]{:S(2)}) collective-permute-start(bf16[32,3584]{1,0:T(8,128)(2,1)S(1)} %collective-permute-done.2), channel_id=1, source_target_pairs={{0,2},{2,4},{4,6},{6,7},{7,5},{5,3},{3,1},{1,0},{8,10},{10,12},{12... | collective-permute-start | bytes 688136 | tf_op jit(solution)/shard_map/ppermute | solution.py:36
  36.8 9.6 %collective-permute-start.5 = (bf16[32,3584]{1,0:T(8,128)(2,1)}, bf16[32,3584]{1,0:T(8,128)(2,1)S(1)}, u32[]{:S(2)}, u32[]{:S(2)}) collective-permute-start(bf16[32,3584]{1,0:T(8,128)(2,1)} %collective-permute-done.3), channel_id=1, source_target_pairs={{0,2},{2,4},{4,6},{6,7},{7,5},{5,3},{3,1},{1,0},{8,10},{10,12},{12... | collective-permute-start | bytes 688136 | tf_op jit(solution)/shard_map/ppermute | solution.py:36
  43.4 18.8 %collective-permute-start.19 = (bf16[512,2,224]{0,2,1:T(8,128)(2,1)S(1)}, bf16[512,2,224]{0,2,1:T(8,128)(2,1)S(1)}, u32[]{:S(2)}, u32[]{:S(2)}) collective-permute-start(bf16[512,2,224]{0,2,1:T(8,128)(2,1)S(1)} %pad_maximum_fusion), channel_id=1, source_target_pairs={{0,16},{8,24},{16,0},{24,8},{1,17},{9,25},{17,1},{25,9},{2,18},{10... | collective-permute-start | bytes 1376264 | tf_op jit(solution)/shard_map/ppermute | solution.py:103
  44.9 20.2 %collective-permute-start.18 = (bf16[512,2,224]{0,2,1:T(8,128)(2,1)S(1)}, bf16[512,2,224]{0,2,1:T(8,128)(2,1)S(1)}, u32[]{:S(2)}, u32[]{:S(2)}) collective-permute-start(bf16[512,2,224]{0,2,1:T(8,128)(2,1)S(1)} %pad_maximum_fusion), channel_id=1, source_target_pairs={{0,24},{8,16},{16,8},{24,0},{1,25},{9,17},{17,9},{25,1},{2,26},{10... | collective-permute-start | bytes 1376264 | tf_op jit(solution)/shard_map/ppermute | solution.py:103
  46.4 23.1 %collective-permute-start.10 = (bf16[32,3584]{1,0:T(8,128)(2,1)S(1)}, bf16[32,3584]{1,0:T(8,128)(2,1)S(1)}, u32[]{:S(2)}, u32[]{:S(2)}) collective-permute-start(bf16[32,3584]{1,0:T(8,128)(2,1)S(1)} %collective-permute-done.9), channel_id=1, source_target_pairs={{0,1},{2,0},{4,2},{6,4},{7,6},{5,7},{3,5},{1,3},{8,9},{10,8},{12,1... | collective-permute-start | bytes 688136 | tf_op jit(solution)/shard_map/ppermute | solution.py:39
  46.4 23.1 %collective-permute-start.13 = (bf16[32,3584]{1,0:T(8,128)(2,1)S(1)}, bf16[32,3584]{1,0:T(8,128)(2,1)S(1)}, u32[]{:S(2)}, u32[]{:S(2)}) collective-permute-start(bf16[32,3584]{1,0:T(8,128)(2,1)S(1)} %collective-permute-done.12), channel_id=1, source_target_pairs={{0,1},{2,0},{4,2},{6,4},{7,6},{5,7},{3,5},{1,3},{8,9},{10,8},{12,1... | collective-permute-start | bytes 688136 | tf_op jit(solution)/shard_map/ppermute | solution.py:39
  47.2 18.1 %collective-permute-start.6 = (bf16[32,3584]{1,0:T(8,128)(2,1)S(1)}, bf16[32,3584]{1,0:T(8,128)(2,1)S(1)}, u32[]{:S(2)}, u32[]{:S(2)}) collective-permute-start(bf16[32,3584]{1,0:T(8,128)(2,1)S(1)} %collective-permute-done.4), channel_id=1, source_target_pairs={{0,2},{2,4},{4,6},{6,7},{7,5},{5,3},{3,1},{1,0},{8,10},{10,12},{12... | collective-permute-start | bytes 688136 | tf_op jit(solution)/shard_map/ppermute | solution.py:36
  62.2 6.4 %collective-permute-start.7 = (bf16[32,3584]{1,0:T(8,128)(2,1)S(1)}, bf16[32,3584]{1,0:T(8,128)(2,1)S(1)}, u32[]{:S(2)}, u32[]{:S(2)}) collective-permute-start(bf16[32,3584]{1,0:T(8,128)(2,1)S(1)} %collective-permute-done.5), channel_id=1, source_target_pairs={{0,2},{2,4},{4,6},{6,7},{7,5},{5,3},{3,1},{1,0},{8,10},{10,12},{12... | collective-permute-start | bytes 688136 | tf_op jit(solution)/shard_map/ppermute | solution.py:36
  89.9 6.0 %collective-permute-start.21 = (bf16[32,1792]{1,0:T(8,128)(2,1)S(1)}, bf16[32,1792]{1,0:T(8,128)(2,1)S(1)}, u32[]{:S(2)}, u32[]{:S(2)}) collective-permute-start(bf16[32,1792]{1,0:T(8,128)(2,1)S(1)} %get-tuple-element.34), channel_id=1, source_target_pairs={{0,2},{2,4},{4,6},{6,7},{7,5},{5,3},{3,1},{1,0},{8,10},{10,12},{12... | collective-permute-start | bytes 344072 | tf_op jit(solution)/shard_map/ppermute | solution.py:52
  92.4 5.8 %collective-permute-start.28 = (bf16[32,1792]{1,0:T(8,128)(2,1)S(1)}, bf16[32,1792]{1,0:T(8,128)(2,1)S(1)}, u32[]{:S(2)}, u32[]{:S(2)}) collective-permute-start(bf16[32,1792]{1,0:T(8,128)(2,1)S(1)} %get-tuple-element.36), channel_id=1, source_target_pairs={{0,2},{2,4},{4,6},{6,7},{7,5},{5,3},{3,1},{1,0},{8,10},{10,12},{12... | collective-permute-start | bytes 344072 | tf_op jit(solution)/shard_map/ppermute | solution.py:52
  94.1 7.7 %collective-permute-start.32 = (bf16[32,1792]{1,0:T(8,128)(2,1)S(1)}, bf16[32,1792]{1,0:T(8,128)(2,1)S(1)}, u32[]{:S(2)}, u32[]{:S(2)}) collective-permute-start(bf16[32,1792]{1,0:T(8,128)(2,1)S(1)} %get-tuple-element.35), channel_id=1, source_target_pairs={{0,1},{2,0},{4,2},{6,4},{7,6},{5,7},{3,5},{1,3},{8,9},{10,8},{12,1... | collective-permute-start | bytes 344072 | tf_op jit(solution)/shard_map/ppermute | solution.py:57
  94.1 7.7 %collective-permute-start.25 = (bf16[32,1792]{1,0:T(8,128)(2,1)S(1)}, bf16[32,1792]{1,0:T(8,128)(2,1)S(1)}, u32[]{:S(2)}, u32[]{:S(2)}) collective-permute-start(bf16[32,1792]{1,0:T(8,128)(2,1)S(1)} %get-tuple-element.37), channel_id=1, source_target_pairs={{0,1},{2,0},{4,2},{6,4},{7,6},{5,7},{3,5},{1,3},{8,9},{10,8},{12,1... | collective-permute-start | bytes 344072 | tf_op jit(solution)/shard_map/ppermute | solution.py:57
  99.3 4.9 %collective-permute-start.22 = (bf16[32,1792]{1,0:T(8,128)(2,1)S(1)}, bf16[32,1792]{1,0:T(8,128)(2,1)S(1)}, u32[]{:S(2)}, u32[]{:S(2)}) collective-permute-start(bf16[32,1792]{1,0:T(8,128)(2,1)S(1)} %get-tuple-element.28), channel_id=1, source_target_pairs={{0,2},{2,4},{4,6},{6,7},{7,5},{5,3},{3,1},{1,0},{8,10},{10,12},{12... | collective-permute-start | bytes 344072 | tf_op jit(solution)/shard_map/ppermute | solution.py:52
  106.7 5.9 %collective-permute-start.23 = (bf16[32,1792]{1,0:T(8,128)(2,1)S(1)}, bf16[32,1792]{1,0:T(8,128)(2,1)S(1)}, u32[]{:S(2)}, u32[]{:S(2)}) collective-permute-start(bf16[32,1792]{1,0:T(8,128)(2,1)S(1)} %get-tuple-element.24), channel_id=1, source_target_pairs={{0,2},{2,4},{4,6},{6,7},{7,5},{5,3},{3,1},{1,0},{8,10},{10,12},{12... | collective-permute-start | bytes 344072 | tf_op jit(solution)/shard_map/ppermute | solution.py:52
  117.4 26.2 %collective-permute-start.24 = (bf16[32,1792]{1,0:T(8,128)(2,1)S(1)}, bf16[32,1792]{1,0:T(8,128)(2,1)S(1)}, u32[]{:S(2)}, u32[]{:S(2)}) collective-permute-start(bf16[32,1792]{1,0:T(8,128)(2,1)S(1)} %get-tuple-element.20), channel_id=1, source_target_pairs={{0,2},{2,4},{4,6},{6,7},{7,5},{5,3},{3,1},{1,0},{8,10},{10,12},{12... | collective-permute-start | bytes 344072 | tf_op jit(solution)/shard_map/ppermute | solution.py:52
  117.6 25.9 %collective-permute-start.34 = (bf16[32,1792]{1,0:T(8,128)(2,1)S(1)}, bf16[32,1792]{1,0:T(8,128)(2,1)S(1)}, u32[]{:S(2)}, u32[]{:S(2)}) collective-permute-start(bf16[32,1792]{1,0:T(8,128)(2,1)S(1)} %get-tuple-element.21), channel_id=1, source_target_pairs={{0,1},{2,0},{4,2},{6,4},{7,6},{5,7},{3,5},{1,3},{8,9},{10,8},{12,1... | collective-permute-start | bytes 344072 | tf_op jit(solution)/shard_map/ppermute | solution.py:57
  117.9 25.7 %collective-permute-start.31 = (bf16[32,1792]{1,0:T(8,128)(2,1)S(1)}, bf16[32,1792]{1,0:T(8,128)(2,1)S(1)}, u32[]{:S(2)}, u32[]{:S(2)}) collective-permute-start(bf16[32,1792]{1,0:T(8,128)(2,1)S(1)} %get-tuple-element.22), channel_id=1, source_target_pairs={{0,2},{2,4},{4,6},{6,7},{7,5},{5,3},{3,1},{1,0},{8,10},{10,12},{12... | collective-permute-start | bytes 344072 | tf_op jit(solution)/shard_map/ppermute | solution.py:52
  119.7 23.9 %collective-permute-start.27 = (bf16[32,1792]{1,0:T(8,128)(2,1)S(1)}, bf16[32,1792]{1,0:T(8,128)(2,1)S(1)}, u32[]{:S(2)}, u32[]{:S(2)}) collective-permute-start(bf16[32,1792]{1,0:T(8,128)(2,1)S(1)} %get-tuple-element.23), channel_id=1, source_target_pairs={{0,1},{2,0},{4,2},{6,4},{7,6},{5,7},{3,5},{1,3},{8,9},{10,8},{12,1... | collective-permute-start | bytes 344072 | tf_op jit(solution)/shard_map/ppermute | solution.py:57
  144.7 5.8 %collective-permute-start.43 = (bf16[32,1792]{1,0:T(8,128)(2,1)S(1)}, bf16[32,1792]{1,0:T(8,128)(2,1)S(1)}, u32[]{:S(2)}, u32[]{:S(2)}) collective-permute-start(bf16[32,1792]{1,0:T(8,128)(2,1)S(1)} %get-tuple-element.18), channel_id=1, source_target_pairs={{0,1},{2,0},{4,2},{6,4},{7,6},{5,7},{3,5},{1,3},{8,9},{10,8},{12,1... | collective-permute-start | bytes 344072 | tf_op jit(solution)/shard_map/ppermute | solution.py:39
  144.7 5.8 %collective-permute-start.35 = (bf16[32,1792]{1,0:T(8,128)(2,1)S(1)}, bf16[32,1792]{1,0:T(8,128)(2,1)S(1)}, u32[]{:S(2)}, u32[]{:S(2)}) collective-permute-start(bf16[32,1792]{1,0:T(8,128)(2,1)S(1)} %get-tuple-element.18), channel_id=1, source_target_pairs={{0,2},{2,4},{4,6},{6,7},{7,5},{5,3},{3,1},{1,0},{8,10},{10,12},{12... | collective-permute-start | bytes 344072 | tf_op jit(solution)/shard_map/ppermute | solution.py:36
  146.7 6.2 %collective-permute-start.46 = (bf16[32,1792]{1,0:T(8,128)(2,1)S(1)}, bf16[32,1792]{1,0:T(8,128)(2,1)S(1)}, u32[]{:S(2)}, u32[]{:S(2)}) collective-permute-start(bf16[32,1792]{1,0:T(8,128)(2,1)S(1)} %get-tuple-element.19), channel_id=1, source_target_pairs={{0,1},{2,0},{4,2},{6,4},{7,6},{5,7},{3,5},{1,3},{8,9},{10,8},{12,1... | collective-permute-start | bytes 344072 | tf_op jit(solution)/shard_map/ppermute | solution.py:39
  146.8 6.2 %collective-permute-start.36 = (bf16[32,1792]{1,0:T(8,128)(2,1)S(1)}, bf16[32,1792]{1,0:T(8,128)(2,1)S(1)}, u32[]{:S(2)}, u32[]{:S(2)}) collective-permute-start(bf16[32,1792]{1,0:T(8,128)(2,1)S(1)} %get-tuple-element.19), channel_id=1, source_target_pairs={{0,2},{2,4},{4,6},{6,7},{7,5},{5,3},{3,1},{1,0},{8,10},{10,12},{12... | collective-permute-start | bytes 344072 | tf_op jit(solution)/shard_map/ppermute | solution.py:36
  150.5 5.6 %collective-permute-start.44 = (bf16[32,1792]{1,0:T(8,128)(2,1)S(1)}, bf16[32,1792]{1,0:T(8,128)(2,1)S(1)}, u32[]{:S(2)}, u32[]{:S(2)}) collective-permute-start(bf16[32,1792]{1,0:T(8,128)(2,1)S(1)} %collective-permute-done.43), channel_id=1, source_target_pairs={{0,1},{2,0},{4,2},{6,4},{7,6},{5,7},{3,5},{1,3},{8,9},{10,8},{12,1... | collective-permute-start | bytes 344072 | tf_op jit(solution)/shard_map/ppermute | solution.py:39
  150.5 5.6 %collective-permute-start.37 = (bf16[32,1792]{1,0:T(8,128)(2,1)S(1)}, bf16[32,1792]{1,0:T(8,128)(2,1)S(1)}, u32[]{:S(2)}, u32[]{:S(2)}) collective-permute-start(bf16[32,1792]{1,0:T(8,128)(2,1)S(1)} %collective-permute-done.35), channel_id=1, source_target_pairs={{0,2},{2,4},{4,6},{6,7},{7,5},{5,3},{3,1},{1,0},{8,10},{10,12},{12... | collective-permute-start | bytes 344072 | tf_op jit(solution)/shard_map/ppermute | solution.py:36
  153.0 5.7 %collective-permute-start.47 = (bf16[32,1792]{1,0:T(8,128)(2,1)S(1)}, bf16[32,1792]{1,0:T(8,128)(2,1)S(1)}, u32[]{:S(2)}, u32[]{:S(2)}) collective-permute-start(bf16[32,1792]{1,0:T(8,128)(2,1)S(1)} %collective-permute-done.46), channel_id=1, source_target_pairs={{0,1},{2,0},{4,2},{6,4},{7,6},{5,7},{3,5},{1,3},{8,9},{10,8},{12,1... | collective-permute-start | bytes 344072 | tf_op jit(solution)/shard_map/ppermute | solution.py:39
  153.0 5.7 %collective-permute-start.38 = (bf16[32,1792]{1,0:T(8,128)(2,1)S(1)}, bf16[32,1792]{1,0:T(8,128)(2,1)S(1)}, u32[]{:S(2)}, u32[]{:S(2)}) collective-permute-start(bf16[32,1792]{1,0:T(8,128)(2,1)S(1)} %collective-permute-done.36), channel_id=1, source_target_pairs={{0,2},{2,4},{4,6},{6,7},{7,5},{5,3},{3,1},{1,0},{8,10},{10,12},{12... | collective-permute-start | bytes 344072 | tf_op jit(solution)/shard_map/ppermute | solution.py:36
  156.1 11.8 %collective-permute-start.45 = (bf16[32,1792]{1,0:T(8,128)(2,1)S(1)}, bf16[32,1792]{1,0:T(8,128)(2,1)S(1)}, u32[]{:S(2)}, u32[]{:S(2)}) collective-permute-start(bf16[32,1792]{1,0:T(8,128)(2,1)S(1)} %collective-permute-done.44), channel_id=1, source_target_pairs={{0,1},{2,0},{4,2},{6,4},{7,6},{5,7},{3,5},{1,3},{8,9},{10,8},{12,1... | collective-permute-start | bytes 344072 | tf_op jit(solution)/shard_map/ppermute | solution.py:39
  158.6 9.3 %collective-permute-start.48 = (bf16[32,1792]{1,0:T(8,128)(2,1)S(1)}, bf16[32,1792]{1,0:T(8,128)(2,1)S(1)}, u32[]{:S(2)}, u32[]{:S(2)}) collective-permute-start(bf16[32,1792]{1,0:T(8,128)(2,1)S(1)} %collective-permute-done.47), channel_id=1, source_target_pairs={{0,1},{2,0},{4,2},{6,4},{7,6},{5,7},{3,5},{1,3},{8,9},{10,8},{12,1... | collective-permute-start | bytes 344072 | tf_op jit(solution)/shard_map/ppermute | solution.py:39
  184.3 6.0 %collective-permute-start.49 = (bf16[32,1792]{1,0:T(8,128)(2,1)S(1)}, bf16[32,1792]{1,0:T(8,128)(2,1)S(1)}, u32[]{:S(2)}, u32[]{:S(2)}) collective-permute-start(bf16[32,1792]{1,0:T(8,128)(2,1)S(1)} %get-tuple-element.30), channel_id=1, source_target_pairs={{0,2},{2,4},{4,6},{6,7},{7,5},{5,3},{3,1},{1,0},{8,10},{10,12},{12... | collective-permute-start | bytes 344072 | tf_op jit(solution)/shard_map/ppermute | solution.py:52
  186.7 5.8 %collective-permute-start.56 = (bf16[32,1792]{1,0:T(8,128)(2,1)S(1)}, bf16[32,1792]{1,0:T(8,128)(2,1)S(1)}, u32[]{:S(2)}, u32[]{:S(2)}) collective-permute-start(bf16[32,1792]{1,0:T(8,128)(2,1)S(1)} %get-tuple-element.32), channel_id=1, source_target_pairs={{0,2},{2,4},{4,6},{6,7},{7,5},{5,3},{3,1},{1,0},{8,10},{10,12},{12... | collective-permute-start | bytes 344072 | tf_op jit(solution)/shard_map/ppermute | solution.py:52
  188.7 6.4 %collective-permute-start.60 = (bf16[32,1792]{1,0:T(8,128)(2,1)S(1)}, bf16[32,1792]{1,0:T(8,128)(2,1)S(1)}, u32[]{:S(2)}, u32[]{:S(2)}) collective-permute-start(bf16[32,1792]{1,0:T(8,128)(2,1)S(1)} %get-tuple-element.31), channel_id=1, source_target_pairs={{0,1},{2,0},{4,2},{6,4},{7,6},{5,7},{3,5},{1,3},{8,9},{10,8},{12,1... | collective-permute-start | bytes 344072 | tf_op jit(solution)/shard_map/ppermute | solution.py:57
  188.8 6.4 %collective-permute-start.53 = (bf16[32,1792]{1,0:T(8,128)(2,1)S(1)}, bf16[32,1792]{1,0:T(8,128)(2,1)S(1)}, u32[]{:S(2)}, u32[]{:S(2)}) collective-permute-start(bf16[32,1792]{1,0:T(8,128)(2,1)S(1)} %get-tuple-element.33), channel_id=1, source_target_pairs={{0,1},{2,0},{4,2},{6,4},{7,6},{5,7},{3,5},{1,3},{8,9},{10,8},{12,1... | collective-permute-start | bytes 344072 | tf_op jit(solution)/shard_map/ppermute | solution.py:57
  192.6 4.9 %collective-permute-start.50 = (bf16[32,1792]{1,0:T(8,128)(2,1)S(1)}, bf16[32,1792]{1,0:T(8,128)(2,1)S(1)}, u32[]{:S(2)}, u32[]{:S(2)}) collective-permute-start(bf16[32,1792]{1,0:T(8,128)(2,1)S(1)} %get-tuple-element.16), channel_id=1, source_target_pairs={{0,2},{2,4},{4,6},{6,7},{7,5},{5,3},{3,1},{1,0},{8,10},{10,12},{12... | collective-permute-start | bytes 344072 | tf_op jit(solution)/shard_map/ppermute | solution.py:52
  198.7 5.9 %collective-permute-start.51 = (bf16[32,1792]{1,0:T(8,128)(2,1)S(1)}, bf16[32,1792]{1,0:T(8,128)(2,1)S(1)}, u32[]{:S(2)}, u32[]{:S(2)}) collective-permute-start(bf16[32,1792]{1,0:T(8,128)(2,1)S(1)} %get-tuple-element.12), channel_id=1, source_target_pairs={{0,2},{2,4},{4,6},{6,7},{7,5},{5,3},{3,1},{1,0},{8,10},{10,12},{12... | collective-permute-start | bytes 344072 | tf_op jit(solution)/shard_map/ppermute | solution.py:52
  208.4 5.3 %collective-permute-start.62 = (bf16[32,1792]{1,0:T(8,128)(2,1)S(1)}, bf16[32,1792]{1,0:T(8,128)(2,1)S(1)}, u32[]{:S(2)}, u32[]{:S(2)}) collective-permute-start(bf16[32,1792]{1,0:T(8,128)(2,1)S(1)} %get-tuple-element.9), channel_id=1, source_target_pairs={{0,1},{2,0},{4,2},{6,4},{7,6},{5,7},{3,5},{1,3},{8,9},{10,8},{12,1... | collective-permute-start | bytes 344072 | tf_op jit(solution)/shard_map/ppermute | solution.py:57
  208.7 5.3 %collective-permute-start.59 = (bf16[32,1792]{1,0:T(8,128)(2,1)S(1)}, bf16[32,1792]{1,0:T(8,128)(2,1)S(1)}, u32[]{:S(2)}, u32[]{:S(2)}) collective-permute-start(bf16[32,1792]{1,0:T(8,128)(2,1)S(1)} %get-tuple-element.10), channel_id=1, source_target_pairs={{0,2},{2,4},{4,6},{6,7},{7,5},{5,3},{3,1},{1,0},{8,10},{10,12},{12... | collective-permute-start | bytes 344072 | tf_op jit(solution)/shard_map/ppermute | solution.py:52
  (26 other events, 304.5 us)

commit v2 on v1

v2 whole, which is shorter than its diff:
```python
import functools

import jax
import jax.numpy as jnp
from jax import lax
from jax.experimental import pallas as pl
from jax.experimental.pallas import tpu as pltpu
from jax.sharding import PartitionSpec as P

HD = 224
EPS = 1e-05
F32 = jnp.float32
BF16 = jnp.bfloat16
NT = (((1,), (1,)), ((), ()))
VMEM = pl.BlockSpec(memory_space=pltpu.VMEM)
SMEM = pl.BlockSpec(memory_space=pltpu.SMEM)
ANY = pl.BlockSpec(memory_space=pl.ANY)


def params(mib=56):
    return pltpu.CompilerParams(vmem_limit_bytes=mib * 2**20)


def split_cols(block, count):
    width = block.shape[1] // count
    return [block[:, i * width : (i + 1) * width] for i in range(count)]


def tile_of(width):
    return 256 if width % 256 == 0 else width


def norm_body(tok_ref, gain_ref, *outs):
    t = tok_ref[...].astype(F32)
    scale = lax.rsqrt(jnp.mean(t * t, axis=-1, keepdims=True) + EPS)
    normed = (t * scale * gain_ref[...]).astype(BF16)
    width = t.shape[1] // len(outs)
    for i, out in enumerate(outs):
        out[...] = normed[:, i * width : (i + 1) * width]


def norm_rows(tokens, gain, count):
    rows, width = tokens.shape
    return pl.pallas_call(
        norm_body,
        in_specs=[VMEM, VMEM],
        out_specs=[VMEM] * count,
        out_shape=[jax.ShapeDtypeStruct((rows, width // count), BF16)] * count,
        compiler_params=params(16),
        name="norm_rows",
    )(tokens, gain)


def unpair_body(w_ref, _, out_ref):
    out_ref[...] = jnp.swapaxes(w_ref[...], 0, 1)


def unpair(weights, part, parts, after):
    depth, two, width = weights.shape
    rows = depth // parts
    step = rows // 2
    return pl.pallas_call(
        unpair_body,
        grid=(2,),
        in_specs=[pl.BlockSpec((step, two, width), lambda i: (2 * part + i, 0, 0)), ANY],
        out_specs=pl.BlockSpec((two, step, width), lambda i: (0, i, 0)),
        out_shape=jax.ShapeDtypeStruct((two, rows, width), BF16),
        compiler_params=params(40),
        cost_estimate=pl.CostEstimate(flops=0, bytes_accessed=4 * rows * two * width, transcendentals=0),
        name="unpair",
    )(weights, after)


def project_step(pieces, w_ref, down_ref, rows_ref, acc_ref, lat_ref, first):
    step = pl.program_id(0)
    kb = w_ref.shape[1]

    @pl.when(step == 0)
    def _():
        at = 0
        for piece in pieces:
            n = piece.shape[0]
            for s in range(rows_ref.shape[0]):
                rows_ref[s, at : at + n, :] = piece[:, s * kb : (s + 1) * kb]
            at += n
        first()

    x = rows_ref[step]
    acc_ref[...] += lax.dot_general(x, w_ref[...], NT, preferred_element_type=F32)
    lat_ref[...] += jnp.dot(x, down_ref[...], preferred_element_type=F32)


def project_body(count, *refs):
    pieces, (w_ref, down_ref, acc_ref, lat_ref, rows_ref) = refs[:count], refs[count:]

    def first():
        acc_ref[...] = jnp.zeros_like(acc_ref)
        lat_ref[...] = jnp.zeros_like(lat_ref)

    project_step(pieces, w_ref, down_ref, rows_ref, acc_ref, lat_ref, first)


def attend_body(count, dims, place_ref, len_ref, *refs):
    pieces = refs[:count]
    w_ref, down_ref, up_ref, kv_ref, acc_in, lat_in, out_ref, rows_ref, acc_ref, lat_ref = refs[count:]
    rows, cols, chips, tok_dev = dims
    steps = rows_ref.shape[0]

    def first():
        acc_ref[...] = acc_in[...]
        lat_ref[...] = lat_in[...]

    project_step(pieces, w_ref, down_ref, rows_ref, acc_ref, lat_ref, first)

    @pl.when(pl.program_id(0) == steps - 1)
    def _():
        chip, core = place_ref[0], place_ref[1]
        keys = acc_ref[:, cols : 2 * cols].astype(BF16)
        vals = acc_ref[:, 2 * cols :].astype(BF16)
        up = up_ref[...]
        scale = HD ** (-0.5)
        pair = 2 * tok_dev

        def spots(row):
            slot = row // pair
            inside = row - slot * pair
            side = inside // tok_dev
            owner = chip - slot
            owner = jnp.where(owner < 0, owner + chips, owner)
            at = jnp.where(core == 0, side, 1 - side)
            return owner * pair + at * tok_dev + inside - side * tok_dev

        def requests(spot):
            end = len_ref[0, 0]
            found = (spot >= end).astype(jnp.int32)
            for j in range(1, len_ref.shape[1]):
                end = end + len_ref[0, j]
                found = found + (spot >= end).astype(jnp.int32)
            return found

        block = min(256, rows)
        col_spot = spots(lax.broadcasted_iota(jnp.int32, (1, rows), 1))
        col_req = requests(col_spot)

        def one_block(b, carry):
            r0 = pl.multiple_of(b * block, block)
            lat = lat_ref[pl.ds(r0, block), :].astype(BF16)
            q = acc_ref[pl.ds(r0, block), :cols] + lax.dot_general(lat, up, NT, preferred_element_type=F32)
            q = q.astype(BF16)
            row_spot = spots(r0 + lax.broadcasted_iota(jnp.int32, (block, 1), 0))
            allowed = jnp.logical_and(requests(row_spot) == col_req, col_spot <= row_spot)
            pre = lax.dot_general(q, kv_ref[0], NT, preferred_element_type=F32) * scale
            suf = lax.dot_general(q, keys, NT, preferred_element_type=F32) * scale
            suf = jnp.where(allowed, suf, -jnp.inf)
            top = jnp.maximum(jnp.max(pre, axis=1, keepdims=True), jnp.max(suf, axis=1, keepdims=True))
            pre = jnp.exp(pre - top)
            suf = jnp.exp(suf - top)
            total = jnp.sum(pre, axis=1, keepdims=True) + jnp.sum(suf, axis=1, keepdims=True)
            weighted = jnp.dot(pre.astype(BF16), kv_ref[1], preferred_element_type=F32) + jnp.dot(
                suf.astype(BF16), vals, preferred_element_type=F32
            )
            heads = (weighted / total).astype(BF16)
            for k in range(block // tok_dev):
                base = r0 + (k // 2) * pair
                shift = (core if k % 2 == 0 else 1 - core) * tok_dev
                at = pl.multiple_of(base + shift, tok_dev)
                out_ref[pl.ds(at, tok_dev), :] = heads[k * tok_dev : (k + 1) * tok_dev]
            return carry

        if rows == block:
            one_block(0, 0)
        else:
            lax.fori_loop(0, rows // block, one_block, 0)


def project_specs(part, cols3, rank, width):
    kb = width // 4
    return 4, kb, [
        pl.BlockSpec((cols3, kb), lambda i: (0, 4 * part + i)),
        pl.BlockSpec((kb, rank), lambda i: (4 * part + i, 0)),
    ]


def project(pieces, part, w_t, down):
    rows = sum(p.shape[0] for p in pieces)
    width = pieces[0].shape[1]
    cols3, rank = w_t.shape[0], down.shape[1]
    steps, kb, specs = project_specs(part, cols3, rank, width)
    whole = lambda shape: pl.BlockSpec(shape, lambda i: (0, 0))
    return pl.pallas_call(
        functools.partial(project_body, len(pieces)),
        grid=(steps,),
        in_specs=[VMEM] * len(pieces) + specs,
        out_specs=[whole((rows, cols3)), whole((rows, rank))],
        out_shape=[jax.ShapeDtypeStruct((rows, cols3), F32), jax.ShapeDtypeStruct((rows, rank), F32)],
        scratch_shapes=[pltpu.VMEM((steps, rows, kb), BF16)],
        compiler_params=params(),
        cost_estimate=pl.CostEstimate(
            flops=2 * rows * width * (cols3 + rank), bytes_accessed=2 * width * (cols3 + rank), transcendentals=0
        ),
        name="project",
    )(*pieces, w_t, down)


def attend(pieces, part, w_t, down, up_t, kv, acc, lat, place, lengths, chips):
    rows = sum(p.shape[0] for p in pieces)
    width = pieces[0].shape[1]
    cols3, rank = w_t.shape[0], down.shape[1]
    cols = cols3 // 3
    steps, kb, specs = project_specs(part, cols3, rank, width)
    dims = (rows, cols, chips, pieces[0].shape[0])
    return pl.pallas_call(
        functools.partial(attend_body, len(pieces), dims),
        grid=(steps,),
        in_specs=[SMEM, SMEM] + [VMEM] * len(pieces) + specs + [VMEM] * 4,
        out_specs=pl.BlockSpec((rows, cols), lambda i: (0, 0)),
        out_shape=jax.ShapeDtypeStruct((rows, cols), BF16),
        scratch_shapes=[
            pltpu.VMEM((steps, rows, kb), BF16),
            pltpu.VMEM((rows, cols3), F32),
            pltpu.VMEM((rows, rank), F32),
        ],
        compiler_params=params(),
        cost_estimate=pl.CostEstimate(
            flops=2 * rows * width * (cols3 + rank), bytes_accessed=2 * width * (cols3 + rank), transcendentals=0
        ),
        name="attend",
    )(place, lengths, *pieces, w_t, down, up_t, kv, acc, lat)


def out_body(a_ref, b_ref, wa_ref, wb_ref, out_ref):
    out_ref[...] = jnp.dot(a_ref[...], wa_ref[...], preferred_element_type=F32) + jnp.dot(
        b_ref[...], wb_ref[...], preferred_element_type=F32
    )


def out_project(own, got, w_own, w_got):
    rows, cols = own.shape
    width = w_own.shape[1]
    tile = 896 if width % 896 == 0 else width
    whole = pl.BlockSpec((rows, cols), lambda j: (0, 0))
    wide = pl.BlockSpec((cols, tile), lambda j: (0, j))
    return pl.pallas_call(
        out_body,
        grid=(width // tile,),
        in_specs=[whole, whole, wide, wide],
        out_specs=pl.BlockSpec((rows, tile), lambda j: (0, j)),
        out_shape=jax.ShapeDtypeStruct((rows, width), F32),
        compiler_params=params(),
        name="out_project",
    )(own, got, w_own, w_got)


def gate_body(count, dims, place_ref, gain_ref, *refs):
    slots, chunks, parts = dims
    pieces = refs[:count]
    weights = refs[count : count + parts]
    out_ref, x_ref = refs[count + parts :]
    core = place_ref[1]
    half = x_ref.shape[2]

    @pl.when(pl.program_id(0) == 0)
    def _():
        at = iter(pieces)
        row = 0
        for _k in range(slots):
            own = [next(at)[...].astype(F32) for _c in range(chunks)]
            got = [next(at)[...].astype(F32) for _c in range(chunks)]
            own = jnp.concatenate(own, axis=1)
            got = jnp.concatenate(got, axis=1)
            n = own.shape[0]
            square = jnp.sum(own * own, axis=-1, keepdims=True) + jnp.sum(got * got, axis=-1, keepdims=True)
            scale = lax.rsqrt(square * (0.5 / half) + EPS)
            x_ref[core, row : row + n, :] = (own * scale * gain_ref[core]).astype(BF16)
            x_ref[1 - core, row : row + n, :] = (got * scale * gain_ref[1 - core]).astype(BF16)
            row += n

    gate = up = None
    per = half * 2 // parts
    for p, w_ref in enumerate(weights):
        side, at = divmod(p * per, half)
        x = x_ref[side, :, at : at + per]
        g = jnp.dot(x, w_ref[0], preferred_element_type=F32)
        u = jnp.dot(x, w_ref[1], preferred_element_type=F32)
        gate = g if gate is None else gate + g
        up = u if up is None else up + u
    out_ref[...] = (gate / (1.0 + jnp.exp(-gate)) * up).astype(BF16)


def gate_up(pieces, slots, chunks, weights, gain, place):
    half = gain.shape[2]
    rows = slots * pieces[0].shape[0]
    parts = len(weights)
    _, depth, units = weights[0].shape
    tile = tile_of(units)
    return pl.pallas_call(
        functools.partial(gate_body, len(pieces), (slots, chunks, parts)),
        grid=(units // tile,),
        in_specs=[SMEM, VMEM] + [VMEM] * len(pieces) + [pl.BlockSpec((2, depth, tile), lambda j: (0, 0, j))] * parts,
        out_specs=pl.BlockSpec((rows, tile), lambda j: (0, j)),
        out_shape=jax.ShapeDtypeStruct((rows, units), BF16),
        scratch_shapes=[pltpu.VMEM((2, rows, half), BF16)],
        compiler_params=params(),
        cost_estimate=pl.CostEstimate(
            flops=8 * rows * half * units, bytes_accessed=8 * half * units, transcendentals=rows * units
        ),
        name="gate_up",
    )(place, gain, *pieces, *weights)


def down_body(side_ref, x_ref, w_ref, *rest):
    out_ref = rest[-1]
    total = jnp.dot(x_ref[...], w_ref[...], preferred_element_type=F32)
    out_ref[...] = total.astype(out_ref.dtype)


def down_half(hidden, w_down, side, dtype):
    rows, units = hidden.shape
    half = w_down.shape[1] // 2
    tile = tile_of(half)
    steps = half // tile
    return pl.pallas_call(
        down_body,
        grid_spec=pltpu.PrefetchScalarGridSpec(
            num_scalar_prefetch=1,
            grid=(steps,),
            in_specs=[
                pl.BlockSpec((rows, units), lambda j, s: (0, 0)),
                pl.BlockSpec((units, tile), lambda j, s: (0, s[0] * steps + j)),
            ],
            out_specs=pl.BlockSpec((rows, tile), lambda j, s: (0, j)),
        ),
        out_shape=jax.ShapeDtypeStruct((rows, half), dtype),
        compiler_params=params(),
        cost_estimate=pl.CostEstimate(
            flops=2 * rows * half * units, bytes_accessed=2 * half * units, transcendentals=0
        ),
        name="down_half",
    )(side, hidden, w_down)


def make(mesh):
    n = mesh.shape["hid"]
    n_req = mesh.shape["req"]
    chips = n // 2
    both = [(h, h ^ 1) for h in range(n)]
    ring = [(h, (h + 2) % n) for h in range(n)]

    def swap(v):
        return lax.ppermute(v, "hid", both)

    def onward(v):
        return lax.ppermute(v, "hid", ring)

    def gather(own):
        slots = []
        here = list(own)
        for k in range(chips):
            if k:
                here = [onward(v) for v in here]
            slots.append(here)
        return [(s, [swap(v) for v in s]) for s in slots]

    def scatter(partial, count):
        rows = partial.shape[0] // chips
        parts = split_cols(partial, count)
        block = lambda i, k: parts[i][k * rows : (k + 1) * rows]
        sums = [block(i, 1).astype(BF16) for i in range(count)]
        for k in range(2, chips + 1):
            sums = [onward(v) for v in sums]
            sums = [v.astype(F32) + block(i, k % chips) for i, v in enumerate(sums)]
            sums = [v.astype(BF16) for v in sums]
        return sums

    def per_device(tokens, gain_in, w_qkv, adapt_down, adapt_up, w_out, gain_ff, w_gate_up, w_down,
                   prefix_cache, prefix_owner, group_prefix, lengths):
        tok_dev, width_in = tokens.shape
        cols = w_qkv.shape[2]
        model_width = w_out.shape[1]
        half = model_width // 2
        hid = lax.axis_index("hid")
        core = hid % 2
        chip = hid // 2
        place = jnp.stack([chip, core]).astype(jnp.int32)

        normed = norm_rows(tokens, gain_in[None, :], 2)
        slots = gather(normed)

        cache = jnp.swapaxes(prefix_cache[0], 0, 1).reshape(2, -1, chips, 2, cols)
        mine = lax.dynamic_index_in_dim(cache, core, 3, keepdims=False)
        other = lax.dynamic_index_in_dim(cache, 1 - core, 3, keepdims=False)
        cache = jnp.concatenate([mine, swap(other)], axis=1)
        blocks = [lax.dynamic_index_in_dim(cache, chip, 2, keepdims=False)]
        for k in range(1, chips):
            block = lax.dynamic_index_in_dim(cache, chip ^ k, 2, keepdims=False)
            blocks.append(lax.ppermute(block, "hid", [(h, h ^ (2 * k)) for h in range(n)]))
        heads_cache = jnp.concatenate(blocks, axis=1)
        req = lax.axis_index("req")
        away = prefix_owner[group_prefix[req]] ^ req
        chosen = heads_cache
        for k in range(1, n_req):
            seen = lax.ppermute(heads_cache, "req", [(r, r ^ k) for r in range(n_req)])
            chosen = jnp.where(away == k, seen, chosen)

        w_own = lax.dynamic_slice_in_dim(w_out, core * half, half, 1)
        w_got = swap(lax.dynamic_slice_in_dim(w_out, (1 - core) * half, half, 1))

        parts = 4
        w_pairs = [unpair(w_gate_up, p, parts, slots[min(p, chips - 1)][0][0]) for p in range(parts)]

        w_t = jnp.transpose(w_qkv, (1, 2, 0)).reshape(3 * cols, width_in)
        pick = lambda i: [v for s in slots for v in (s[0][i], s[1][i])]
        acc, lat = project(pick(0), 0, w_t, adapt_down)
        heads = attend(pick(1), 1, w_t, adapt_down, adapt_up.T, chosen, acc, lat, place, lengths, chips)
        partial = out_project(heads, swap(heads), w_own, w_got)

        sums = scatter(partial, 2)
        summed = gather(sums)
        own_rows = lambda v: lax.dynamic_slice_in_dim(v, core * tok_dev, tok_dev, 0)
        near = jnp.concatenate([own_rows(v) for v in summed[0][0]], axis=1)
        far = jnp.concatenate([own_rows(v) for v in summed[0][1]], axis=1)
        attn_own = jnp.where(core == 0, jnp.concatenate([near, far], axis=1), jnp.concatenate([far, near], axis=1))

        pieces = [v for s in summed for v in s[0] + s[1]]
        hidden = gate_up(pieces, chips, 2, w_pairs, gain_ff.reshape(2, 1, half), place)
        away_half = down_half(hidden, w_down, (1 - core).astype(jnp.int32)[None], BF16)
        got_half = swap(away_half)
        own_half = down_half(hidden, w_down, core.astype(jnp.int32)[None], F32)
        ends = scatter(own_half + got_half.astype(F32), 2)
        ends = jnp.concatenate(ends, axis=1)
        near = own_rows(ends)
        far = swap(lax.dynamic_slice_in_dim(ends, (1 - core) * tok_dev, tok_dev, 0))
        block_own = jnp.where(core == 0, jnp.concatenate([near, far], axis=1), jnp.concatenate([far, near], axis=1))
        return attn_own, block_own

    return per_device


def solution(mesh):
    placed = (
        P(("req", "hid"), None),
        P(),
        P(None, None, "hid"),
        P(),
        P(None, "hid"),
        P("hid", None),
        P(),
        P(None, None, "hid"),
        P("hid", None),
        P("req", "hid", None, None),
        P(),
        P(),
        P("req", None),
    )
    return jax.shard_map(
        make(mesh),
        mesh=mesh,
        in_specs=placed,
        out_specs=(P(("req", "hid"), None), P(("req", "hid"), None)),
        check_vma=False,
    )
```

time: 217 us -> 237 us (1.092)
  Pallas kernels: 0 us -> 64.5 us
  waiting for transfers between devices: 56 us -> 113 us
  starting transfers between devices: 74.3 us -> 21.6 us
  matrix products: 31.3 us -> 0 us
  other arithmetic: 20.2 us -> 9.18 us
  local copies, waits for them, and re-layouts: 30.7 us -> 23.4 us
    pallas_call x0 -> x11, Pallas kernels: none -> 64.5 us  [the longest x1 15.9 us: gate_up(): pl.pallas_call(functools.partial(gate_body, len(pieces), (slots, chunks,...]
    ppermute x57 -> x45, starting transfers between devices: 65.2 us -> 13.6 us  [the longest x24 10.2 us: onward(): return lax.ppermute(v, 'hid', ring)]
    ppermute x57 -> x45, waiting for transfers between devices: 37.9 us -> 85.1 us  [the longest x24 83.3 us: onward(): return lax.ppermute(v, 'hid', ring)]
    dot_general x8 -> x0, matrix products: 31.3 us -> none  [the longest x1 12.1 us: per_device(): jnp.dot(ff_in, w_gate_up.reshape(model_width, 2 * units), preferred_eleme...]
    ppermute x3, waiting for transfers between devices: 5.63 us -> 20.7 us  [per_device(): lax.ppermute(block, 'hid', [(h, h ^ 2 * k) for h in range(n)])]
    unnamed x15 -> x0, other arithmetic: 9.63 us -> none
    unnamed x23 -> x104, local copies, waits for them, and re-layouts: 23.9 us -> 17 us
    ppermute x3, waiting for transfers between devices: 12.5 us -> 7.14 us  [per_device(): seen = lax.ppermute(heads_cache, 'req', [(r, r ^ k) for r in range(n_req)])]
  transfers between devices with their start and end apart: 63 -> 51, of which waited for: 26 -> 28; matrix products, arithmetic and copies ran while one was open for 17% -> 5% of each run, Pallas kernels for 0% -> 16%
where the time goes in v2:
time: 237 us; the launch traced here: 236 us
  waiting for transfers between devices  113 us (48%)
  Pallas kernels  64.5 us (27%)
  local copies, waits for them, and re-layouts  23.4 us (10%)
  starting transfers between devices  21.6 us (9%)
  other arithmetic  9.18 us (4%)
  between operations  4.04 us (2%)
    ppermute x24, waiting for transfers between devices, onward(): return lax.ppermute(v, 'hid', ring)  83.3 us
    ppermute x3, waiting for transfers between devices, per_device(): lax.ppermute(block, 'hid', [(h, h ^ 2 * k) for h in range(n)])  20.7 us
    unnamed x104, local copies, waits for them, and re-layouts  17 us
    pallas_call x1, Pallas kernels, gate_up(): pl.pallas_call(functools.partial(gate_body, len(pieces), (slots, chunks,...  15.9 us
    pallas_call x2, Pallas kernels, down_half(): pl.pallas_call(down_body, grid_spec=pltpu.PrefetchScalarGridSpec(num_scal...  15.5 us
    pallas_call x4, Pallas kernels, unpair(): pl.pallas_call(unpair_body, grid=(2,), in_specs=[pl.BlockSpec((step, two,...  15.1 us
    ppermute x24, starting transfers between devices, onward(): return lax.ppermute(v, 'hid', ring)  10.2 us
    pallas_call x1, Pallas kernels, attend(): pl.pallas_call(functools.partial(attend_body, len(pieces), dims), grid=(s...  7.87 us
  transfers between devices with their start and end apart: 51, of which 28 were waited for; matrix products, arithmetic and copies ran while one was open for 5% of the time, Pallas kernels for 16%

profile of v2, /device:TPU:0, one launch (start us, length us, event | category | flops | bytes accessed | tf_op | source)
XLA Modules:
  0.0 235.6 jit_solution(56455670527520382)
XLA Ops:
  2.7 3.1 %collective-permute-start.15 = (bf16[32,3584]{1,0:T(8,128)(2,1)S(1)}, bf16[32,3584]{1,0:T(8,128)(2,1)S(1)}, u32[]{:S(2)}, u32[]{:S(2)}) collective-permute-start(bf16[32,3584]{1,0:T(8,128)(2,1)S(1)} %get-tuple-element.7.refs_0_._), channel_id=1, source_target_pairs={{0,2},{1,3},{2,4},{3,5},{4,6},{5,7},{6,0},{7,1},{8,10},{9,11},{10,... | collective-permute-start | bytes 688136 | tf_op jit(solution)/shard_map/ppermute | solution.py:353
  5.8 1.8 reshape.14
  8.9 1.6 collective-permute-start.1
  10.7 2.7 %collective-permute-done.15.refs_2_._ = bf16[32,3584]{1,0:T(8,128)(2,1)S(1)} collective-permute-done((bf16[32,3584]{1,0:T(8,128)(2,1)S(1)}, bf16[32,3584]{1,0:T(8,128)(2,1)S(1)}, u32[]{:S(2)}, u32[]{:S(2)}) %collective-permute-start.15) | collective-permute-done | bytes 229408 | tf_op jit(solution)/shard_map/ppermute | solution.py:353
  14.5 3.8 %collective-permute-start.10 = (bf16[2,128,224]{2,1,0:T(8,128)(2,1)S(1)}, bf16[2,128,224]{2,1,0:T(8,128)(2,1)S(1)}, u32[]{:S(2)}, u32[]{:S(2)}) collective-permute-start(bf16[2,128,224]{2,1,0:T(8,128)(2,1)S(1)} %get-tuple-element.33), channel_id=1, source_target_pairs={{0,6},{1,7},{2,4},{3,5},{4,2},{5,3},{6,0},{7,1},{8,14},{9,15},{10,... | collective-permute-start | bytes 344072 | tf_op jit(solution)/shard_map/ppermute | solution.py:396
  19.4 7.6 %collective-permute-done.10 = bf16[2,128,224]{2,1,0:T(8,128)(2,1)S(1)} collective-permute-done((bf16[2,128,224]{2,1,0:T(8,128)(2,1)S(1)}, bf16[2,128,224]{2,1,0:T(8,128)(2,1)S(1)}, u32[]{:S(2)}, u32[]{:S(2)}) %collective-permute-start.10) | collective-permute-done | bytes 114720 | tf_op jit(solution)/shard_map/ppermute | solution.py:396
  27.0 2.4 collective-permute-done.8
  29.3 2.0 collective-permute-start.3
  31.3 2.6 %collective-permute-start.19 = (bf16[32,3584]{1,0:T(8,128)(2,1)S(1)}, bf16[32,3584]{1,0:T(8,128)(2,1)S(1)}, u32[]{:S(2)}, u32[]{:S(2)}) collective-permute-start(bf16[32,3584]{1,0:T(8,128)(2,1)S(1)} %collective-permute-done.17.refs_4_._), channel_id=1, source_target_pairs={{0,2},{1,3},{2,4},{3,5},{4,6},{5,7},{6,0},{7,1},{8,10},{9,11},{10,... | collective-permute-start | bytes 688136 | tf_op jit(solution)/shard_map/ppermute | solution.py:353
  33.9 10.8 %collective-permute-done.9 = bf16[2,128,224]{2,1,0:T(8,128)(2,1)S(1)} collective-permute-done((bf16[2,128,224]{2,1,0:T(8,128)(2,1)S(1)}, bf16[2,128,224]{2,1,0:T(8,128)(2,1)S(1)}, u32[]{:S(2)}, u32[]{:S(2)}) %collective-permute-start.9) | collective-permute-done | bytes 114720 | tf_op jit(solution)/shard_map/ppermute | solution.py:396
  44.8 2.5 %collective-permute-start.11 = (bf16[2,512,224]{2,1,0:T(8,128)(2,1)S(1)}, bf16[2,512,224]{2,1,0:T(8,128)(2,1)}, u32[]{:S(2)}, u32[]{:S(2)}) collective-permute-start(bf16[2,512,224]{2,1,0:T(8,128)(2,1)S(1)} %pad_maximum_fusion), channel_id=1, source_target_pairs={{0,24},{8,16},{16,8},{24,0},{1,25},{9,17},{17,9},{25,1},{2,26},{10... | collective-permute-start | bytes 1376264 | tf_op jit(solution)/shard_map/ppermute | solution.py:402
  49.4 1.3 constant_dynamic-slice_fusion.4
  50.7 8.1 %collective-permute-done.5.refs_6_ = bf16[32,3584]{1,0:T(8,128)(2,1)S(1)} collective-permute-done((bf16[32,3584]{1,0:T(8,128)(2,1)}, bf16[32,3584]{1,0:T(8,128)(2,1)S(1)}, u32[]{:S(2)}, u32[]{:S(2)}) %collective-permute-start.5) | collective-permute-done | bytes 229408 | tf_op jit(solution)/shard_map/ppermute | solution.py:353
  64.4 7.1 %collective-permute-done.12 = bf16[2,512,224]{2,1,0:T(8,128)(2,1)} collective-permute-done((bf16[2,512,224]{2,1,0:T(8,128)(2,1)S(1)}, bf16[2,512,224]{2,1,0:T(8,128)(2,1)}, u32[]{:S(2)}, u32[]{:S(2)}) %collective-permute-start.12) | collective-permute-done | bytes 458784 | tf_op jit(solution)/shard_map/ppermute | solution.py:402
  72.1 2.0 select_select_fusion.refs_11_
  74.1 6.7 %project.1 = (f32[256,672]{1,0:T(8,128)}, f32[256,128]{1,0:T(8,128)}) custom-call(bf16[32,3584]{1,0:T(8,128)(2,1)} %copy-done.4, bf16[32,3584]{1,0:T(8,128)(2,1)} %copy-done.34, bf16[32,3584]{1,0:T(8,128)(2,1)} %copy-done.6, bf16[32,3584]{1,0:T(8,128)(2,1)} %copy-done.35, bf16[32,3584]{1,0:T(8,128)(2,1)} %copy-done.8, ...), custom_call_target="tpu_custom_call" | custom-call | flops 1468006400 | bytes 5734400 | tf_op jit(solution)/shard_map/project/pallas_call | solution.py:190
  81.7 7.9 %attend.1.a_ref = bf16[256,224]{1,0:T(8,128)(2,1)} custom-call(s32[2]{0:T(128)} %pad_add_fusion.place_ref, s32[1,6]{1,0:T(1,128)} %len_ref.1, bf16[32,3584]{1,0:T(8,128)(2,1)} %copy-done.13, bf16[32,3584]{1,0:T(8,128)(2,1)} %copy-done.30, bf16[32,3584]{1,0:T(8,128)(2,1)} %collective-permute-done.1.refs_2_, bf16[32,3584]{1,0:T(8,128)(2,1)} %copy-done.31, ...), custom_call_target="tpu_custom_call" | custom-call | flops 1468006400 | bytes 5734400 | tf_op jit(solution)/shard_map/attend/pallas_call | solution.py:212
  91.9 3.1 %out_project.1 = f32[256,1792]{1,0:T(8,128)} custom-call(bf16[256,224]{1,0:T(8,128)(2,1)} %attend.1.a_ref, bf16[256,224]{1,0:T(8,128)(2,1)} %copy-done.36, bf16[224,1792]{1,0:T(8,128)(2,1)} %get-tuple-element.25.wa_ref, bf16[224,1792]{1,0:T(8,128)(2,1)} %copy-done.17), custom_call_target="tpu_custom_call" | custom-call | tf_op jit(solution)/shard_map/out_project/pallas_call | solution.py:243
  95.0 1.7 convert.8
  96.9 7.7 %collective-permute-done.23 = bf16[64,896]{1,0:T(8,128)(2,1)S(1)} collective-permute-done((bf16[64,896]{1,0:T(8,128)(2,1)S(1)}, bf16[64,896]{1,0:T(8,128)(2,1)S(1)}, u32[]{:S(2)}, u32[]{:S(2)}) %collective-permute-start.23) | collective-permute-done | bytes 114720 | tf_op jit(solution)/shard_map/ppermute | solution.py:353
  104.6 1.9 collective-permute-done.26
  106.7 7.5 %collective-permute-done.24 = bf16[64,896]{1,0:T(8,128)(2,1)S(1)} collective-permute-done((bf16[64,896]{1,0:T(8,128)(2,1)S(1)}, bf16[64,896]{1,0:T(8,128)(2,1)S(1)}, u32[]{:S(2)}, u32[]{:S(2)}) %collective-permute-start.24) | collective-permute-done | bytes 114720 | tf_op jit(solution)/shard_map/ppermute | solution.py:353
  114.2 1.2 collective-permute-done.27
  115.6 6.6 %collective-permute-done.25 = bf16[64,896]{1,0:T(8,128)(2,1)S(1)} collective-permute-done((bf16[64,896]{1,0:T(8,128)(2,1)S(1)}, bf16[64,896]{1,0:T(8,128)(2,1)S(1)}, u32[]{:S(2)}, u32[]{:S(2)}) %collective-permute-start.25) | collective-permute-done | bytes 114720 | tf_op jit(solution)/shard_map/ppermute | solution.py:353
  122.3 1.2 collective-permute-done.28
  123.7 6.5 %collective-permute-done.31.refs_4_ = bf16[64,896]{1,0:T(8,128)(2,1)S(1)} collective-permute-done((bf16[64,896]{1,0:T(8,128)(2,1)S(1)}, bf16[64,896]{1,0:T(8,128)(2,1)S(1)}, u32[]{:S(2)}, u32[]{:S(2)}) %collective-permute-start.31) | collective-permute-done | bytes 114720 | tf_op jit(solution)/shard_map/ppermute | solution.py:353
  130.2 1.4 collective-permute-done.32.refs_5_
  132.2 4.6 %collective-permute-done.35.refs_8_ = bf16[64,896]{1,0:T(8,128)(2,1)S(1)} collective-permute-done((bf16[64,896]{1,0:T(8,128)(2,1)S(1)}, bf16[64,896]{1,0:T(8,128)(2,1)S(1)}, u32[]{:S(2)}, u32[]{:S(2)}) %collective-permute-start.35) | collective-permute-done | bytes 114720 | tf_op jit(solution)/shard_map/ppermute | solution.py:353
  136.8 2.3 collective-permute-done.36.refs_9_
  139.8 3.6 %collective-permute-done.39.refs_12_ = bf16[64,896]{1,0:T(8,128)(2,1)S(1)} collective-permute-done((bf16[64,896]{1,0:T(8,128)(2,1)S(1)}, bf16[64,896]{1,0:T(8,128)(2,1)S(1)}, u32[]{:S(2)}, u32[]{:S(2)}) %collective-permute-start.39) | collective-permute-done | bytes 114720 | tf_op jit(solution)/shard_map/ppermute | solution.py:353
  143.4 2.3 collective-permute-done.40.refs_13_
  145.7 3.8 %unpair.4.refs_16_ = bf16[2,896,1792]{2,1,0:T(8,128)(2,1)S(1)} custom-call(bf16[3584,2,1792]{2,1,0:T(2,128)(2,1)} %w_ref.9, bf16[32,3584]{1,0:T(8,128)(2,1)S(1)} %copy-done.5), custom_call_target="tpu_custom_call" | custom-call | bytes 12845056 | tf_op jit(solution)/shard_map/unpair/pallas_call | solution.py:62
  149.6 2.6 %copy-done = bf16[2,896,1792]{2,1,0:T(8,128)(2,1)} copy-done((bf16[2,896,1792]{2,1,0:T(8,128)(2,1)}, bf16[2,896,1792]{2,1,0:T(8,128)(2,1)S(1)}, u32[]{:S(2)}) %copy-start) | copy-done | bytes 6422552
  152.9 3.8 %unpair.5.refs_17_ = bf16[2,896,1792]{2,1,0:T(8,128)(2,1)S(1)} custom-call(bf16[3584,2,1792]{2,1,0:T(2,128)(2,1)} %w_ref.9, bf16[32,3584]{1,0:T(8,128)(2,1)S(1)} %copy-done.7), custom_call_target="tpu_custom_call" | custom-call | bytes 12845056 | tf_op jit(solution)/shard_map/unpair/pallas_call | solution.py:62
  156.7 2.7 %copy-done.1 = bf16[2,896,1792]{2,1,0:T(8,128)(2,1)} copy-done((bf16[2,896,1792]{2,1,0:T(8,128)(2,1)}, bf16[2,896,1792]{2,1,0:T(8,128)(2,1)S(1)}, u32[]{:S(2)}) %copy-start.1) | copy-done | bytes 6422552
  159.4 3.8 %unpair.6.refs_18_ = bf16[2,896,1792]{2,1,0:T(8,128)(2,1)S(1)} custom-call(bf16[3584,2,1792]{2,1,0:T(2,128)(2,1)} %w_ref.9, bf16[32,3584]{1,0:T(8,128)(2,1)S(1)} %copy-done.9), custom_call_target="tpu_custom_call" | custom-call | bytes 12845056 | tf_op jit(solution)/shard_map/unpair/pallas_call | solution.py:62
  163.2 2.6 %copy-done.2 = bf16[2,896,1792]{2,1,0:T(8,128)(2,1)} copy-done((bf16[2,896,1792]{2,1,0:T(8,128)(2,1)}, bf16[2,896,1792]{2,1,0:T(8,128)(2,1)S(1)}, u32[]{:S(2)}) %copy-start.2) | copy-done | bytes 6422552
  165.8 3.7 %unpair.7.refs_19_ = bf16[2,896,1792]{2,1,0:T(8,128)(2,1)S(1)} custom-call(bf16[3584,2,1792]{2,1,0:T(2,128)(2,1)} %w_ref.9, bf16[32,3584]{1,0:T(8,128)(2,1)S(1)} %copy-done.11), custom_call_target="tpu_custom_call" | custom-call | bytes 12845056 | tf_op jit(solution)/shard_map/unpair/pallas_call | solution.py:62
  169.6 2.7 %copy-done.3 = bf16[2,896,1792]{2,1,0:T(8,128)(2,1)} copy-done((bf16[2,896,1792]{2,1,0:T(8,128)(2,1)}, bf16[2,896,1792]{2,1,0:T(8,128)(2,1)S(1)}, u32[]{:S(2)}) %copy-start.3) | copy-done | bytes 6422552
  173.7 15.9 %gate_up.1.x_ref = bf16[256,1792]{1,0:T(8,128)(2,1)} custom-call(s32[2]{0:T(128)} %pad_add_fusion.place_ref, f32[2,1,1792]{2,1,0:T(1,128)} %reshape.15.gain_ref, bf16[64,896]{1,0:T(8,128)(2,1)} %copy-done.18, bf16[64,896]{1,0:T(8,128)(2,1)} %copy-done.20, bf16[64,896]{1,0:T(8,128)(2,1)} %copy-done.24, bf16[64,896]{1,0:T(8,128)(2,1)} %copy-done.26, ...), custom_call_target="tpu_custom_call" | custom-call | flops 6576668672 | bytes 25690112 | tf_op jit(solution)/shard_map/gate_up/pallas_call | solution.py:296
  189.7 7.7 %down_half.3 = bf16[256,1792]{1,0:T(8,128)(2,1)} custom-call(s32[1]{0:T(128)} %bitcast.17.side_ref, bf16[256,1792]{1,0:T(8,128)(2,1)} %gate_up.1.x_ref, bf16[1792,3584]{1,0:T(8,128)(2,1)} %w_ref.11), custom_call_target="tpu_custom_call" | custom-call | flops 1644167168 | bytes 6422528 | tf_op jit(solution)/shard_map/down_half/pallas_call | solution.py:322
  197.8 7.9 %down_half.2 = f32[256,1792]{1,0:T(8,128)} custom-call(s32[1]{0:T(128)} %bitcast.1.side_ref, bf16[256,1792]{1,0:T(8,128)(2,1)} %gate_up.1.x_ref, bf16[1792,3584]{1,0:T(8,128)(2,1)} %w_ref.11), custom_call_target="tpu_custom_call" | custom-call | flops 1644167168 | bytes 6422528 | tf_op jit(solution)/shard_map/down_half/pallas_call | solution.py:322
  205.6 1.7 fusion.22
  207.6 7.7 %collective-permute-done.44 = bf16[64,896]{1,0:T(8,128)(2,1)S(1)} collective-permute-done((bf16[64,896]{1,0:T(8,128)(2,1)S(1)}, bf16[64,896]{1,0:T(8,128)(2,1)S(1)}, u32[]{:S(2)}, u32[]{:S(2)}) %collective-permute-start.44) | collective-permute-done | bytes 114720 | tf_op jit(solution)/shard_map/ppermute | solution.py:353
  215.3 1.5 collective-permute-done.47
  217.1 7.1 %collective-permute-done.45 = bf16[64,896]{1,0:T(8,128)(2,1)S(1)} collective-permute-done((bf16[64,896]{1,0:T(8,128)(2,1)S(1)}, bf16[64,896]{1,0:T(8,128)(2,1)S(1)}, u32[]{:S(2)}, u32[]{:S(2)}) %collective-permute-start.45) | collective-permute-done | bytes 114720 | tf_op jit(solution)/shard_map/ppermute | solution.py:353
  224.2 1.2 collective-permute-done.48
  225.7 6.4 %collective-permute-done.46 = bf16[64,896]{1,0:T(8,128)(2,1)S(1)} collective-permute-done((bf16[64,896]{1,0:T(8,128)(2,1)S(1)}, bf16[64,896]{1,0:T(8,128)(2,1)S(1)}, u32[]{:S(2)}, u32[]{:S(2)}) %collective-permute-start.46) | collective-permute-done | bytes 114720 | tf_op jit(solution)/shard_map/ppermute | solution.py:353
  (197 shorter events, 23.1 us)
Async XLA Ops:
  2.7 10.7 %collective-permute-start.15 = (bf16[32,3584]{1,0:T(8,128)(2,1)S(1)}, bf16[32,3584]{1,0:T(8,128)(2,1)S(1)}, u32[]{:S(2)}, u32[]{:S(2)}) collective-permute-start(bf16[32,3584]{1,0:T(8,128)(2,1)S(1)} %get-tuple-element.7.refs_0_._), channel_id=1, source_target_pairs={{0,2},{1,3},{2,4},{3,5},{4,6},{5,7},{6,0},{7,1},{8,10},{9,11},{10,... | collective-permute-start | bytes 688136 | tf_op jit(solution)/shard_map/ppermute | solution.py:353
  8.9 10.5 %collective-permute-start.1 = (bf16[32,3584]{1,0:T(8,128)(2,1)S(1)}, bf16[32,3584]{1,0:T(8,128)(2,1)}, u32[]{:S(2)}, u32[]{:S(2)}) collective-permute-start(bf16[32,3584]{1,0:T(8,128)(2,1)S(1)} %get-tuple-element.6.refs_0_), channel_id=1, source_target_pairs={{0,2},{1,3},{2,4},{3,5},{4,6},{5,7},{6,0},{7,1},{8,10},{9,11},{10,... | collective-permute-start | bytes 688136 | tf_op jit(solution)/shard_map/ppermute | solution.py:353
  13.4 17.9 %collective-permute-start.17 = (bf16[32,3584]{1,0:T(8,128)(2,1)S(1)}, bf16[32,3584]{1,0:T(8,128)(2,1)S(1)}, u32[]{:S(2)}, u32[]{:S(2)}) collective-permute-start(bf16[32,3584]{1,0:T(8,128)(2,1)S(1)} %collective-permute-done.15.refs_2_._), channel_id=1, source_target_pairs={{0,2},{1,3},{2,4},{3,5},{4,6},{5,7},{6,0},{7,1},{8,10},{9,11},{10,... | collective-permute-start | bytes 688136 | tf_op jit(solution)/shard_map/ppermute | solution.py:353
  14.5 12.4 %collective-permute-start.10 = (bf16[2,128,224]{2,1,0:T(8,128)(2,1)S(1)}, bf16[2,128,224]{2,1,0:T(8,128)(2,1)S(1)}, u32[]{:S(2)}, u32[]{:S(2)}) collective-permute-start(bf16[2,128,224]{2,1,0:T(8,128)(2,1)S(1)} %get-tuple-element.33), channel_id=1, source_target_pairs={{0,6},{1,7},{2,4},{3,5},{4,2},{5,3},{6,0},{7,1},{8,14},{9,15},{10,... | collective-permute-start | bytes 344072 | tf_op jit(solution)/shard_map/ppermute | solution.py:396
  18.3 11.0 %collective-permute-start.8 = (bf16[2,128,224]{2,1,0:T(8,128)(2,1)S(1)}, bf16[2,128,224]{2,1,0:T(8,128)(2,1)S(1)}, u32[]{:S(2)}, u32[]{:S(2)}) collective-permute-start(bf16[2,128,224]{2,1,0:T(8,128)(2,1)S(1)} %get-tuple-element.31), channel_id=1, source_target_pairs={{0,2},{1,3},{2,0},{3,1},{4,6},{5,7},{6,4},{7,5},{8,10},{9,11},{10,... | collective-permute-start | bytes 344072 | tf_op jit(solution)/shard_map/ppermute | solution.py:396
  18.3 26.3 %collective-permute-start.9 = (bf16[2,128,224]{2,1,0:T(8,128)(2,1)S(1)}, bf16[2,128,224]{2,1,0:T(8,128)(2,1)S(1)}, u32[]{:S(2)}, u32[]{:S(2)}) collective-permute-start(bf16[2,128,224]{2,1,0:T(8,128)(2,1)S(1)} %get-tuple-element.32), channel_id=1, source_target_pairs={{0,4},{1,5},{2,6},{3,7},{4,0},{5,1},{6,2},{7,3},{8,12},{9,13},{10,... | collective-permute-start | bytes 344072 | tf_op jit(solution)/shard_map/ppermute | solution.py:396
  19.4 25.5 %collective-permute-start.14 = (bf16[32,3584]{1,0:T(8,128)(2,1)S(1)}, bf16[32,3584]{1,0:T(8,128)(2,1)S(1)}, u32[]{:S(2)}, u32[]{:S(2)}) collective-permute-start(bf16[32,3584]{1,0:T(8,128)(2,1)S(1)} %get-tuple-element.7.refs_0_._), channel_id=1, source_target_pairs={{0,1},{1,0},{2,3},{3,2},{4,5},{5,4},{6,7},{7,6},{8,9},{9,8},{10,11... | collective-permute-start | bytes 688136 | tf_op jit(solution)/shard_map/ppermute | solution.py:350
  27.0 20.4 %collective-permute-start.16 = (bf16[32,3584]{1,0:T(8,128)(2,1)S(1)}, bf16[32,3584]{1,0:T(8,128)(2,1)S(1)}, u32[]{:S(2)}, u32[]{:S(2)}) collective-permute-start(bf16[32,3584]{1,0:T(8,128)(2,1)S(1)} %collective-permute-done.15.refs_2_._), channel_id=1, source_target_pairs={{0,1},{1,0},{2,3},{3,2},{4,5},{5,4},{6,7},{7,6},{8,9},{9,8},{10,11... | collective-permute-start | bytes 688136 | tf_op jit(solution)/shard_map/ppermute | solution.py:350
  29.3 18.5 %collective-permute-start.3 = (bf16[32,3584]{1,0:T(8,128)(2,1)}, bf16[32,3584]{1,0:T(8,128)(2,1)S(1)}, u32[]{:S(2)}, u32[]{:S(2)}) collective-permute-start(bf16[32,3584]{1,0:T(8,128)(2,1)} %collective-permute-done.1.refs_2_), channel_id=1, source_target_pairs={{0,2},{1,3},{2,4},{3,5},{4,6},{5,7},{6,0},{7,1},{8,10},{9,11},{10,... | collective-permute-start | bytes 688136 | tf_op jit(solution)/shard_map/ppermute | solution.py:353
  31.3 18.0 %collective-permute-start.19 = (bf16[32,3584]{1,0:T(8,128)(2,1)S(1)}, bf16[32,3584]{1,0:T(8,128)(2,1)S(1)}, u32[]{:S(2)}, u32[]{:S(2)}) collective-permute-start(bf16[32,3584]{1,0:T(8,128)(2,1)S(1)} %collective-permute-done.17.refs_4_._), channel_id=1, source_target_pairs={{0,2},{1,3},{2,4},{3,5},{4,6},{5,7},{6,0},{7,1},{8,10},{9,11},{10,... | collective-permute-start | bytes 688136 | tf_op jit(solution)/shard_map/ppermute | solution.py:353
  44.7 4.6 %collective-permute-start.18 = (bf16[32,3584]{1,0:T(8,128)(2,1)S(1)}, bf16[32,3584]{1,0:T(8,128)(2,1)}, u32[]{:S(2)}, u32[]{:S(2)}) collective-permute-start(bf16[32,3584]{1,0:T(8,128)(2,1)S(1)} %collective-permute-done.17.refs_4_._), channel_id=1, source_target_pairs={{0,1},{1,0},{2,3},{3,2},{4,5},{5,4},{6,7},{7,6},{8,9},{9,8},{10,11... | collective-permute-start | bytes 688136 | tf_op jit(solution)/shard_map/ppermute | solution.py:350
  44.8 19.0 %collective-permute-start.11 = (bf16[2,512,224]{2,1,0:T(8,128)(2,1)S(1)}, bf16[2,512,224]{2,1,0:T(8,128)(2,1)}, u32[]{:S(2)}, u32[]{:S(2)}) collective-permute-start(bf16[2,512,224]{2,1,0:T(8,128)(2,1)S(1)} %pad_maximum_fusion), channel_id=1, source_target_pairs={{0,24},{8,16},{16,8},{24,0},{1,25},{9,17},{17,9},{25,1},{2,26},{10... | collective-permute-start | bytes 1376264 | tf_op jit(solution)/shard_map/ppermute | solution.py:402
  47.3 24.1 %collective-permute-start.12 = (bf16[2,512,224]{2,1,0:T(8,128)(2,1)S(1)}, bf16[2,512,224]{2,1,0:T(8,128)(2,1)}, u32[]{:S(2)}, u32[]{:S(2)}) collective-permute-start(bf16[2,512,224]{2,1,0:T(8,128)(2,1)S(1)} %pad_maximum_fusion), channel_id=1, source_target_pairs={{0,16},{8,24},{16,0},{24,8},{1,17},{9,25},{17,1},{25,9},{2,18},{10... | collective-permute-start | bytes 1376264 | tf_op jit(solution)/shard_map/ppermute | solution.py:402
  48.7 22.8 %collective-permute-start.13 = (bf16[2,512,224]{2,1,0:T(8,128)(2,1)S(1)}, bf16[2,512,224]{2,1,0:T(8,128)(2,1)}, u32[]{:S(2)}, u32[]{:S(2)}) collective-permute-start(bf16[2,512,224]{2,1,0:T(8,128)(2,1)S(1)} %pad_maximum_fusion), channel_id=1, source_target_pairs={{0,8},{8,0},{16,24},{24,16},{1,9},{9,1},{17,25},{25,17},{2,10},{10... | collective-permute-start | bytes 1376264 | tf_op jit(solution)/shard_map/ppermute | solution.py:402
  49.3 9.5 %collective-permute-start.5 = (bf16[32,3584]{1,0:T(8,128)(2,1)}, bf16[32,3584]{1,0:T(8,128)(2,1)S(1)}, u32[]{:S(2)}, u32[]{:S(2)}) collective-permute-start(bf16[32,3584]{1,0:T(8,128)(2,1)} %copy-done.28), channel_id=1, source_target_pairs={{0,2},{1,3},{2,4},{3,5},{4,6},{5,7},{6,0},{7,1},{8,10},{9,11},{10,... | collective-permute-start | bytes 688136 | tf_op jit(solution)/shard_map/ppermute | solution.py:353
  49.3 22.7 %collective-permute-start.20 = (bf16[32,3584]{1,0:T(8,128)(2,1)S(1)}, bf16[32,3584]{1,0:T(8,128)(2,1)}, u32[]{:S(2)}, u32[]{:S(2)}) collective-permute-start(bf16[32,3584]{1,0:T(8,128)(2,1)S(1)} %collective-permute-done.19.refs_6_._), channel_id=1, source_target_pairs={{0,1},{1,0},{2,3},{3,2},{4,5},{5,4},{6,7},{7,6},{8,9},{9,8},{10,11... | collective-permute-start | bytes 688136 | tf_op jit(solution)/shard_map/ppermute | solution.py:350
  59.4 30.6 %collective-permute-start.22 = (bf16[224,1792]{1,0:T(8,128)(2,1)}, bf16[224,1792]{1,0:T(8,128)(2,1)S(1)}, u32[]{:S(2)}, u32[]{:S(2)}) collective-permute-start(bf16[224,1792]{1,0:T(8,128)(2,1)} %get-tuple-element.24), channel_id=1, source_target_pairs={{0,1},{1,0},{2,3},{3,2},{4,5},{5,4},{6,7},{7,6},{8,9},{9,8},{10,11... | collective-permute-start | bytes 2408456 | tf_op jit(solution)/shard_map/ppermute | solution.py:350
  63.9 16.9 %collective-permute-start = (bf16[32,3584]{1,0:T(8,128)(2,1)S(1)}, bf16[32,3584]{1,0:T(8,128)(2,1)S(1)}, u32[]{:S(2)}, u32[]{:S(2)}) collective-permute-start(bf16[32,3584]{1,0:T(8,128)(2,1)S(1)} %get-tuple-element.6.refs_0_), channel_id=1, source_target_pairs={{0,1},{1,0},{2,3},{3,2},{4,5},{5,4},{6,7},{7,6},{8,9},{9,8},{10,11... | collective-permute-start | bytes 688136 | tf_op jit(solution)/shard_map/ppermute | solution.py:350
  71.5 9.4 %collective-permute-start.2 = (bf16[32,3584]{1,0:T(8,128)(2,1)}, bf16[32,3584]{1,0:T(8,128)(2,1)S(1)}, u32[]{:S(2)}, u32[]{:S(2)}) collective-permute-start(bf16[32,3584]{1,0:T(8,128)(2,1)} %collective-permute-done.1.refs_2_), channel_id=1, source_target_pairs={{0,1},{1,0},{2,3},{3,2},{4,5},{5,4},{6,7},{7,6},{8,9},{9,8},{10,11... | collective-permute-start | bytes 688136 | tf_op jit(solution)/shard_map/ppermute | solution.py:350
  71.6 9.3 %collective-permute-start.4 = (bf16[32,3584]{1,0:T(8,128)(2,1)}, bf16[32,3584]{1,0:T(8,128)(2,1)S(1)}, u32[]{:S(2)}, u32[]{:S(2)}) collective-permute-start(bf16[32,3584]{1,0:T(8,128)(2,1)} %copy-done.28), channel_id=1, source_target_pairs={{0,1},{1,0},{2,3},{3,2},{4,5},{5,4},{6,7},{7,6},{8,9},{9,8},{10,11... | collective-permute-start | bytes 688136 | tf_op jit(solution)/shard_map/ppermute | solution.py:350
  72.0 8.9 %collective-permute-start.6 = (bf16[32,3584]{1,0:T(8,128)(2,1)}, bf16[32,3584]{1,0:T(8,128)(2,1)S(1)}, u32[]{:S(2)}, u32[]{:S(2)}) collective-permute-start(bf16[32,3584]{1,0:T(8,128)(2,1)} %copy-done.29), channel_id=1, source_target_pairs={{0,1},{1,0},{2,3},{3,2},{4,5},{5,4},{6,7},{7,6},{8,9},{9,8},{10,11... | collective-permute-start | bytes 688136 | tf_op jit(solution)/shard_map/ppermute | solution.py:350
  96.8 7.8 %collective-permute-start.23 = (bf16[64,896]{1,0:T(8,128)(2,1)S(1)}, bf16[64,896]{1,0:T(8,128)(2,1)S(1)}, u32[]{:S(2)}, u32[]{:S(2)}) collective-permute-start(bf16[64,896]{1,0:T(8,128)(2,1)S(1)} %get-tuple-element.28), channel_id=1, source_target_pairs={{0,2},{1,3},{2,4},{3,5},{4,6},{5,7},{6,0},{7,1},{8,10},{9,11},{10,... | collective-permute-start | bytes 344072 | tf_op jit(solution)/shard_map/ppermute | solution.py:353
  96.8 9.6 %collective-permute-start.26 = (bf16[64,896]{1,0:T(8,128)(2,1)S(1)}, bf16[64,896]{1,0:T(8,128)(2,1)S(1)}, u32[]{:S(2)}, u32[]{:S(2)}) collective-permute-start(bf16[64,896]{1,0:T(8,128)(2,1)S(1)} %get-tuple-element.29), channel_id=1, source_target_pairs={{0,2},{1,3},{2,4},{3,5},{4,6},{5,7},{6,0},{7,1},{8,10},{9,11},{10,... | collective-permute-start | bytes 344072 | tf_op jit(solution)/shard_map/ppermute | solution.py:353
  106.5 7.7 %collective-permute-start.24 = (bf16[64,896]{1,0:T(8,128)(2,1)S(1)}, bf16[64,896]{1,0:T(8,128)(2,1)S(1)}, u32[]{:S(2)}, u32[]{:S(2)}) collective-permute-start(bf16[64,896]{1,0:T(8,128)(2,1)S(1)} %get-tuple-element.22), channel_id=1, source_target_pairs={{0,2},{1,3},{2,4},{3,5},{4,6},{5,7},{6,0},{7,1},{8,10},{9,11},{10,... | collective-permute-start | bytes 344072 | tf_op jit(solution)/shard_map/ppermute | solution.py:353
  106.6 8.8 %collective-permute-start.27 = (bf16[64,896]{1,0:T(8,128)(2,1)S(1)}, bf16[64,896]{1,0:T(8,128)(2,1)S(1)}, u32[]{:S(2)}, u32[]{:S(2)}) collective-permute-start(bf16[64,896]{1,0:T(8,128)(2,1)S(1)} %get-tuple-element.23), channel_id=1, source_target_pairs={{0,2},{1,3},{2,4},{3,5},{4,6},{5,7},{6,0},{7,1},{8,10},{9,11},{10,... | collective-permute-start | bytes 344072 | tf_op jit(solution)/shard_map/ppermute | solution.py:353
  115.5 6.8 %collective-permute-start.25 = (bf16[64,896]{1,0:T(8,128)(2,1)S(1)}, bf16[64,896]{1,0:T(8,128)(2,1)S(1)}, u32[]{:S(2)}, u32[]{:S(2)}) collective-permute-start(bf16[64,896]{1,0:T(8,128)(2,1)S(1)} %get-tuple-element.20), channel_id=1, source_target_pairs={{0,2},{1,3},{2,4},{3,5},{4,6},{5,7},{6,0},{7,1},{8,10},{9,11},{10,... | collective-permute-start | bytes 344072 | tf_op jit(solution)/shard_map/ppermute | solution.py:353
  115.6 7.9 %collective-permute-start.28 = (bf16[64,896]{1,0:T(8,128)(2,1)S(1)}, bf16[64,896]{1,0:T(8,128)(2,1)S(1)}, u32[]{:S(2)}, u32[]{:S(2)}) collective-permute-start(bf16[64,896]{1,0:T(8,128)(2,1)S(1)} %get-tuple-element.21), channel_id=1, source_target_pairs={{0,2},{1,3},{2,4},{3,5},{4,6},{5,7},{6,0},{7,1},{8,10},{9,11},{10,... | collective-permute-start | bytes 344072 | tf_op jit(solution)/shard_map/ppermute | solution.py:353
  123.6 6.6 %collective-permute-start.31 = (bf16[64,896]{1,0:T(8,128)(2,1)S(1)}, bf16[64,896]{1,0:T(8,128)(2,1)S(1)}, u32[]{:S(2)}, u32[]{:S(2)}) collective-permute-start(bf16[64,896]{1,0:T(8,128)(2,1)S(1)} %get-tuple-element.18.refs_0_), channel_id=1, source_target_pairs={{0,2},{1,3},{2,4},{3,5},{4,6},{5,7},{6,0},{7,1},{8,10},{9,11},{10,... | collective-permute-start | bytes 344072 | tf_op jit(solution)/shard_map/ppermute | solution.py:353
  123.6 8.0 %collective-permute-start.32 = (bf16[64,896]{1,0:T(8,128)(2,1)S(1)}, bf16[64,896]{1,0:T(8,128)(2,1)S(1)}, u32[]{:S(2)}, u32[]{:S(2)}) collective-permute-start(bf16[64,896]{1,0:T(8,128)(2,1)S(1)} %get-tuple-element.19.refs_1_), channel_id=1, source_target_pairs={{0,2},{1,3},{2,4},{3,5},{4,6},{5,7},{6,0},{7,1},{8,10},{9,11},{10,... | collective-permute-start | bytes 344072 | tf_op jit(solution)/shard_map/ppermute | solution.py:353
  130.2 6.6 %collective-permute-start.35 = (bf16[64,896]{1,0:T(8,128)(2,1)S(1)}, bf16[64,896]{1,0:T(8,128)(2,1)S(1)}, u32[]{:S(2)}, u32[]{:S(2)}) collective-permute-start(bf16[64,896]{1,0:T(8,128)(2,1)S(1)} %collective-permute-done.31.refs_4_), channel_id=1, source_target_pairs={{0,2},{1,3},{2,4},{3,5},{4,6},{5,7},{6,0},{7,1},{8,10},{9,11},{10,... | collective-permute-start | bytes 344072 | tf_op jit(solution)/shard_map/ppermute | solution.py:353
  131.6 7.5 %collective-permute-start.36 = (bf16[64,896]{1,0:T(8,128)(2,1)S(1)}, bf16[64,896]{1,0:T(8,128)(2,1)S(1)}, u32[]{:S(2)}, u32[]{:S(2)}) collective-permute-start(bf16[64,896]{1,0:T(8,128)(2,1)S(1)} %collective-permute-done.32.refs_5_), channel_id=1, source_target_pairs={{0,2},{1,3},{2,4},{3,5},{4,6},{5,7},{6,0},{7,1},{8,10},{9,11},{10,... | collective-permute-start | bytes 344072 | tf_op jit(solution)/shard_map/ppermute | solution.py:353
  131.6 7.5 %collective-permute-start.29 = (bf16[64,896]{1,0:T(8,128)(2,1)S(1)}, bf16[64,896]{1,0:T(8,128)(2,1)S(1)}, u32[]{:S(2)}, u32[]{:S(2)}) collective-permute-start(bf16[64,896]{1,0:T(8,128)(2,1)S(1)} %get-tuple-element.18.refs_0_), channel_id=1, source_target_pairs={{0,1},{1,0},{2,3},{3,2},{4,5},{5,4},{6,7},{7,6},{8,9},{9,8},{10,11... | collective-permute-start | bytes 344072 | tf_op jit(solution)/shard_map/ppermute | solution.py:350
  131.7 7.6 %collective-permute-start.30 = (bf16[64,896]{1,0:T(8,128)(2,1)S(1)}, bf16[64,896]{1,0:T(8,128)(2,1)S(1)}, u32[]{:S(2)}, u32[]{:S(2)}) collective-permute-start(bf16[64,896]{1,0:T(8,128)(2,1)S(1)} %get-tuple-element.19.refs_1_), channel_id=1, source_target_pairs={{0,1},{1,0},{2,3},{3,2},{4,5},{5,4},{6,7},{7,6},{8,9},{9,8},{10,11... | collective-permute-start | bytes 344072 | tf_op jit(solution)/shard_map/ppermute | solution.py:350
  132.2 7.6 %collective-permute-start.33 = (bf16[64,896]{1,0:T(8,128)(2,1)S(1)}, bf16[64,896]{1,0:T(8,128)(2,1)S(1)}, u32[]{:S(2)}, u32[]{:S(2)}) collective-permute-start(bf16[64,896]{1,0:T(8,128)(2,1)S(1)} %collective-permute-done.31.refs_4_), channel_id=1, source_target_pairs={{0,1},{1,0},{2,3},{3,2},{4,5},{5,4},{6,7},{7,6},{8,9},{9,8},{10,11... | collective-permute-start | bytes 344072 | tf_op jit(solution)/shard_map/ppermute | solution.py:350
  136.8 6.6 %collective-permute-start.39 = (bf16[64,896]{1,0:T(8,128)(2,1)S(1)}, bf16[64,896]{1,0:T(8,128)(2,1)S(1)}, u32[]{:S(2)}, u32[]{:S(2)}) collective-permute-start(bf16[64,896]{1,0:T(8,128)(2,1)S(1)} %collective-permute-done.35.refs_8_), channel_id=1, source_target_pairs={{0,2},{1,3},{2,4},{3,5},{4,6},{5,7},{6,0},{7,1},{8,10},{9,11},{10,... | collective-permute-start | bytes 344072 | tf_op jit(solution)/shard_map/ppermute | solution.py:353
  139.1 6.6 %collective-permute-start.40 = (bf16[64,896]{1,0:T(8,128)(2,1)S(1)}, bf16[64,896]{1,0:T(8,128)(2,1)S(1)}, u32[]{:S(2)}, u32[]{:S(2)}) collective-permute-start(bf16[64,896]{1,0:T(8,128)(2,1)S(1)} %collective-permute-done.36.refs_9_), channel_id=1, source_target_pairs={{0,2},{1,3},{2,4},{3,5},{4,6},{5,7},{6,0},{7,1},{8,10},{9,11},{10,... | collective-permute-start | bytes 344072 | tf_op jit(solution)/shard_map/ppermute | solution.py:353
  139.1 33.1 %collective-permute-start.34 = (bf16[64,896]{1,0:T(8,128)(2,1)S(1)}, bf16[64,896]{1,0:T(8,128)(2,1)S(1)}, u32[]{:S(2)}, u32[]{:S(2)}) collective-permute-start(bf16[64,896]{1,0:T(8,128)(2,1)S(1)} %collective-permute-done.32.refs_5_), channel_id=1, source_target_pairs={{0,1},{1,0},{2,3},{3,2},{4,5},{5,4},{6,7},{7,6},{8,9},{9,8},{10,11... | collective-permute-start | bytes 344072 | tf_op jit(solution)/shard_map/ppermute | solution.py:350
  139.2 33.0 %collective-permute-start.37 = (bf16[64,896]{1,0:T(8,128)(2,1)S(1)}, bf16[64,896]{1,0:T(8,128)(2,1)S(1)}, u32[]{:S(2)}, u32[]{:S(2)}) collective-permute-start(bf16[64,896]{1,0:T(8,128)(2,1)S(1)} %collective-permute-done.35.refs_8_), channel_id=1, source_target_pairs={{0,1},{1,0},{2,3},{3,2},{4,5},{5,4},{6,7},{7,6},{8,9},{9,8},{10,11... | collective-permute-start | bytes 344072 | tf_op jit(solution)/shard_map/ppermute | solution.py:350
  139.7 32.6 %collective-permute-start.38 = (bf16[64,896]{1,0:T(8,128)(2,1)S(1)}, bf16[64,896]{1,0:T(8,128)(2,1)S(1)}, u32[]{:S(2)}, u32[]{:S(2)}) collective-permute-start(bf16[64,896]{1,0:T(8,128)(2,1)S(1)} %collective-permute-done.36.refs_9_), channel_id=1, source_target_pairs={{0,1},{1,0},{2,3},{3,2},{4,5},{5,4},{6,7},{7,6},{8,9},{9,8},{10,11... | collective-permute-start | bytes 344072 | tf_op jit(solution)/shard_map/ppermute | solution.py:350
  143.4 28.9 %collective-permute-start.41 = (bf16[64,896]{1,0:T(8,128)(2,1)S(1)}, bf16[64,896]{1,0:T(8,128)(2,1)S(1)}, u32[]{:S(2)}, u32[]{:S(2)}) collective-permute-start(bf16[64,896]{1,0:T(8,128)(2,1)S(1)} %collective-permute-done.39.refs_12_), channel_id=1, source_target_pairs={{0,1},{1,0},{2,3},{3,2},{4,5},{5,4},{6,7},{7,6},{8,9},{9,8},{10,11... | collective-permute-start | bytes 344072 | tf_op jit(solution)/shard_map/ppermute | solution.py:350
  145.7 26.6 %collective-permute-start.42 = (bf16[64,896]{1,0:T(8,128)(2,1)S(1)}, bf16[64,896]{1,0:T(8,128)(2,1)S(1)}, u32[]{:S(2)}, u32[]{:S(2)}) collective-permute-start(bf16[64,896]{1,0:T(8,128)(2,1)S(1)} %collective-permute-done.40.refs_13_), channel_id=1, source_target_pairs={{0,1},{1,0},{2,3},{3,2},{4,5},{5,4},{6,7},{7,6},{8,9},{9,8},{10,11... | collective-permute-start | bytes 344072 | tf_op jit(solution)/shard_map/ppermute | solution.py:350
  197.3 8.3 %collective-permute-start.43 = (bf16[256,1792]{1,0:T(8,128)(2,1)}, bf16[256,1792]{1,0:T(8,128)(2,1)S(1)}, u32[]{:S(2)}, u32[]{:S(2)}) collective-permute-start(bf16[256,1792]{1,0:T(8,128)(2,1)} %down_half.3), channel_id=1, source_target_pairs={{0,1},{1,0},{2,3},{3,2},{4,5},{5,4},{6,7},{7,6},{8,9},{9,8},{10,11... | collective-permute-start | bytes 2752520 | tf_op jit(solution)/shard_map/ppermute | solution.py:350
  207.4 7.9 %collective-permute-start.44 = (bf16[64,896]{1,0:T(8,128)(2,1)S(1)}, bf16[64,896]{1,0:T(8,128)(2,1)S(1)}, u32[]{:S(2)}, u32[]{:S(2)}) collective-permute-start(bf16[64,896]{1,0:T(8,128)(2,1)S(1)} %get-tuple-element.27), channel_id=1, source_target_pairs={{0,2},{1,3},{2,4},{3,5},{4,6},{5,7},{6,0},{7,1},{8,10},{9,11},{10,... | collective-permute-start | bytes 344072 | tf_op jit(solution)/shard_map/ppermute | solution.py:353
  207.5 9.3 %collective-permute-start.47 = (bf16[64,896]{1,0:T(8,128)(2,1)S(1)}, bf16[64,896]{1,0:T(8,128)(2,1)S(1)}, u32[]{:S(2)}, u32[]{:S(2)}) collective-permute-start(bf16[64,896]{1,0:T(8,128)(2,1)S(1)} %get-tuple-element.26), channel_id=1, source_target_pairs={{0,2},{1,3},{2,4},{3,5},{4,6},{5,7},{6,0},{7,1},{8,10},{9,11},{10,... | collective-permute-start | bytes 344072 | tf_op jit(solution)/shard_map/ppermute | solution.py:353
  216.9 7.3 %collective-permute-start.45 = (bf16[64,896]{1,0:T(8,128)(2,1)S(1)}, bf16[64,896]{1,0:T(8,128)(2,1)S(1)}, u32[]{:S(2)}, u32[]{:S(2)}) collective-permute-start(bf16[64,896]{1,0:T(8,128)(2,1)S(1)} %get-tuple-element.17), channel_id=1, source_target_pairs={{0,2},{1,3},{2,4},{3,5},{4,6},{5,7},{6,0},{7,1},{8,10},{9,11},{10,... | collective-permute-start | bytes 344072 | tf_op jit(solution)/shard_map/ppermute | solution.py:353
  217.0 8.5 %collective-permute-start.48 = (bf16[64,896]{1,0:T(8,128)(2,1)S(1)}, bf16[64,896]{1,0:T(8,128)(2,1)S(1)}, u32[]{:S(2)}, u32[]{:S(2)}) collective-permute-start(bf16[64,896]{1,0:T(8,128)(2,1)S(1)} %get-tuple-element.16), channel_id=1, source_target_pairs={{0,2},{1,3},{2,4},{3,5},{4,6},{5,7},{6,0},{7,1},{8,10},{9,11},{10,... | collective-permute-start | bytes 344072 | tf_op jit(solution)/shard_map/ppermute | solution.py:353
  225.5 6.6 %collective-permute-start.46 = (bf16[64,896]{1,0:T(8,128)(2,1)S(1)}, bf16[64,896]{1,0:T(8,128)(2,1)S(1)}, u32[]{:S(2)}, u32[]{:S(2)}) collective-permute-start(bf16[64,896]{1,0:T(8,128)(2,1)S(1)} %get-tuple-element.15), channel_id=1, source_target_pairs={{0,2},{1,3},{2,4},{3,5},{4,6},{5,7},{6,0},{7,1},{8,10},{9,11},{10,... | collective-permute-start | bytes 344072 | tf_op jit(solution)/shard_map/ppermute | solution.py:353
  225.6 7.8 %collective-permute-start.49 = (bf16[64,896]{1,0:T(8,128)(2,1)S(1)}, bf16[64,896]{1,0:T(8,128)(2,1)S(1)}, u32[]{:S(2)}, u32[]{:S(2)}) collective-permute-start(bf16[64,896]{1,0:T(8,128)(2,1)S(1)} %get-tuple-element.14), channel_id=1, source_target_pairs={{0,2},{1,3},{2,4},{3,5},{4,6},{5,7},{6,0},{7,1},{8,10},{9,11},{10,... | collective-permute-start | bytes 344072 | tf_op jit(solution)/shard_map/ppermute | solution.py:353
  (55 other events, 631.0 us)

commit v3 on v1

v3 whole, which is shorter than its diff:
```python
import functools

import jax
import jax.numpy as jnp
from jax import lax
from jax.experimental import pallas as pl
from jax.experimental.pallas import tpu as pltpu
from jax.sharding import PartitionSpec as P

HD = 224
EPS = 1e-05
F32 = jnp.float32
BF16 = jnp.bfloat16
NT = (((1,), (1,)), ((), ()))
TN = (((0,), (0,)), ((), ()))
VMEM = pl.BlockSpec(memory_space=pltpu.VMEM)
SMEM = pl.BlockSpec(memory_space=pltpu.SMEM)
ANY = pl.BlockSpec(memory_space=pl.ANY)
TOKEN = jax.ShapeDtypeStruct((8, 128), F32)
QUICK = pl.CostEstimate(flops=1, bytes_accessed=1, transcendentals=0)
HBM = pl.BlockSpec(memory_space=pltpu.HBM)


def params(mib=56):
    return pltpu.CompilerParams(vmem_limit_bytes=mib * 2**20)


def split_cols(block, count):
    width = block.shape[1] // count
    return [block[:, i * width : (i + 1) * width] for i in range(count)]


def tile_of(width):
    return 256 if width % 256 == 0 else width


def norm_body(tok_ref, gain_ref, *outs):
    t = tok_ref[...].astype(F32)
    scale = lax.rsqrt(jnp.mean(t * t, axis=-1, keepdims=True) + EPS)
    normed = (t * scale * gain_ref[...]).astype(BF16)
    width = t.shape[1] // len(outs)
    for i, out in enumerate(outs):
        out[...] = normed[:, i * width : (i + 1) * width]


def norm_rows(tokens, gain, count):
    rows, width = tokens.shape
    return pl.pallas_call(
        norm_body,
        in_specs=[VMEM, VMEM],
        out_specs=[VMEM] * count,
        out_shape=[jax.ShapeDtypeStruct((rows, width // count), BF16)] * count,
        compiler_params=params(16),
        cost_estimate=QUICK,
        name="norm_rows",
    )(tokens, gain)


def unpair_body(first, w_ref, _, out_ref, token_ref, buf, sems):
    token_ref[...] = jnp.zeros_like(token_ref)
    count, step = buf.shape[:2]

    def fetch(i):
        return pltpu.make_async_copy(w_ref.at[pl.ds(first + i * step, step)], buf.at[i], sems.at[i])

    for i in range(count):
        fetch(i).start()
    for i in range(count):
        fetch(i).wait()
        out_ref[:, i * step : (i + 1) * step, :] = jnp.swapaxes(buf[i], 0, 1)


def unpair(weights, part, parts, after):
    depth, two, width = weights.shape
    rows = depth // parts
    count = 4
    step = rows // count
    return pl.pallas_call(
        functools.partial(unpair_body, part * rows),
        in_specs=[HBM, ANY],
        out_specs=[VMEM] * 2,
        out_shape=[jax.ShapeDtypeStruct((two, rows, width), BF16), TOKEN],
        scratch_shapes=[pltpu.VMEM((count, step, two, width), BF16), pltpu.SemaphoreType.DMA((count,))],
        compiler_params=params(10),
        cost_estimate=QUICK,
        name="unpair",
    )(pltpu.with_memory_space_constraint(weights, pltpu.HBM), after)


def hold_body(place_ref, w_ref, down_ref, _, w_out, down_out, token_ref, sems):
    token_ref[...] = jnp.zeros_like(token_ref)
    copies = [pltpu.make_async_copy(down_ref, down_out, sems.at[0])]
    count = sems.shape[0] - 1
    step = w_ref.shape[0] // count
    for i in range(count):
        rows = pl.ds(i * step, step)
        copies.append(pltpu.make_async_copy(w_ref.at[rows], w_out.at[rows], sems.at[1 + i]))
    for c in copies:
        c.start()
    for c in copies:
        c.wait()


def hold(w_t, down, place, after):
    return pl.pallas_call(
        hold_body,
        in_specs=[SMEM, HBM, HBM, ANY],
        out_specs=[VMEM] * 3,
        out_shape=[jax.ShapeDtypeStruct(w_t.shape, BF16), jax.ShapeDtypeStruct(down.shape, BF16), TOKEN],
        scratch_shapes=[pltpu.SemaphoreType.DMA((7,))],
        compiler_params=params(2),
        cost_estimate=QUICK,
        name="hold",
    )(place, pltpu.with_memory_space_constraint(w_t, pltpu.HBM), pltpu.with_memory_space_constraint(down, pltpu.HBM), after)


def bring_body(flip, place_ref, w_ref, _, out_ref, token_ref, sems):
    token_ref[...] = jnp.zeros_like(token_ref)
    units, half = out_ref.shape
    core = place_ref[1]
    at = pl.multiple_of((1 - core if flip else core) * half, 128)
    count = sems.shape[0]
    step = units // count

    def fetch(i):
        rows = pl.ds(i * step, step)
        return pltpu.make_async_copy(w_ref.at[rows, pl.ds(at, half)], out_ref.at[rows], sems.at[i])

    for i in range(count):
        fetch(i).start()
    for i in range(count):
        fetch(i).wait()


def bring(w_down, place, flip, after):
    units, width = w_down.shape
    return pl.pallas_call(
        functools.partial(bring_body, flip),
        in_specs=[SMEM, HBM, ANY],
        out_specs=[VMEM] * 2,
        out_shape=[jax.ShapeDtypeStruct((units, width // 2), BF16), TOKEN],
        scratch_shapes=[pltpu.SemaphoreType.DMA((4,))],
        compiler_params=params(2),
        cost_estimate=QUICK,
        name="bring",
    )(place, pltpu.with_memory_space_constraint(w_down, pltpu.HBM), after)


def pass_body(_in, _token, _out):
    pass


def pass_on(value, token):
    return pl.pallas_call(
        pass_body,
        in_specs=[ANY, ANY],
        out_specs=ANY,
        out_shape=jax.ShapeDtypeStruct(value.shape, value.dtype),
        input_output_aliases={0: 0},
        compiler_params=params(1),
        cost_estimate=QUICK,
        name="pass_on",
    )(value, token)


def split_body(count, place_ref, owner_ref, group_ref, *refs):
    candidates = refs[:count]
    mine_ref, other_ref = refs[-2:]
    core, req = place_ref[1], place_ref[2]
    away = owner_ref[group_ref[req]] ^ req
    chips = mine_ref.shape[0]
    cols = mine_ref.shape[3]
    chosen = candidates[0][...]
    for k in range(1, count):
        chosen = jnp.where(away == k, candidates[k][...], chosen)
    chosen = jnp.swapaxes(chosen, 0, 1)
    for c in range(chips):
        even = chosen[:, :, 2 * c * cols : (2 * c + 1) * cols]
        odd = chosen[:, :, (2 * c + 1) * cols : (2 * c + 2) * cols]
        mine_ref[c] = jnp.where(core == 0, even, odd)
        other_ref[c] = jnp.where(core == 0, odd, even)


def split_heads(candidates, place, owner, group, chips, ties):
    positions, two, width = candidates[0].shape
    shape = jax.ShapeDtypeStruct((chips, two, positions, width // (2 * chips)), BF16)
    return pl.pallas_call(
        functools.partial(split_body, len(candidates)),
        in_specs=[SMEM] * 3 + [VMEM] * len(candidates) + [ANY] * len(ties),
        out_specs=[VMEM] * 2,
        out_shape=[shape] * 2,
        compiler_params=params(16),
        cost_estimate=QUICK,
        name="split_heads",
    )(place, owner, group, *candidates, *ties)


def pack_body(place_ref, mine_ref, got_ref, *outs):
    chip = place_ref[0]
    for k, out in enumerate(outs):
        out[0] = mine_ref[chip ^ k]
        out[1] = got_ref[chip ^ k]


def pack_blocks(mine, got, place):
    chips = mine.shape[0]
    shape = jax.ShapeDtypeStruct((2, *mine.shape[1:]), BF16)
    return pl.pallas_call(
        pack_body,
        in_specs=[SMEM, VMEM, VMEM],
        out_specs=[VMEM] * chips,
        out_shape=[shape] * chips,
        compiler_params=params(4),
        cost_estimate=QUICK,
        name="pack_blocks",
    )(place, mine, got)


def halves_body(place_ref, w_ref, _, own_ref, away_ref, token_ref, sems):
    token_ref[...] = jnp.zeros_like(token_ref)
    half = own_ref.shape[1]
    core = place_ref[1]
    copies = [
        pltpu.make_async_copy(w_ref.at[:, pl.ds(pl.multiple_of(side * half, 128), half)], out, sems.at[i])
        for i, (side, out) in enumerate(((core, own_ref), (1 - core, away_ref)))
    ]
    for c in copies:
        c.start()
    for c in copies:
        c.wait()


def halves(weights, place, after):
    rows, width = weights.shape
    shape = jax.ShapeDtypeStruct((rows, width // 2), BF16)
    return pl.pallas_call(
        halves_body,
        in_specs=[SMEM, HBM, ANY],
        out_specs=[VMEM] * 3,
        out_shape=[shape] * 2 + [TOKEN],
        scratch_shapes=[pltpu.SemaphoreType.DMA((2,))],
        compiler_params=params(2),
        cost_estimate=QUICK,
        name="halves",
    )(place, pltpu.with_memory_space_constraint(weights, pltpu.HBM), after)


def rows_body(count, shift, place_ref, *refs):
    core = place_ref[1]
    out = refs[-1]
    rows = out.shape[0]
    side = core if shift == 0 else 1 - core
    at = pl.multiple_of(side * rows, rows)
    width = refs[0].shape[1]
    for i in range(count):
        out[:, i * width : (i + 1) * width] = refs[i][pl.ds(at, rows), :]


def core_rows(chunks, place, shift):
    rows = chunks[0].shape[0] // 2
    width = sum(c.shape[1] for c in chunks)
    return pl.pallas_call(
        functools.partial(rows_body, len(chunks), shift),
        in_specs=[SMEM] + [VMEM] * len(chunks),
        out_specs=VMEM,
        out_shape=jax.ShapeDtypeStruct((rows, width), BF16),
        compiler_params=params(4),
        cost_estimate=QUICK,
        name="core_rows",
    )(place, *chunks)


def join_body(place_ref, near_ref, far_ref, out_ref):
    half = near_ref.shape[1]
    own = place_ref[1] == 0
    near, far = near_ref[...], far_ref[...]
    out_ref[:, :half] = jnp.where(own, near, far)
    out_ref[:, half:] = jnp.where(own, far, near)


def join(near, far, place):
    rows, half = near.shape
    return pl.pallas_call(
        join_body,
        in_specs=[SMEM, VMEM, VMEM],
        out_specs=VMEM,
        out_shape=jax.ShapeDtypeStruct((rows, 2 * half), BF16),
        compiler_params=params(4),
        cost_estimate=QUICK,
        name="join",
    )(place, near, far)


def project_part(pieces, part, w_ref, down_ref, rows_ref, acc_ref, lat_ref, acc, lat):
    at = 0
    for piece in pieces:
        rows_ref[at : at + piece.shape[0], :] = piece[...]
        at += piece.shape[0]
    width = rows_ref.shape[1]
    kb = width // 4
    for s in range(4):
        x = rows_ref[:, s * kb : (s + 1) * kb]
        k = part * width + s * kb
        more = lax.dot_general(w_ref[:, k : k + kb], x, NT, preferred_element_type=F32)
        extra = jnp.dot(x, down_ref[k : k + kb, :], preferred_element_type=F32)
        if s == 0 and acc is None:
            acc_ref[...] = more
            lat_ref[...] = extra
        elif s == 0:
            acc_ref[...] = acc[...] + more
            lat_ref[...] = lat[...] + extra
        else:
            acc_ref[...] += more
            lat_ref[...] += extra


def project_body(count, ties, *refs):
    pieces = refs[:count]
    w_ref, down_ref, acc_ref, lat_ref, rows_ref = refs[count : count + 2] + refs[count + 2 + ties :]
    project_part(pieces, 0, w_ref, down_ref, rows_ref, acc_ref, lat_ref, None, None)


def attend_body(count, blocks, dims, place_ref, len_ref, *refs):
    pieces = refs[:count]
    kv_refs = refs[count : count + blocks]
    w_ref, down_ref, up_ref, acc_in, lat_in, out_ref, rows_ref, acc_ref, lat_ref = refs[count + blocks :]
    rows, cols, chips, tok_dev = dims
    project_part(pieces, 1, w_ref, down_ref, rows_ref, acc_ref, lat_ref, acc_in, lat_in)

    chip, core = place_ref[0], place_ref[1]
    keys_t = acc_ref[cols : 2 * cols, :].astype(BF16)
    vals_t = acc_ref[2 * cols :, :].astype(BF16)
    cached_k = jnp.concatenate([kv[s, 0] for kv in kv_refs for s in range(2)], axis=0)
    cached_v = jnp.concatenate([kv[s, 1] for kv in kv_refs for s in range(2)], axis=0)
    up = up_ref[...]
    scale = HD ** (-0.5)
    pair = 2 * tok_dev

    def spots(row):
        slot = row // pair
        inside = row - slot * pair
        side = inside // tok_dev
        owner = chip - slot
        owner = jnp.where(owner < 0, owner + chips, owner)
        at = jnp.where(core == 0, side, 1 - side)
        return owner * pair + at * tok_dev + inside - side * tok_dev

    def requests(spot):
        end = len_ref[0, 0]
        found = (spot >= end).astype(jnp.int32)
        for j in range(1, len_ref.shape[1]):
            end = end + len_ref[0, j]
            found = found + (spot >= end).astype(jnp.int32)
        return found

    block = min(256, rows)
    key_spot = spots(lax.broadcasted_iota(jnp.int32, (rows, 1), 0))
    key_req = requests(key_spot)

    def one_block(b, carry):
        r0 = pl.multiple_of(b * block, block)
        lat = lat_ref[pl.ds(r0, block), :].astype(BF16)
        q = acc_ref[:cols, pl.ds(r0, block)] + lax.dot_general(up, lat, NT, preferred_element_type=F32)
        q = q.astype(BF16)
        q_spot = spots(r0 + lax.broadcasted_iota(jnp.int32, (1, block), 1))
        allowed = jnp.logical_and(requests(q_spot) == key_req, key_spot <= q_spot)
        pre = jnp.dot(cached_k, q, preferred_element_type=F32) * scale
        suf = lax.dot_general(keys_t, q, TN, preferred_element_type=F32) * scale
        suf = jnp.where(allowed, suf, -jnp.inf)
        top = jnp.maximum(jnp.max(pre, axis=0, keepdims=True), jnp.max(suf, axis=0, keepdims=True))
        pre = jnp.exp(pre - top)
        suf = jnp.exp(suf - top)
        total = jnp.sum(pre, axis=0, keepdims=True) + jnp.sum(suf, axis=0, keepdims=True)
        weighted = lax.dot_general(cached_v, pre.astype(BF16), TN, preferred_element_type=F32) + jnp.dot(
            vals_t, suf.astype(BF16), preferred_element_type=F32
        )
        heads = (weighted / total).T.astype(BF16)
        for k in range(block // tok_dev):
            base = r0 + (k // 2) * pair
            shift = (core if k % 2 == 0 else 1 - core) * tok_dev
            at = pl.multiple_of(base + shift, tok_dev)
            out_ref[pl.ds(at, tok_dev), :] = heads[k * tok_dev : (k + 1) * tok_dev]
        return carry

    if rows == block:
        one_block(0, 0)
    else:
        lax.fori_loop(0, rows // block, one_block, 0)


def project(pieces, w_t, down, ties):
    rows = sum(p.shape[0] for p in pieces)
    width = pieces[0].shape[1]
    cols3, rank = w_t.shape[0], down.shape[1]
    return pl.pallas_call(
        functools.partial(project_body, len(pieces), len(ties)),
        in_specs=[VMEM] * (len(pieces) + 2) + [ANY] * len(ties),
        out_specs=[VMEM] * 2,
        out_shape=[jax.ShapeDtypeStruct((cols3, rows), F32), jax.ShapeDtypeStruct((rows, rank), F32)],
        scratch_shapes=[pltpu.VMEM((rows, width), BF16)],
        compiler_params=params(6 + rows * width * 4 // 2**20),
        cost_estimate=QUICK,
        name="project",
    )(*pieces, w_t, down, *ties)


def attend(pieces, w_t, down, up_t, kv_blocks, acc, lat, place, lengths, chips):
    rows = sum(p.shape[0] for p in pieces)
    width = pieces[0].shape[1]
    cols3, rank = w_t.shape[0], down.shape[1]
    cols = cols3 // 3
    dims = (rows, cols, chips, pieces[0].shape[0])
    return pl.pallas_call(
        functools.partial(attend_body, len(pieces), len(kv_blocks), dims),
        in_specs=[SMEM, SMEM] + [VMEM] * (len(pieces) + len(kv_blocks) + 5),
        out_specs=VMEM,
        out_shape=jax.ShapeDtypeStruct((rows, cols), BF16),
        scratch_shapes=[
            pltpu.VMEM((rows, width), BF16),
            pltpu.VMEM((cols3, rows), F32),
            pltpu.VMEM((rows, rank), F32),
        ],
        compiler_params=params(10 + rows * width * 5 // 2**20),
        cost_estimate=QUICK,
        name="attend",
    )(place, lengths, *pieces, *kv_blocks, w_t, down, up_t, acc, lat)


def out_body(a_ref, b_ref, wa_ref, wb_ref, out_ref):
    out_ref[...] = jnp.dot(a_ref[...], wa_ref[...], preferred_element_type=F32) + jnp.dot(
        b_ref[...], wb_ref[...], preferred_element_type=F32
    )


def out_project(own, got, w_own, w_got):
    rows, width = own.shape[0], w_own.shape[1]
    return pl.pallas_call(
        out_body,
        in_specs=[VMEM] * 4,
        out_specs=VMEM,
        out_shape=jax.ShapeDtypeStruct((rows, width), F32),
        compiler_params=params(4 + rows * width * 8 // 2**20),
        cost_estimate=QUICK,
        name="out_project",
    )(own, got, w_own, w_got)


def add_body(row, col, got_ref, part_ref, *rest):
    rows, width = got_ref.shape
    out_ref = rest[-1]
    total = got_ref[...].astype(F32) + part_ref[row : row + rows, col : col + width]
    out_ref[...] = total.astype(BF16)


def add_slot(got, partial, row, col, ties=()):
    return pl.pallas_call(
        functools.partial(add_body, row, col),
        in_specs=[VMEM] * 2 + [ANY] * len(ties),
        out_specs=VMEM,
        out_shape=jax.ShapeDtypeStruct(got.shape, BF16),
        compiler_params=params(4),
        cost_estimate=QUICK,
        name="add_slot",
    )(got, partial, *ties)


def finish_body(count, place_ref, part_ref, *refs):
    gots = refs[:count]
    near_ref, far_ref = refs[-2:]
    core = place_ref[1]
    rows = near_ref.shape[0]
    width = gots[0].shape[1]
    for out, side in ((near_ref, core), (far_ref, 1 - core)):
        at = pl.multiple_of(side * rows, rows)
        for i, got in enumerate(gots):
            cols = slice(i * width, (i + 1) * width)
            total = got[pl.ds(at, rows), :].astype(F32) + part_ref[pl.ds(at, rows), cols]
            out[:, cols] = total.astype(BF16)


def finish(gots, partial, place):
    rows = gots[0].shape[0] // 2
    shape = jax.ShapeDtypeStruct((rows, partial.shape[1]), BF16)
    return pl.pallas_call(
        functools.partial(finish_body, len(gots)),
        in_specs=[SMEM] + [VMEM] * (1 + len(gots)),
        out_specs=[VMEM] * 2,
        out_shape=[shape] * 2,
        compiler_params=params(4),
        cost_estimate=QUICK,
        name="finish",
    )(place, partial, *gots)


def gate_body(count, dims, place_ref, gain_ref, *refs):
    slots, chunks, parts = dims
    pieces = refs[:count]
    weights = refs[count : count + parts]
    down_ref, out_ref, away_ref, x_ref = refs[count + parts :]
    core = place_ref[1]
    half = x_ref.shape[2]
    tile = tile_of(out_ref.shape[1])
    steps = out_ref.shape[1] // tile

    low, high = gain_ref[:half].reshape(1, half), gain_ref[half:].reshape(1, half)
    own_gain = jnp.where(core == 0, low, high)
    got_gain = jnp.where(core == 0, high, low)
    at = iter(pieces)
    row = 0
    for _k in range(slots):
        own = [next(at)[...].astype(F32) for _c in range(chunks)]
        got = [next(at)[...].astype(F32) for _c in range(chunks)]
        own = jnp.concatenate(own, axis=1)
        got = jnp.concatenate(got, axis=1)
        n = own.shape[0]
        square = jnp.sum(own * own, axis=-1, keepdims=True) + jnp.sum(got * got, axis=-1, keepdims=True)
        scale = lax.rsqrt(square * (0.5 / half) + EPS)
        x_ref[core, row : row + n, :] = (own * scale * own_gain).astype(BF16)
        x_ref[1 - core, row : row + n, :] = (got * scale * got_gain).astype(BF16)
        row += n

    per = half * 2 // parts
    for j in range(steps):
        gate = up = None
        for p in range(parts):
            side, at = divmod(p * per, half)
            x = x_ref[side, :, at : at + per]
            g = jnp.dot(x, weights[p][0, :, j * tile : (j + 1) * tile], preferred_element_type=F32)
            u = jnp.dot(x, weights[p][1, :, j * tile : (j + 1) * tile], preferred_element_type=F32)
            gate = g if gate is None else gate + g
            up = u if up is None else up + u
        out_ref[:, j * tile : (j + 1) * tile] = (gate / (1.0 + jnp.exp(-gate)) * up).astype(BF16)

    hidden = out_ref[...]
    wide = tile_of(half)
    for j in range(0, half, wide):
        away_ref[:, j : j + wide] = jnp.dot(hidden, down_ref[:, j : j + wide], preferred_element_type=F32).astype(BF16)


def gate_up(pieces, slots, chunks, weights, down, gain, place):
    half = gain.shape[0] // 2
    rows = slots * pieces[0].shape[0]
    parts = len(weights)
    units = weights[0].shape[2]
    return pl.pallas_call(
        functools.partial(gate_body, len(pieces), (slots, chunks, parts)),
        in_specs=[SMEM] + [VMEM] * (2 + len(pieces) + parts),
        out_specs=[VMEM] * 2,
        out_shape=[jax.ShapeDtypeStruct((rows, units), BF16), jax.ShapeDtypeStruct((rows, half), BF16)],
        scratch_shapes=[pltpu.VMEM((2, rows, half), BF16)],
        compiler_params=params(3 + rows * half * 18 // 2**20),
        cost_estimate=QUICK,
        name="gate_up",
    )(place, gain, *pieces, *weights, down)


def down_body(x_ref, w_ref, got_ref, out_ref):
    half = out_ref.shape[1]
    wide = tile_of(half)
    x = x_ref[...]
    for j in range(0, half, wide):
        out_ref[:, j : j + wide] = jnp.dot(x, w_ref[:, j : j + wide], preferred_element_type=F32)


def down_half(hidden, down):
    rows, units = hidden.shape
    half = down.shape[1]
    return pl.pallas_call(
        lambda x_ref, w_ref, out_ref: down_body(x_ref, w_ref, None, out_ref),
        in_specs=[VMEM] * 2,
        out_specs=VMEM,
        out_shape=jax.ShapeDtypeStruct((rows, half), F32),
        compiler_params=params(4 + rows * half * 4 // 2**20),
        cost_estimate=QUICK,
        name="down_half",
    )(hidden, down)


def make(mesh):
    n = mesh.shape["hid"]
    n_req = mesh.shape["req"]
    chips = n // 2
    both = [(h, h ^ 1) for h in range(n)]
    ring = [(h, (h + 2) % n) for h in range(n)]

    def swap(v):
        return lax.ppermute(v, "hid", both)

    def onward(v):
        return lax.ppermute(v, "hid", ring)

    def gather(own, fillers=()):
        slots = [list(own)]
        here = list(own)
        gave = []
        fillers = list(fillers)
        for k in range(1, chips):
            done = [fillers.pop(0)(here[-1])] if fillers else []
            here = [onward(v) for v in here]
            for what, token in done:
                here = [pass_on(v, token) for v in here]
                gave.append(what)
            slots.append(here)
        gave += [f(here[-1])[0] for f in fillers]
        return [(s, [swap(v) for v in s]) for s in slots], gave

    def scatter(partial, count, fillers=(), place=None):
        rows = partial.shape[0] // chips
        width = partial.shape[1] // count
        sums = [partial[rows : 2 * rows, i * width : (i + 1) * width].astype(BF16) for i in range(count)]
        gave = []
        fillers = list(fillers)
        for k in range(2, chips + 1):
            done = [fillers.pop(0)(sums[-1])] if fillers else []
            ties = [d[1] for d in done]
            gave += [d[0] for d in done]
            sums = [onward(v) for v in sums]
            if k == chips and place is not None:
                return finish(sums, partial, place), gave
            sums = [add_slot(v, partial, k % chips * rows, i * width, ties) for i, v in enumerate(sums)]
        gave += [f(sums[-1])[0] for f in fillers]
        return sums, gave

    def per_device(tokens, gain_in, w_qkv, adapt_down, adapt_up, w_out, gain_ff, w_gate_up, w_down,
                   prefix_cache, prefix_owner, group_prefix, lengths):
        tok_dev, width_in = tokens.shape
        cols = w_qkv.shape[2]
        model_width = w_out.shape[1]
        half = model_width // 2
        hid = lax.axis_index("hid")
        req = lax.axis_index("req")
        core = hid % 2
        chip = hid // 2
        place = jnp.stack([chip, core, req]).astype(jnp.int32)

        here = norm_rows(tokens, gain_in[None, :], 2)
        w_t = jnp.transpose(w_qkv, (1, 2, 0)).reshape(3 * cols, width_in)

        def hold_weights(v):
            *held, token = hold(w_t, adapt_down, place, v)
            return held, token

        def split_out(v):
            *sides, token = halves(w_out, place, v)
            return sides, token

        def cached(v):
            mine, other = split_heads(candidates, place, prefix_owner, group_prefix, chips, [v])
            blocks = pack_blocks(mine, swap(other), place)
            return blocks, blocks[0]

        cache = prefix_cache[0]
        candidates = [cache] + [
            lax.ppermute(cache, "req", [(r, r ^ k) for r in range(n_req)]) for k in range(1, n_req)
        ]
        slots, given = gather(here, [hold_weights, split_out, cached])
        (w_t, adapt_down), (w_own, w_away), kv_blocks = given
        kv_blocks = [
            lax.ppermute(block, "hid", [(h, h ^ (2 * k)) for h in range(n)]) if k else block
            for k, block in enumerate(kv_blocks)
        ]
        w_got = swap(w_away)

        pick = lambda i: [v for s in slots for v in (s[0][i], s[1][i])]
        acc, lat = project(pick(0), w_t, adapt_down, kv_blocks[1:])
        heads = attend(pick(1), w_t, adapt_down, adapt_up.T, kv_blocks, acc, lat, place, lengths, chips)
        partial = out_project(heads, swap(heads), w_own, w_got)

        parts = 4
        work = [lambda v, p=p: unpair(w_gate_up, p, parts, v) for p in range(parts)]
        work += [lambda v, flip=flip: bring(w_down, place, flip, v) for flip in (True, False)]
        sums, early = scatter(partial, 2, work[:3])
        summed, late = gather(sums, work[3:])
        *w_pairs, down_away, down_own = early + late

        def first_output(_):
            attn_own = join(core_rows(summed[0][0], place, 0), core_rows(summed[0][1], place, 0), place)
            return attn_own, attn_own

        pieces = [v for s in summed for v in s[0] + s[1]]
        hidden, away_half = gate_up(pieces, chips, 2, w_pairs, down_away, gain_ff, place)
        got_half = swap(away_half)
        own_half = down_half(hidden, down_own)
        ends, (attn_own,) = scatter(own_half + got_half.astype(F32), 2, [first_output], place)
        block_own = join(ends[0], swap(ends[1]), place)
        return attn_own, block_own

    return per_device


def solution(mesh):
    placed = (
        P(("req", "hid"), None),
        P(),
        P(None, None, "hid"),
        P(),
        P(None, "hid"),
        P("hid", None),
        P(),
        P(None, None, "hid"),
        P("hid", None),
        P("req", "hid", None, None),
        P(),
        P(),
        P("req", None),
    )
    return jax.shard_map(
        make(mesh),
        mesh=mesh,
        in_specs=placed,
        out_specs=(P(("req", "hid"), None), P(("req", "hid"), None)),
        check_vma=False,
    )
```

time: 217 us -> 150 us (0.69)
  Pallas kernels: 0 us -> 52.9 us
  starting transfers between devices: 74.3 us -> 31.3 us
  matrix products: 31.3 us -> 0 us
  local copies, waits for them, and re-layouts: 30.7 us -> 2.76 us
  other arithmetic: 20.2 us -> 0.4 us
  waiting for transfers between devices: 56 us -> 61.7 us
  between operations: 3.48 us -> 1.12 us
    pallas_call x0 -> x43, Pallas kernels: none -> 52.9 us  [the longest x4 12.9 us: unpair(): pl.pallas_call(functools.partial(unpair_body, part * rows), in_specs=[HBM...]
    ppermute x60 -> x48, starting transfers between devices: 69.8 us -> 25.3 us  [the longest x24 16.9 us: onward(): return lax.ppermute(v, 'hid', ring)]
    dot_general x8 -> x0, matrix products: 31.3 us -> none  [the longest x1 12.1 us: per_device(): jnp.dot(ff_in, w_gate_up.reshape(model_width, 2 * units), preferred_eleme...]
    unnamed x23 -> x18, local copies, waits for them, and re-layouts: 23.9 us -> 2.72 us
    unnamed x15 -> x0, other arithmetic: 9.63 us -> none
    ppermute x60 -> x48, waiting for transfers between devices: 50.4 us -> 56.7 us  [the longest x24 52.7 us: onward(): return lax.ppermute(v, 'hid', ring)]
    convert_element_type x6 -> x0, other arithmetic: 4.04 us -> none  [ring_scatter(): ahead = lax.ppermute(ahead.astype(BF16), 'hid', fwd).astype(F32)]
    dynamic_slice x9 -> x0, local copies, waits for them, and re-layouts: 3.02 us -> none  [the longest x2 1.24 us: per_device(): other = lax.dynamic_index_in_dim(cache, 1 - core, 3, keepdims=False)]
  transfers between devices with their start and end apart: 63 -> 51, of which waited for: 26 -> 29; matrix products, arithmetic and copies ran while one was open for 17% -> 0% of each run, Pallas kernels for 0% -> 26%
where the time goes in v3:
time: 150 us
  waiting for transfers between devices  61.7 us (41%)
  Pallas kernels  52.9 us (35%)
  starting transfers between devices  31.3 us (21%)
  local copies, waits for them, and re-layouts  2.76 us (2%)
    ppermute x24, waiting for transfers between devices, onward(): return lax.ppermute(v, 'hid', ring)  52.7 us
    ppermute x24, starting transfers between devices, onward(): return lax.ppermute(v, 'hid', ring)  16.9 us
    pallas_call x4, Pallas kernels, unpair(): pl.pallas_call(functools.partial(unpair_body, part * rows), in_specs=[HBM...  12.9 us
    pallas_call x1, Pallas kernels, gate_up(): pl.pallas_call(functools.partial(gate_body, len(pieces), (slots, chunks,...  11 us
    pallas_call x2, Pallas kernels, bring(): pl.pallas_call(functools.partial(bring_body, flip), in_specs=[SMEM, HBM,...  6.9 us
    ppermute x3, starting transfers between devices, per_device(): lax.ppermute(block, 'hid', [(h, h ^ 2 * k) for h in range(n)])  5.98 us
    ppermute x3, waiting for transfers between devices, per_device(): lax.ppermute(block, 'hid', [(h, h ^ 2 * k) for h in range(n)])  5.03 us
    pallas_call x1, Pallas kernels, hold(): pl.pallas_call(hold_body, in_specs=[SMEM, HBM, HBM, ANY], out_specs=[VMEM...  4.91 us
  transfers between devices with their start and end apart: 51, of which 29 were waited for; matrix products, arithmetic and copies ran while one was open for 0% of the time, Pallas kernels for 26%

profile of v3, /device:TPU:0, one launch (start us, length us, event | category | flops | bytes accessed | tf_op | source)
XLA Modules:
  0.0 150.1 jit_solution(17436836778007092315)
XLA Ops:
  0.6 1.0 copy-done.1
  2.7 3.1 %collective-permute-start.15 = (bf16[32,3584]{1,0:T(8,128)(2,1)S(1)}, bf16[32,3584]{1,0:T(8,128)(2,1)S(1)}, u32[]{:S(2)}, u32[]{:S(2)}) collective-permute-start(bf16[32,3584]{1,0:T(8,128)(2,1)S(1)} %get-tuple-element.45.refs_0_), channel_id=1, source_target_pairs={{0,2},{1,3},{2,4},{3,5},{4,6},{5,7},{6,0},{7,1},{8,10},{9,11},{10,... | collective-permute-start | bytes 688136 | tf_op jit(solution)/shard_map/ppermute | solution.py:590
  5.7 1.6 %collective-permute-start.1 = (bf16[32,3584]{1,0:T(8,128)(2,1)S(1)}, bf16[32,3584]{1,0:T(8,128)(2,1)S(1)}, u32[]{:S(2)}, u32[]{:S(2)}) collective-permute-start(bf16[32,3584]{1,0:T(8,128)(2,1)S(1)} %get-tuple-element.34._.refs_0_), channel_id=1, source_target_pairs={{0,2},{1,3},{2,4},{3,5},{4,6},{5,7},{6,0},{7,1},{8,10},{9,11},{10,... | collective-permute-start | bytes 688136 | tf_op jit(solution)/shard_map/ppermute | solution.py:590
  7.3 1.5 collective-permute-start.6
  8.8 1.5 %collective-permute-start.7 = (bf16[64,2,1792]{2,1,0:T(2,128)(2,1)}, bf16[64,2,1792]{2,1,0:T(2,128)(2,1)S(1)}, u32[]{:S(2)}, u32[]{:S(2)}) collective-permute-start(bf16[64,2,1792]{2,1,0:T(2,128)(2,1)} %bitcast.10), channel_id=1, source_target_pairs={{0,16},{8,24},{16,0},{24,8},{1,17},{9,25},{17,1},{25,9},{2,18},{10... | collective-permute-start | bytes 1376264 | tf_op jit(solution)/shard_map/ppermute | solution.py:654
  10.9 4.9 %hold.1 = (bf16[672,7168]{1,0:T(8,128)(2,1)S(1)}, bf16[7168,128]{1,0:T(8,128)(2,1)S(1)}, f32[8,128]{1,0:T(8,128)S(1)}) custom-call(s32[3]{0:T(128)S(1)} %pad_add_fusion.place_ref, bf16[672,7168]{1,0:T(8,128)(2,1)} %bitcast.15, bf16[7168,128]{1,0:T(8,128)(2,1)} %down_ref.1, bf16[32,3584]{1,0:T(8,128)(2,1)S(1)} %get-tuple-element.34._.refs_0_), custom_call_target="tpu_custom_call" | custom-call | flops 1 | bytes 1 | tf_op jit(solution)/shard_map/hold/pallas_call | solution.py:105
  15.8 1.6 %collective-permute-start.17 = (bf16[32,3584]{1,0:T(8,128)(2,1)S(1)}, bf16[32,3584]{1,0:T(8,128)(2,1)S(1)}, u32[]{:S(2)}, u32[]{:S(2)}) collective-permute-start(bf16[32,3584]{1,0:T(8,128)(2,1)S(1)} %pass_on.15.refs_2_), channel_id=1, source_target_pairs={{0,2},{1,3},{2,4},{3,5},{4,6},{5,7},{6,0},{7,1},{8,10},{9,11},{10,... | collective-permute-start | bytes 688136 | tf_op jit(solution)/shard_map/ppermute | solution.py:590
  18.3 1.9 %halves.1 = (bf16[224,1792]{1,0:T(8,128)(2,1)S(1)}, bf16[224,1792]{1,0:T(8,128)(2,1)S(1)}, f32[8,128]{1,0:T(8,128)S(1)}) custom-call(s32[3]{0:T(128)S(1)} %pad_add_fusion.place_ref, bf16[224,3584]{1,0:T(8,128)(2,1)} %w_ref.7, bf16[32,3584]{1,0:T(8,128)(2,1)S(1)} %pass_on.12._.refs_2_), custom_call_target="tpu_custom_call" | custom-call | flops 1 | bytes 1 | tf_op jit(solution)/shard_map/halves/pallas_call | solution.py:236
  20.2 5.2 %collective-permute-done.17._in = bf16[32,3584]{1,0:T(8,128)(2,1)S(1)} collective-permute-done((bf16[32,3584]{1,0:T(8,128)(2,1)S(1)}, bf16[32,3584]{1,0:T(8,128)(2,1)S(1)}, u32[]{:S(2)}, u32[]{:S(2)}) %collective-permute-start.17) | collective-permute-done | bytes 229408 | tf_op jit(solution)/shard_map/ppermute | solution.py:590
  26.0 4.4 %collective-permute-done.3._in = bf16[32,3584]{1,0:T(8,128)(2,1)S(1)} collective-permute-done((bf16[32,3584]{1,0:T(8,128)(2,1)S(1)}, bf16[32,3584]{1,0:T(8,128)(2,1)S(1)}, u32[]{:S(2)}, u32[]{:S(2)}) %collective-permute-start.3) | collective-permute-done | bytes 229408 | tf_op jit(solution)/shard_map/ppermute | solution.py:590
  30.4 1.2 split_heads.1
  33.5 1.2 collective-permute-start.5
  35.4 1.1 collective-permute-start.11
  36.5 2.3 %collective-permute-start.12 = (bf16[2,2,64,224]{3,2,1,0:T(8,128)(2,1)S(1)}, bf16[2,2,64,224]{3,2,1,0:T(8,128)(2,1)S(1)}, u32[]{:S(2)}, u32[]{:S(2)}) collective-permute-start(bf16[2,2,64,224]{3,2,1,0:T(8,128)(2,1)S(1)} %get-tuple-element.41), channel_id=1, source_target_pairs={{0,4},{1,5},{2,6},{3,7},{4,0},{5,1},{6,2},{7,3},{8,12},{9,13},{10,... | collective-permute-start | bytes 344072 | tf_op jit(solution)/shard_map/ppermute | solution.py:659
  38.8 5.0 %collective-permute-done.5._in = bf16[32,3584]{1,0:T(8,128)(2,1)S(1)} collective-permute-done((bf16[32,3584]{1,0:T(8,128)(2,1)S(1)}, bf16[32,3584]{1,0:T(8,128)(2,1)S(1)}, u32[]{:S(2)}, u32[]{:S(2)}) %collective-permute-start.5) | collective-permute-done | bytes 229408 | tf_op jit(solution)/shard_map/ppermute | solution.py:590
  43.9 2.5 %collective-permute-start.13 = (bf16[2,2,64,224]{3,2,1,0:T(8,128)(2,1)S(1)}, bf16[2,2,64,224]{3,2,1,0:T(8,128)(2,1)S(1)}, u32[]{:S(2)}, u32[]{:S(2)}) collective-permute-start(bf16[2,2,64,224]{3,2,1,0:T(8,128)(2,1)S(1)} %get-tuple-element.42), channel_id=1, source_target_pairs={{0,6},{1,7},{2,4},{3,5},{4,2},{5,3},{6,0},{7,1},{8,14},{9,15},{10,... | collective-permute-start | bytes 344072 | tf_op jit(solution)/shard_map/ppermute | solution.py:659
  46.4 2.7 %collective-permute-done.11.refs_10_.refs_9_ = bf16[2,2,64,224]{3,2,1,0:T(8,128)(2,1)S(1)} collective-permute-done((bf16[2,2,64,224]{3,2,1,0:T(8,128)(2,1)S(1)}, bf16[2,2,64,224]{3,2,1,0:T(8,128)(2,1)S(1)}, u32[]{:S(2)}, u32[]{:S(2)}) %collective-permute-start.11) | collective-permute-done | bytes 114720 | tf_op jit(solution)/shard_map/ppermute | solution.py:659
  49.7 2.3 %collective-permute-done.13.refs_12_.refs_11_ = bf16[2,2,64,224]{3,2,1,0:T(8,128)(2,1)S(1)} collective-permute-done((bf16[2,2,64,224]{3,2,1,0:T(8,128)(2,1)S(1)}, bf16[2,2,64,224]{3,2,1,0:T(8,128)(2,1)S(1)}, u32[]{:S(2)}, u32[]{:S(2)}) %collective-permute-start.13) | collective-permute-done | bytes 114720 | tf_op jit(solution)/shard_map/ppermute | solution.py:659
  52.5 2.1 %project.1 = (f32[672,256]{1,0:T(8,128)S(1)}, f32[256,128]{1,0:T(8,128)S(1)}) custom-call(bf16[32,3584]{1,0:T(8,128)(2,1)S(1)} %get-tuple-element.45.refs_0_, bf16[32,3584]{1,0:T(8,128)(2,1)S(1)} %collective-permute-done.14.refs_1_, bf16[32,3584]{1,0:T(8,128)(2,1)S(1)} %pass_on.15.refs_2_, bf16[32,3584]{1,0:T(8,128)(2,1)S(1)} %collective-permute-done.16.refs_3_, ...), custom_call_target="tpu_custom_call" | custom-call | flops 1 | bytes 1 | tf_op jit(solution)/shard_map/project/pallas_call | solution.py:395
  54.7 4.0 %attend.1.a_ref = bf16[256,224]{1,0:T(8,128)(2,1)S(1)} custom-call(s32[3]{0:T(128)S(1)} %pad_add_fusion.place_ref, s32[1,6]{1,0:T(1,128)S(1)} %copy-done.6, bf16[32,3584]{1,0:T(8,128)(2,1)S(1)} %get-tuple-element.34._.refs_0_, bf16[32,3584]{1,0:T(8,128)(2,1)S(1)} %collective-permute-done.refs_1_, bf16[32,3584]{1,0:T(8,128)(2,1)S(1)} %pass_on.12._.refs_2_, ...), custom_call_target="tpu_custom_call" | custom-call | flops 1 | bytes 1 | tf_op jit(solution)/shard_map/attend/pallas_call | solution.py:413
  58.8 1.3 collective-permute-done.21.b_ref
  60.9 3.3 %collective-permute-start.25 = (bf16[64,896]{1,0:T(8,128)(2,1)S(1)}, bf16[64,896]{1,0:T(8,128)(2,1)S(1)}, u32[]{:S(2)}, u32[]{:S(2)}) collective-permute-start(bf16[64,896]{1,0:T(8,128)(2,1)S(1)} %get-tuple-element.70._), channel_id=1, source_target_pairs={{0,2},{1,3},{2,4},{3,5},{4,6},{5,7},{6,0},{7,1},{8,10},{9,11},{10,... | collective-permute-start | bytes 344072 | tf_op jit(solution)/shard_map/ppermute | solution.py:590
  64.2 3.2 %unpair.4 = (bf16[2,896,1792]{2,1,0:T(8,128)(2,1)S(1)}, f32[8,128]{1,0:T(8,128)S(1)}) custom-call(bf16[3584,2,1792]{2,1,0:T(2,128)(2,1)} %w_ref.11, bf16[64,896]{1,0:T(8,128)(2,1)S(1)} %get-tuple-element.70._), custom_call_target="tpu_custom_call" | custom-call | flops 1 | bytes 1 | tf_op jit(solution)/shard_map/unpair/pallas_call | solution.py:78
  68.0 2.3 %collective-permute-start.27 = (bf16[64,896]{1,0:T(8,128)(2,1)S(1)}, bf16[64,896]{1,0:T(8,128)(2,1)S(1)}, u32[]{:S(2)}, u32[]{:S(2)}) collective-permute-start(bf16[64,896]{1,0:T(8,128)(2,1)S(1)} %add_slot.11._), channel_id=1, source_target_pairs={{0,2},{1,3},{2,4},{3,5},{4,6},{5,7},{6,0},{7,1},{8,10},{9,11},{10,... | collective-permute-start | bytes 344072 | tf_op jit(solution)/shard_map/ppermute | solution.py:590
  70.9 1.4 collective-permute-start.24
  72.3 3.2 %unpair.5 = (bf16[2,896,1792]{2,1,0:T(8,128)(2,1)S(1)}, f32[8,128]{1,0:T(8,128)S(1)}) custom-call(bf16[3584,2,1792]{2,1,0:T(2,128)(2,1)} %w_ref.11, bf16[64,896]{1,0:T(8,128)(2,1)S(1)} %add_slot.11._), custom_call_target="tpu_custom_call" | custom-call | flops 1 | bytes 1 | tf_op jit(solution)/shard_map/unpair/pallas_call | solution.py:78
  76.3 1.2 collective-permute-done.24.got_ref
  77.8 3.2 %unpair.6 = (bf16[2,896,1792]{2,1,0:T(8,128)(2,1)S(1)}, f32[8,128]{1,0:T(8,128)S(1)}) custom-call(bf16[3584,2,1792]{2,1,0:T(2,128)(2,1)} %w_ref.11, bf16[64,896]{1,0:T(8,128)(2,1)S(1)} %add_slot.13._), custom_call_target="tpu_custom_call" | custom-call | flops 1 | bytes 1 | tf_op jit(solution)/shard_map/unpair/pallas_call | solution.py:78
  81.1 1.7 %collective-permute-done.28.got_ref = bf16[64,896]{1,0:T(8,128)(2,1)S(1)} collective-permute-done((bf16[64,896]{1,0:T(8,128)(2,1)S(1)}, bf16[64,896]{1,0:T(8,128)(2,1)S(1)}, u32[]{:S(2)}, u32[]{:S(2)}) %collective-permute-start.28) | collective-permute-done | bytes 114720 | tf_op jit(solution)/shard_map/ppermute | solution.py:590
  82.9 1.7 %collective-permute-done.26.got_ref = bf16[64,896]{1,0:T(8,128)(2,1)S(1)} collective-permute-done((bf16[64,896]{1,0:T(8,128)(2,1)S(1)}, bf16[64,896]{1,0:T(8,128)(2,1)S(1)}, u32[]{:S(2)}, u32[]{:S(2)}) %collective-permute-start.26) | collective-permute-done | bytes 114720 | tf_op jit(solution)/shard_map/ppermute | solution.py:590
  84.7 3.2 %unpair.7 = (bf16[2,896,1792]{2,1,0:T(8,128)(2,1)S(1)}, f32[8,128]{1,0:T(8,128)S(1)}) custom-call(bf16[3584,2,1792]{2,1,0:T(2,128)(2,1)} %w_ref.11, bf16[64,896]{1,0:T(8,128)(2,1)S(1)} %add_slot.15.refs_1_._), custom_call_target="tpu_custom_call" | custom-call | flops 1 | bytes 1 | tf_op jit(solution)/shard_map/unpair/pallas_call | solution.py:78
  87.9 1.5 collective-permute-done.32._in
  89.5 3.0 %collective-permute-done.31._in = bf16[64,896]{1,0:T(8,128)(2,1)S(1)} collective-permute-done((bf16[64,896]{1,0:T(8,128)(2,1)S(1)}, bf16[64,896]{1,0:T(8,128)(2,1)S(1)}, u32[]{:S(2)}, u32[]{:S(2)}) %collective-permute-start.31) | collective-permute-done | bytes 114720 | tf_op jit(solution)/shard_map/ppermute | solution.py:590
  92.5 3.5 %bring.2 = (bf16[1792,1792]{1,0:T(8,128)(2,1)S(1)}, f32[8,128]{1,0:T(8,128)S(1)}) custom-call(s32[3]{0:T(128)S(1)} %pad_add_fusion.place_ref, bf16[1792,3584]{1,0:T(8,128)(2,1)} %w_ref.13, bf16[64,896]{1,0:T(8,128)(2,1)S(1)} %pass_on.19._.refs_5_), custom_call_target="tpu_custom_call" | custom-call | flops 1 | bytes 1 | tf_op jit(solution)/shard_map/bring/pallas_call | solution.py:137
  96.5 3.8 %collective-permute-done.35._in = bf16[64,896]{1,0:T(8,128)(2,1)S(1)} collective-permute-done((bf16[64,896]{1,0:T(8,128)(2,1)S(1)}, bf16[64,896]{1,0:T(8,128)(2,1)S(1)}, u32[]{:S(2)}, u32[]{:S(2)}) %collective-permute-start.35) | collective-permute-done | bytes 114720 | tf_op jit(solution)/shard_map/ppermute | solution.py:590
  100.9 3.5 %bring.3 = (bf16[1792,1792]{1,0:T(8,128)(2,1)S(1)}, f32[8,128]{1,0:T(8,128)S(1)}) custom-call(s32[3]{0:T(128)S(1)} %pad_add_fusion.place_ref, bf16[1792,3584]{1,0:T(8,128)(2,1)} %w_ref.13, bf16[64,896]{1,0:T(8,128)(2,1)S(1)} %pass_on.21._.refs_9_), custom_call_target="tpu_custom_call" | custom-call | flops 1 | bytes 1 | tf_op jit(solution)/shard_map/bring/pallas_call | solution.py:137
  104.9 2.0 %collective-permute-done.39._in = bf16[64,896]{1,0:T(8,128)(2,1)S(1)} collective-permute-done((bf16[64,896]{1,0:T(8,128)(2,1)S(1)}, bf16[64,896]{1,0:T(8,128)(2,1)S(1)}, u32[]{:S(2)}, u32[]{:S(2)}) %collective-permute-start.39) | collective-permute-done | bytes 114720 | tf_op jit(solution)/shard_map/ppermute | solution.py:590
  108.9 11.0 %gate_up.1 = (bf16[256,1792]{1,0:T(8,128)(2,1)S(1)}, bf16[256,1792]{1,0:T(8,128)(2,1)S(1)}) custom-call(s32[3]{0:T(128)S(1)} %pad_add_fusion.place_ref, f32[3584]{0:T(1024)S(1)} %copy-done.5, bf16[64,896]{1,0:T(8,128)(2,1)S(1)} %add_slot.14.refs_0_, bf16[64,896]{1,0:T(8,128)(2,1)S(1)} %add_slot.15.refs_1_._, ...), custom_call_target="tpu_custom_call" | custom-call | flops 1 | bytes 1 | tf_op jit(solution)/shard_map/gate_up/pallas_call | solution.py:545
  120.4 1.8 %down_half.1 = f32[256,1792]{1,0:T(8,128)S(1)} custom-call(bf16[256,1792]{1,0:T(8,128)(2,1)S(1)} %get-tuple-element.61.x_ref, bf16[1792,1792]{1,0:T(8,128)(2,1)S(1)} %get-tuple-element.62.w_ref), custom_call_target="tpu_custom_call" | custom-call | flops 1 | bytes 1 | tf_op jit(solution)/shard_map/down_half/pallas_call | solution.py:568
  124.0 1.3 join.2.rest_0_
  125.3 5.3 %collective-permute-done.47.got_ref = bf16[64,896]{1,0:T(8,128)(2,1)S(1)} collective-permute-done((bf16[64,896]{1,0:T(8,128)(2,1)S(1)}, bf16[64,896]{1,0:T(8,128)(2,1)S(1)}, u32[]{:S(2)}, u32[]{:S(2)}) %collective-permute-start.47) | collective-permute-done | bytes 114720 | tf_op jit(solution)/shard_map/ppermute | solution.py:590
  130.6 0.9 copy-done
  132.5 6.4 %collective-permute-done.48.got_ref = bf16[64,896]{1,0:T(8,128)(2,1)S(1)} collective-permute-done((bf16[64,896]{1,0:T(8,128)(2,1)S(1)}, bf16[64,896]{1,0:T(8,128)(2,1)S(1)}, u32[]{:S(2)}, u32[]{:S(2)}) %collective-permute-start.48) | collective-permute-done | bytes 114720 | tf_op jit(solution)/shard_map/ppermute | solution.py:590
  139.0 1.1 collective-permute-done.45.got_ref
  140.3 5.3 %collective-permute-done.49.refs_1_ = bf16[64,896]{1,0:T(8,128)(2,1)S(1)} collective-permute-done((bf16[64,896]{1,0:T(8,128)(2,1)S(1)}, bf16[64,896]{1,0:T(8,128)(2,1)S(1)}, u32[]{:S(2)}, u32[]{:S(2)}) %collective-permute-start.49) | collective-permute-done | bytes 114720 | tf_op jit(solution)/shard_map/ppermute | solution.py:590
  145.6 1.2 collective-permute-done.46.refs_0_
  147.5 1.3 collective-permute-done.50.far_ref
  148.8 1.2 join.3
  (120 shorter events, 17.5 us)
Async XLA Ops:
  2.7 13.1 %collective-permute-start.15 = (bf16[32,3584]{1,0:T(8,128)(2,1)S(1)}, bf16[32,3584]{1,0:T(8,128)(2,1)S(1)}, u32[]{:S(2)}, u32[]{:S(2)}) collective-permute-start(bf16[32,3584]{1,0:T(8,128)(2,1)S(1)} %get-tuple-element.45.refs_0_), channel_id=1, source_target_pairs={{0,2},{1,3},{2,4},{3,5},{4,6},{5,7},{6,0},{7,1},{8,10},{9,11},{10,... | collective-permute-start | bytes 688136 | tf_op jit(solution)/shard_map/ppermute | solution.py:590
  5.7 12.5 %collective-permute-start.1 = (bf16[32,3584]{1,0:T(8,128)(2,1)S(1)}, bf16[32,3584]{1,0:T(8,128)(2,1)S(1)}, u32[]{:S(2)}, u32[]{:S(2)}) collective-permute-start(bf16[32,3584]{1,0:T(8,128)(2,1)S(1)} %get-tuple-element.34._.refs_0_), channel_id=1, source_target_pairs={{0,2},{1,3},{2,4},{3,5},{4,6},{5,7},{6,0},{7,1},{8,10},{9,11},{10,... | collective-permute-start | bytes 688136 | tf_op jit(solution)/shard_map/ppermute | solution.py:590
  7.3 23.1 %collective-permute-start.6 = (bf16[64,2,1792]{2,1,0:T(2,128)(2,1)}, bf16[64,2,1792]{2,1,0:T(2,128)(2,1)S(1)}, u32[]{:S(2)}, u32[]{:S(2)}) collective-permute-start(bf16[64,2,1792]{2,1,0:T(2,128)(2,1)} %bitcast.9), channel_id=1, source_target_pairs={{0,8},{8,0},{16,24},{24,16},{1,9},{9,1},{17,25},{25,17},{2,10},{10... | collective-permute-start | bytes 1376264 | tf_op jit(solution)/shard_map/ppermute | solution.py:654
  8.8 21.6 %collective-permute-start.7 = (bf16[64,2,1792]{2,1,0:T(2,128)(2,1)}, bf16[64,2,1792]{2,1,0:T(2,128)(2,1)S(1)}, u32[]{:S(2)}, u32[]{:S(2)}) collective-permute-start(bf16[64,2,1792]{2,1,0:T(2,128)(2,1)} %bitcast.10), channel_id=1, source_target_pairs={{0,16},{8,24},{16,0},{24,8},{1,17},{9,25},{17,1},{25,9},{2,18},{10... | collective-permute-start | bytes 1376264 | tf_op jit(solution)/shard_map/ppermute | solution.py:654
  10.3 20.1 %collective-permute-start.8 = (bf16[64,2,1792]{2,1,0:T(2,128)(2,1)}, bf16[64,2,1792]{2,1,0:T(2,128)(2,1)S(1)}, u32[]{:S(2)}, u32[]{:S(2)}) collective-permute-start(bf16[64,2,1792]{2,1,0:T(2,128)(2,1)} %bitcast.11), channel_id=1, source_target_pairs={{0,24},{8,16},{16,8},{24,0},{1,25},{9,17},{17,9},{25,1},{2,26},{10... | collective-permute-start | bytes 1376264 | tf_op jit(solution)/shard_map/ppermute | solution.py:654
  15.8 9.7 %collective-permute-start.17 = (bf16[32,3584]{1,0:T(8,128)(2,1)S(1)}, bf16[32,3584]{1,0:T(8,128)(2,1)S(1)}, u32[]{:S(2)}, u32[]{:S(2)}) collective-permute-start(bf16[32,3584]{1,0:T(8,128)(2,1)S(1)} %pass_on.15.refs_2_), channel_id=1, source_target_pairs={{0,2},{1,3},{2,4},{3,5},{4,6},{5,7},{6,0},{7,1},{8,10},{9,11},{10,... | collective-permute-start | bytes 688136 | tf_op jit(solution)/shard_map/ppermute | solution.py:590
  18.3 12.1 %collective-permute-start.3 = (bf16[32,3584]{1,0:T(8,128)(2,1)S(1)}, bf16[32,3584]{1,0:T(8,128)(2,1)S(1)}, u32[]{:S(2)}, u32[]{:S(2)}) collective-permute-start(bf16[32,3584]{1,0:T(8,128)(2,1)S(1)} %pass_on.12._.refs_2_), channel_id=1, source_target_pairs={{0,2},{1,3},{2,4},{3,5},{4,6},{5,7},{6,0},{7,1},{8,10},{9,11},{10,... | collective-permute-start | bytes 688136 | tf_op jit(solution)/shard_map/ppermute | solution.py:590
  25.5 8.0 %collective-permute-start.19 = (bf16[32,3584]{1,0:T(8,128)(2,1)S(1)}, bf16[32,3584]{1,0:T(8,128)(2,1)S(1)}, u32[]{:S(2)}, u32[]{:S(2)}) collective-permute-start(bf16[32,3584]{1,0:T(8,128)(2,1)S(1)} %pass_on.16.refs_4_), channel_id=1, source_target_pairs={{0,2},{1,3},{2,4},{3,5},{4,6},{5,7},{6,0},{7,1},{8,10},{9,11},{10,... | collective-permute-start | bytes 688136 | tf_op jit(solution)/shard_map/ppermute | solution.py:590
  31.7 1.9 %collective-permute-start.9 = (bf16[4,2,64,224]{3,2,1,0:T(8,128)(2,1)S(1)}, bf16[4,2,64,224]{3,2,1,0:T(8,128)(2,1)S(1)}, u32[]{:S(2)}, u32[]{:S(2)}) collective-permute-start(bf16[4,2,64,224]{3,2,1,0:T(8,128)(2,1)S(1)} %get-tuple-element.38), channel_id=1, source_target_pairs={{0,1},{1,0},{2,3},{3,2},{4,5},{5,4},{6,7},{7,6},{8,9},{9,8},{10,11... | collective-permute-start | bytes 688136 | tf_op jit(solution)/shard_map/ppermute | solution.py:587
  31.8 3.5 %collective-permute-start.14 = (bf16[32,3584]{1,0:T(8,128)(2,1)S(1)}, bf16[32,3584]{1,0:T(8,128)(2,1)S(1)}, u32[]{:S(2)}, u32[]{:S(2)}) collective-permute-start(bf16[32,3584]{1,0:T(8,128)(2,1)S(1)} %get-tuple-element.45.refs_0_), channel_id=1, source_target_pairs={{0,1},{1,0},{2,3},{3,2},{4,5},{5,4},{6,7},{7,6},{8,9},{9,8},{10,11... | collective-permute-start | bytes 688136 | tf_op jit(solution)/shard_map/ppermute | solution.py:587
  32.2 26.5 %collective-permute-start.22 = (bf16[224,1792]{1,0:T(8,128)(2,1)S(1)}, bf16[224,1792]{1,0:T(8,128)(2,1)S(1)}, u32[]{:S(2)}, u32[]{:S(2)}) collective-permute-start(bf16[224,1792]{1,0:T(8,128)(2,1)S(1)} %get-tuple-element.49), channel_id=1, source_target_pairs={{0,1},{1,0},{2,3},{3,2},{4,5},{5,4},{6,7},{7,6},{8,9},{9,8},{10,11... | collective-permute-start | bytes 2408456 | tf_op jit(solution)/shard_map/ppermute | solution.py:587
  32.3 3.1 %collective-permute-start.16 = (bf16[32,3584]{1,0:T(8,128)(2,1)S(1)}, bf16[32,3584]{1,0:T(8,128)(2,1)S(1)}, u32[]{:S(2)}, u32[]{:S(2)}) collective-permute-start(bf16[32,3584]{1,0:T(8,128)(2,1)S(1)} %pass_on.15.refs_2_), channel_id=1, source_target_pairs={{0,1},{1,0},{2,3},{3,2},{4,5},{5,4},{6,7},{7,6},{8,9},{9,8},{10,11... | collective-permute-start | bytes 688136 | tf_op jit(solution)/shard_map/ppermute | solution.py:587
  33.5 3.0 %collective-permute-start.18 = (bf16[32,3584]{1,0:T(8,128)(2,1)S(1)}, bf16[32,3584]{1,0:T(8,128)(2,1)S(1)}, u32[]{:S(2)}, u32[]{:S(2)}) collective-permute-start(bf16[32,3584]{1,0:T(8,128)(2,1)S(1)} %pass_on.16.refs_4_), channel_id=1, source_target_pairs={{0,1},{1,0},{2,3},{3,2},{4,5},{5,4},{6,7},{7,6},{8,9},{9,8},{10,11... | collective-permute-start | bytes 688136 | tf_op jit(solution)/shard_map/ppermute | solution.py:587
  33.5 10.3 %collective-permute-start.5 = (bf16[32,3584]{1,0:T(8,128)(2,1)S(1)}, bf16[32,3584]{1,0:T(8,128)(2,1)S(1)}, u32[]{:S(2)}, u32[]{:S(2)}) collective-permute-start(bf16[32,3584]{1,0:T(8,128)(2,1)S(1)} %pass_on.13.refs_4_), channel_id=1, source_target_pairs={{0,2},{1,3},{2,4},{3,5},{4,6},{5,7},{6,0},{7,1},{8,10},{9,11},{10,... | collective-permute-start | bytes 688136 | tf_op jit(solution)/shard_map/ppermute | solution.py:590
  35.3 16.7 %collective-permute-start.20 = (bf16[32,3584]{1,0:T(8,128)(2,1)S(1)}, bf16[32,3584]{1,0:T(8,128)(2,1)S(1)}, u32[]{:S(2)}, u32[]{:S(2)}) collective-permute-start(bf16[32,3584]{1,0:T(8,128)(2,1)S(1)} %pass_on.17.refs_6_), channel_id=1, source_target_pairs={{0,1},{1,0},{2,3},{3,2},{4,5},{5,4},{6,7},{7,6},{8,9},{9,8},{10,11... | collective-permute-start | bytes 688136 | tf_op jit(solution)/shard_map/ppermute | solution.py:587
  35.4 13.8 %collective-permute-start.11 = (bf16[2,2,64,224]{3,2,1,0:T(8,128)(2,1)S(1)}, bf16[2,2,64,224]{3,2,1,0:T(8,128)(2,1)S(1)}, u32[]{:S(2)}, u32[]{:S(2)}) collective-permute-start(bf16[2,2,64,224]{3,2,1,0:T(8,128)(2,1)S(1)} %get-tuple-element.40), channel_id=1, source_target_pairs={{0,2},{1,3},{2,0},{3,1},{4,6},{5,7},{6,4},{7,5},{8,10},{9,11},{10,... | collective-permute-start | bytes 344072 | tf_op jit(solution)/shard_map/ppermute | solution.py:659
  36.5 12.7 %collective-permute-start.12 = (bf16[2,2,64,224]{3,2,1,0:T(8,128)(2,1)S(1)}, bf16[2,2,64,224]{3,2,1,0:T(8,128)(2,1)S(1)}, u32[]{:S(2)}, u32[]{:S(2)}) collective-permute-start(bf16[2,2,64,224]{3,2,1,0:T(8,128)(2,1)S(1)} %get-tuple-element.41), channel_id=1, source_target_pairs={{0,4},{1,5},{2,6},{3,7},{4,0},{5,1},{6,2},{7,3},{8,12},{9,13},{10,... | collective-permute-start | bytes 344072 | tf_op jit(solution)/shard_map/ppermute | solution.py:659
  43.9 8.1 %collective-permute-start.13 = (bf16[2,2,64,224]{3,2,1,0:T(8,128)(2,1)S(1)}, bf16[2,2,64,224]{3,2,1,0:T(8,128)(2,1)S(1)}, u32[]{:S(2)}, u32[]{:S(2)}) collective-permute-start(bf16[2,2,64,224]{3,2,1,0:T(8,128)(2,1)S(1)} %get-tuple-element.42), channel_id=1, source_target_pairs={{0,6},{1,7},{2,4},{3,5},{4,2},{5,3},{6,0},{7,1},{8,14},{9,15},{10,... | collective-permute-start | bytes 344072 | tf_op jit(solution)/shard_map/ppermute | solution.py:659
  49.2 5.5 %collective-permute-start = (bf16[32,3584]{1,0:T(8,128)(2,1)S(1)}, bf16[32,3584]{1,0:T(8,128)(2,1)S(1)}, u32[]{:S(2)}, u32[]{:S(2)}) collective-permute-start(bf16[32,3584]{1,0:T(8,128)(2,1)S(1)} %get-tuple-element.34._.refs_0_), channel_id=1, source_target_pairs={{0,1},{1,0},{2,3},{3,2},{4,5},{5,4},{6,7},{7,6},{8,9},{9,8},{10,11... | collective-permute-start | bytes 688136 | tf_op jit(solution)/shard_map/ppermute | solution.py:587
  49.2 5.5 %collective-permute-start.2 = (bf16[32,3584]{1,0:T(8,128)(2,1)S(1)}, bf16[32,3584]{1,0:T(8,128)(2,1)S(1)}, u32[]{:S(2)}, u32[]{:S(2)}) collective-permute-start(bf16[32,3584]{1,0:T(8,128)(2,1)S(1)} %pass_on.12._.refs_2_), channel_id=1, source_target_pairs={{0,1},{1,0},{2,3},{3,2},{4,5},{5,4},{6,7},{7,6},{8,9},{9,8},{10,11... | collective-permute-start | bytes 688136 | tf_op jit(solution)/shard_map/ppermute | solution.py:587
  52.0 2.7 %collective-permute-start.4 = (bf16[32,3584]{1,0:T(8,128)(2,1)S(1)}, bf16[32,3584]{1,0:T(8,128)(2,1)S(1)}, u32[]{:S(2)}, u32[]{:S(2)}) collective-permute-start(bf16[32,3584]{1,0:T(8,128)(2,1)S(1)} %pass_on.13.refs_4_), channel_id=1, source_target_pairs={{0,1},{1,0},{2,3},{3,2},{4,5},{5,4},{6,7},{7,6},{8,9},{9,8},{10,11... | collective-permute-start | bytes 688136 | tf_op jit(solution)/shard_map/ppermute | solution.py:587
  52.0 2.7 %collective-permute-start.10 = (bf16[32,3584]{1,0:T(8,128)(2,1)S(1)}, bf16[32,3584]{1,0:T(8,128)(2,1)S(1)}, u32[]{:S(2)}, u32[]{:S(2)}) collective-permute-start(bf16[32,3584]{1,0:T(8,128)(2,1)S(1)} %pass_on.14.refs_6_), channel_id=1, source_target_pairs={{0,1},{1,0},{2,3},{3,2},{4,5},{5,4},{6,7},{7,6},{8,9},{9,8},{10,11... | collective-permute-start | bytes 688136 | tf_op jit(solution)/shard_map/ppermute | solution.py:587
  58.7 1.4 collective-permute-start.21
  60.9 7.0 %collective-permute-start.25 = (bf16[64,896]{1,0:T(8,128)(2,1)S(1)}, bf16[64,896]{1,0:T(8,128)(2,1)S(1)}, u32[]{:S(2)}, u32[]{:S(2)}) collective-permute-start(bf16[64,896]{1,0:T(8,128)(2,1)S(1)} %get-tuple-element.70._), channel_id=1, source_target_pairs={{0,2},{1,3},{2,4},{3,5},{4,6},{5,7},{6,0},{7,1},{8,10},{9,11},{10,... | collective-permute-start | bytes 344072 | tf_op jit(solution)/shard_map/ppermute | solution.py:590
  64.1 6.7 %collective-permute-start.23 = (bf16[64,896]{1,0:T(8,128)(2,1)S(1)}, bf16[64,896]{1,0:T(8,128)(2,1)S(1)}, u32[]{:S(2)}, u32[]{:S(2)}) collective-permute-start(bf16[64,896]{1,0:T(8,128)(2,1)S(1)} %get-tuple-element.71), channel_id=1, source_target_pairs={{0,2},{1,3},{2,4},{3,5},{4,6},{5,7},{6,0},{7,1},{8,10},{9,11},{10,... | collective-permute-start | bytes 344072 | tf_op jit(solution)/shard_map/ppermute | solution.py:590
  68.0 7.6 %collective-permute-start.27 = (bf16[64,896]{1,0:T(8,128)(2,1)S(1)}, bf16[64,896]{1,0:T(8,128)(2,1)S(1)}, u32[]{:S(2)}, u32[]{:S(2)}) collective-permute-start(bf16[64,896]{1,0:T(8,128)(2,1)S(1)} %add_slot.11._), channel_id=1, source_target_pairs={{0,2},{1,3},{2,4},{3,5},{4,6},{5,7},{6,0},{7,1},{8,10},{9,11},{10,... | collective-permute-start | bytes 344072 | tf_op jit(solution)/shard_map/ppermute | solution.py:590
  70.9 6.6 %collective-permute-start.24 = (bf16[64,896]{1,0:T(8,128)(2,1)S(1)}, bf16[64,896]{1,0:T(8,128)(2,1)S(1)}, u32[]{:S(2)}, u32[]{:S(2)}) collective-permute-start(bf16[64,896]{1,0:T(8,128)(2,1)S(1)} %add_slot.10), channel_id=1, source_target_pairs={{0,2},{1,3},{2,4},{3,5},{4,6},{5,7},{6,0},{7,1},{8,10},{9,11},{10,... | collective-permute-start | bytes 344072 | tf_op jit(solution)/shard_map/ppermute | solution.py:590
  75.6 7.2 %collective-permute-start.28 = (bf16[64,896]{1,0:T(8,128)(2,1)S(1)}, bf16[64,896]{1,0:T(8,128)(2,1)S(1)}, u32[]{:S(2)}, u32[]{:S(2)}) collective-permute-start(bf16[64,896]{1,0:T(8,128)(2,1)S(1)} %add_slot.13._), channel_id=1, source_target_pairs={{0,2},{1,3},{2,4},{3,5},{4,6},{5,7},{6,0},{7,1},{8,10},{9,11},{10,... | collective-permute-start | bytes 344072 | tf_op jit(solution)/shard_map/ppermute | solution.py:590
  77.6 7.0 %collective-permute-start.26 = (bf16[64,896]{1,0:T(8,128)(2,1)S(1)}, bf16[64,896]{1,0:T(8,128)(2,1)S(1)}, u32[]{:S(2)}, u32[]{:S(2)}) collective-permute-start(bf16[64,896]{1,0:T(8,128)(2,1)S(1)} %add_slot.12), channel_id=1, source_target_pairs={{0,2},{1,3},{2,4},{3,5},{4,6},{5,7},{6,0},{7,1},{8,10},{9,11},{10,... | collective-permute-start | bytes 344072 | tf_op jit(solution)/shard_map/ppermute | solution.py:590
  82.8 6.6 %collective-permute-start.32 = (bf16[64,896]{1,0:T(8,128)(2,1)S(1)}, bf16[64,896]{1,0:T(8,128)(2,1)S(1)}, u32[]{:S(2)}, u32[]{:S(2)}) collective-permute-start(bf16[64,896]{1,0:T(8,128)(2,1)S(1)} %add_slot.15.refs_1_._), channel_id=1, source_target_pairs={{0,2},{1,3},{2,4},{3,5},{4,6},{5,7},{6,0},{7,1},{8,10},{9,11},{10,... | collective-permute-start | bytes 344072 | tf_op jit(solution)/shard_map/ppermute | solution.py:590
  84.6 7.9 %collective-permute-start.31 = (bf16[64,896]{1,0:T(8,128)(2,1)S(1)}, bf16[64,896]{1,0:T(8,128)(2,1)S(1)}, u32[]{:S(2)}, u32[]{:S(2)}) collective-permute-start(bf16[64,896]{1,0:T(8,128)(2,1)S(1)} %add_slot.14.refs_0_), channel_id=1, source_target_pairs={{0,2},{1,3},{2,4},{3,5},{4,6},{5,7},{6,0},{7,1},{8,10},{9,11},{10,... | collective-permute-start | bytes 344072 | tf_op jit(solution)/shard_map/ppermute | solution.py:590
  89.4 6.6 %collective-permute-start.36 = (bf16[64,896]{1,0:T(8,128)(2,1)S(1)}, bf16[64,896]{1,0:T(8,128)(2,1)S(1)}, u32[]{:S(2)}, u32[]{:S(2)}) collective-permute-start(bf16[64,896]{1,0:T(8,128)(2,1)S(1)} %pass_on.19._.refs_5_), channel_id=1, source_target_pairs={{0,2},{1,3},{2,4},{3,5},{4,6},{5,7},{6,0},{7,1},{8,10},{9,11},{10,... | collective-permute-start | bytes 344072 | tf_op jit(solution)/shard_map/ppermute | solution.py:590
  92.5 7.8 %collective-permute-start.35 = (bf16[64,896]{1,0:T(8,128)(2,1)S(1)}, bf16[64,896]{1,0:T(8,128)(2,1)S(1)}, u32[]{:S(2)}, u32[]{:S(2)}) collective-permute-start(bf16[64,896]{1,0:T(8,128)(2,1)S(1)} %pass_on.18.refs_4_), channel_id=1, source_target_pairs={{0,2},{1,3},{2,4},{3,5},{4,6},{5,7},{6,0},{7,1},{8,10},{9,11},{10,... | collective-permute-start | bytes 344072 | tf_op jit(solution)/shard_map/ppermute | solution.py:590
  96.0 8.3 %collective-permute-start.40 = (bf16[64,896]{1,0:T(8,128)(2,1)S(1)}, bf16[64,896]{1,0:T(8,128)(2,1)S(1)}, u32[]{:S(2)}, u32[]{:S(2)}) collective-permute-start(bf16[64,896]{1,0:T(8,128)(2,1)S(1)} %pass_on.21._.refs_9_), channel_id=1, source_target_pairs={{0,2},{1,3},{2,4},{3,5},{4,6},{5,7},{6,0},{7,1},{8,10},{9,11},{10,... | collective-permute-start | bytes 344072 | tf_op jit(solution)/shard_map/ppermute | solution.py:590
  100.3 6.6 %collective-permute-start.39 = (bf16[64,896]{1,0:T(8,128)(2,1)S(1)}, bf16[64,896]{1,0:T(8,128)(2,1)S(1)}, u32[]{:S(2)}, u32[]{:S(2)}) collective-permute-start(bf16[64,896]{1,0:T(8,128)(2,1)S(1)} %pass_on.20.refs_8_), channel_id=1, source_target_pairs={{0,2},{1,3},{2,4},{3,5},{4,6},{5,7},{6,0},{7,1},{8,10},{9,11},{10,... | collective-permute-start | bytes 344072 | tf_op jit(solution)/shard_map/ppermute | solution.py:590
  100.3 6.6 %collective-permute-start.30 = (bf16[64,896]{1,0:T(8,128)(2,1)S(1)}, bf16[64,896]{1,0:T(8,128)(2,1)S(1)}, u32[]{:S(2)}, u32[]{:S(2)}) collective-permute-start(bf16[64,896]{1,0:T(8,128)(2,1)S(1)} %add_slot.15.refs_1_._), channel_id=1, source_target_pairs={{0,1},{1,0},{2,3},{3,2},{4,5},{5,4},{6,7},{7,6},{8,9},{9,8},{10,11... | collective-permute-start | bytes 344072 | tf_op jit(solution)/shard_map/ppermute | solution.py:587
  100.3 7.1 %collective-permute-start.29 = (bf16[64,896]{1,0:T(8,128)(2,1)S(1)}, bf16[64,896]{1,0:T(8,128)(2,1)S(1)}, u32[]{:S(2)}, u32[]{:S(2)}) collective-permute-start(bf16[64,896]{1,0:T(8,128)(2,1)S(1)} %add_slot.14.refs_0_), channel_id=1, source_target_pairs={{0,1},{1,0},{2,3},{3,2},{4,5},{5,4},{6,7},{7,6},{8,9},{9,8},{10,11... | collective-permute-start | bytes 344072 | tf_op jit(solution)/shard_map/ppermute | solution.py:587
  100.8 6.7 %collective-permute-start.34 = (bf16[64,896]{1,0:T(8,128)(2,1)S(1)}, bf16[64,896]{1,0:T(8,128)(2,1)S(1)}, u32[]{:S(2)}, u32[]{:S(2)}) collective-permute-start(bf16[64,896]{1,0:T(8,128)(2,1)S(1)} %pass_on.19._.refs_5_), channel_id=1, source_target_pairs={{0,1},{1,0},{2,3},{3,2},{4,5},{5,4},{6,7},{7,6},{8,9},{9,8},{10,11... | collective-permute-start | bytes 344072 | tf_op jit(solution)/shard_map/ppermute | solution.py:587
  104.4 3.6 %collective-permute-start.33 = (bf16[64,896]{1,0:T(8,128)(2,1)S(1)}, bf16[64,896]{1,0:T(8,128)(2,1)S(1)}, u32[]{:S(2)}, u32[]{:S(2)}) collective-permute-start(bf16[64,896]{1,0:T(8,128)(2,1)S(1)} %pass_on.18.refs_4_), channel_id=1, source_target_pairs={{0,1},{1,0},{2,3},{3,2},{4,5},{5,4},{6,7},{7,6},{8,9},{9,8},{10,11... | collective-permute-start | bytes 344072 | tf_op jit(solution)/shard_map/ppermute | solution.py:587
  106.9 1.5 collective-permute-start.37
  107.5 1.4 collective-permute-start.41
  119.9 2.5 %collective-permute-start.43 = (bf16[256,1792]{1,0:T(8,128)(2,1)S(1)}, bf16[256,1792]{1,0:T(8,128)(2,1)S(1)}, u32[]{:S(2)}, u32[]{:S(2)}) collective-permute-start(bf16[256,1792]{1,0:T(8,128)(2,1)S(1)} %get-tuple-element.63), channel_id=1, source_target_pairs={{0,1},{1,0},{2,3},{3,2},{4,5},{5,4},{6,7},{7,6},{8,9},{9,8},{10,11... | collective-permute-start | bytes 2752520 | tf_op jit(solution)/shard_map/ppermute | solution.py:587
  122.7 7.8 %collective-permute-start.47 = (bf16[64,896]{1,0:T(8,128)(2,1)S(1)}, bf16[64,896]{1,0:T(8,128)(2,1)S(1)}, u32[]{:S(2)}, u32[]{:S(2)}) collective-permute-start(bf16[64,896]{1,0:T(8,128)(2,1)S(1)} %get-tuple-element.68), channel_id=1, source_target_pairs={{0,2},{1,3},{2,4},{3,5},{4,6},{5,7},{6,0},{7,1},{8,10},{9,11},{10,... | collective-permute-start | bytes 344072 | tf_op jit(solution)/shard_map/ppermute | solution.py:590
  122.8 9.6 %collective-permute-start.44 = (bf16[64,896]{1,0:T(8,128)(2,1)S(1)}, bf16[64,896]{1,0:T(8,128)(2,1)S(1)}, u32[]{:S(2)}, u32[]{:S(2)}) collective-permute-start(bf16[64,896]{1,0:T(8,128)(2,1)S(1)} %get-tuple-element.69), channel_id=1, source_target_pairs={{0,2},{1,3},{2,4},{3,5},{4,6},{5,7},{6,0},{7,1},{8,10},{9,11},{10,... | collective-permute-start | bytes 344072 | tf_op jit(solution)/shard_map/ppermute | solution.py:590
  131.5 7.4 %collective-permute-start.48 = (bf16[64,896]{1,0:T(8,128)(2,1)S(1)}, bf16[64,896]{1,0:T(8,128)(2,1)S(1)}, u32[]{:S(2)}, u32[]{:S(2)}) collective-permute-start(bf16[64,896]{1,0:T(8,128)(2,1)S(1)} %add_slot.18), channel_id=1, source_target_pairs={{0,2},{1,3},{2,4},{3,5},{4,6},{5,7},{6,0},{7,1},{8,10},{9,11},{10,... | collective-permute-start | bytes 344072 | tf_op jit(solution)/shard_map/ppermute | solution.py:590
  132.5 7.7 %collective-permute-start.45 = (bf16[64,896]{1,0:T(8,128)(2,1)S(1)}, bf16[64,896]{1,0:T(8,128)(2,1)S(1)}, u32[]{:S(2)}, u32[]{:S(2)}) collective-permute-start(bf16[64,896]{1,0:T(8,128)(2,1)S(1)} %add_slot.16), channel_id=1, source_target_pairs={{0,2},{1,3},{2,4},{3,5},{4,6},{5,7},{6,0},{7,1},{8,10},{9,11},{10,... | collective-permute-start | bytes 344072 | tf_op jit(solution)/shard_map/ppermute | solution.py:590
  139.0 6.6 %collective-permute-start.49 = (bf16[64,896]{1,0:T(8,128)(2,1)S(1)}, bf16[64,896]{1,0:T(8,128)(2,1)S(1)}, u32[]{:S(2)}, u32[]{:S(2)}) collective-permute-start(bf16[64,896]{1,0:T(8,128)(2,1)S(1)} %add_slot.19), channel_id=1, source_target_pairs={{0,2},{1,3},{2,4},{3,5},{4,6},{5,7},{6,0},{7,1},{8,10},{9,11},{10,... | collective-permute-start | bytes 344072 | tf_op jit(solution)/shard_map/ppermute | solution.py:590
  140.2 6.6 %collective-permute-start.46 = (bf16[64,896]{1,0:T(8,128)(2,1)S(1)}, bf16[64,896]{1,0:T(8,128)(2,1)S(1)}, u32[]{:S(2)}, u32[]{:S(2)}) collective-permute-start(bf16[64,896]{1,0:T(8,128)(2,1)S(1)} %add_slot.17), channel_id=1, source_target_pairs={{0,2},{1,3},{2,4},{3,5},{4,6},{5,7},{6,0},{7,1},{8,10},{9,11},{10,... | collective-permute-start | bytes 344072 | tf_op jit(solution)/shard_map/ppermute | solution.py:590
  (12 other events, 78.4 us)

commit v4 on v3

--- a/solution.py
+++ b/solution.py
@@ -9,6 +9,8 @@
 
 HD = 224
 EPS = 1e-05
+EARLY = 1
+CUTS = (1, 2, 4)
 F32 = jnp.float32
 BF16 = jnp.bfloat16
 NT = (((1,), (1,)), ((), ()))
@@ -70,18 +72,17 @@
         out_ref[:, i * step : (i + 1) * step, :] = jnp.swapaxes(buf[i], 0, 1)
 
 
-def unpair(weights, part, parts, after):
-    depth, two, width = weights.shape
-    rows = depth // parts
+def unpair(weights, first, rows, after):
+    _, two, width = weights.shape
     count = 4
     step = rows // count
     return pl.pallas_call(
-        functools.partial(unpair_body, part * rows),
+        functools.partial(unpair_body, first),
         in_specs=[HBM, ANY],
         out_specs=[VMEM] * 2,
         out_shape=[jax.ShapeDtypeStruct((two, rows, width), BF16), TOKEN],
         scratch_shapes=[pltpu.VMEM((count, step, two, width), BF16), pltpu.SemaphoreType.DMA((count,))],
-        compiler_params=params(10),
+        compiler_params=params(11),
         cost_estimate=QUICK,
         name="unpair",
     )(pltpu.with_memory_space_constraint(weights, pltpu.HBM), after)
@@ -139,28 +140,28 @@
         in_specs=[SMEM, HBM, ANY],
         out_specs=[VMEM] * 2,
         out_shape=[jax.ShapeDtypeStruct((units, width // 2), BF16), TOKEN],
-        scratch_shapes=[pltpu.SemaphoreType.DMA((4,))],
+        scratch_shapes=[pltpu.SemaphoreType.DMA((8,))],
         compiler_params=params(2),
         cost_estimate=QUICK,
         name="bring",
     )(place, pltpu.with_memory_space_constraint(w_down, pltpu.HBM), after)
 
 
-def pass_body(_in, _token, _out):
+def pass_body(*_refs):
     pass
 
 
-def pass_on(value, token):
+def pass_on(value, tokens):
     return pl.pallas_call(
         pass_body,
-        in_specs=[ANY, ANY],
+        in_specs=[ANY] * (1 + len(tokens)),
         out_specs=ANY,
         out_shape=jax.ShapeDtypeStruct(value.shape, value.dtype),
         input_output_aliases={0: 0},
         compiler_params=params(1),
         cost_estimate=QUICK,
         name="pass_on",
-    )(value, token)
+    )(value, *tokens)
 
 
 def split_body(count, place_ref, owner_ref, group_ref, *refs):
@@ -245,25 +246,22 @@
     )(place, pltpu.with_memory_space_constraint(weights, pltpu.HBM), after)
 
 
-def rows_body(count, shift, place_ref, *refs):
+def rows_body(count, place_ref, *refs):
     core = place_ref[1]
     out = refs[-1]
-    rows = out.shape[0]
-    side = core if shift == 0 else 1 - core
-    at = pl.multiple_of(side * rows, rows)
-    width = refs[0].shape[1]
-    for i in range(count):
-        out[:, i * width : (i + 1) * width] = refs[i][pl.ds(at, rows), :]
-
-
-def core_rows(chunks, place, shift):
-    rows = chunks[0].shape[0] // 2
-    width = sum(c.shape[1] for c in chunks)
-    return pl.pallas_call(
-        functools.partial(rows_body, len(chunks), shift),
-        in_specs=[SMEM] + [VMEM] * len(chunks),
+    step = refs[0].shape[0]
+    for i in range(count // 2):
+        out[i * step : (i + 1) * step, :] = jnp.where(core == 0, refs[i][...], refs[count // 2 + i][...])
+
+
+def core_rows(chunks, place):
+    step, width = chunks[0].shape
+    count = len(chunks)
+    return pl.pallas_call(
+        functools.partial(rows_body, count),
+        in_specs=[SMEM] + [VMEM] * count,
         out_specs=VMEM,
-        out_shape=jax.ShapeDtypeStruct((rows, width), BF16),
+        out_shape=jax.ShapeDtypeStruct((step * count // 2, width), BF16),
         compiler_params=params(4),
         cost_estimate=QUICK,
         name="core_rows",
@@ -445,16 +443,15 @@
     )(own, got, w_own, w_got)
 
 
-def add_body(row, col, got_ref, part_ref, *rest):
-    rows, width = got_ref.shape
+def add_body(row, got_ref, part_ref, *rest):
+    rows = got_ref.shape[0]
     out_ref = rest[-1]
-    total = got_ref[...].astype(F32) + part_ref[row : row + rows, col : col + width]
-    out_ref[...] = total.astype(BF16)
-
-
-def add_slot(got, partial, row, col, ties=()):
-    return pl.pallas_call(
-        functools.partial(add_body, row, col),
+    out_ref[...] = (got_ref[...].astype(F32) + part_ref[row : row + rows, :]).astype(BF16)
+
+
+def add_slot(got, partial, row, ties=()):
+    return pl.pallas_call(
+        functools.partial(add_body, row),
         in_specs=[VMEM] * 2 + [ANY] * len(ties),
         out_specs=VMEM,
         out_shape=jax.ShapeDtypeStruct(got.shape, BF16),
@@ -464,32 +461,32 @@
     )(got, partial, *ties)
 
 
-def finish_body(count, place_ref, part_ref, *refs):
-    gots = refs[:count]
-    near_ref, far_ref = refs[-2:]
-    core = place_ref[1]
-    rows = near_ref.shape[0]
-    width = gots[0].shape[1]
-    for out, side in ((near_ref, core), (far_ref, 1 - core)):
-        at = pl.multiple_of(side * rows, rows)
-        for i, got in enumerate(gots):
-            cols = slice(i * width, (i + 1) * width)
-            total = got[pl.ds(at, rows), :].astype(F32) + part_ref[pl.ds(at, rows), cols]
-            out[:, cols] = total.astype(BF16)
-
-
-def finish(gots, partial, place):
-    rows = gots[0].shape[0] // 2
-    shape = jax.ShapeDtypeStruct((rows, partial.shape[1]), BF16)
-    return pl.pallas_call(
-        functools.partial(finish_body, len(gots)),
-        in_specs=[SMEM] + [VMEM] * (1 + len(gots)),
+def finish_body(ties, by_core, place_ref, part_ref, *refs):
+    gots, outs = refs[:4], refs[4 + ties :]
+    step = gots[0].shape[0]
+    sums = []
+    for i in range(2):
+        total = part_ref[i * step : (i + 1) * step, :]
+        total = total + gots[i][...].astype(F32) + gots[2 + i][...].astype(F32)
+        sums.append(total.astype(BF16))
+    if by_core:
+        own = place_ref[1] == 0
+        sums = [jnp.where(own, sums[0], sums[1]), jnp.where(own, sums[1], sums[0])]
+    for out, value in zip(outs, sums):
+        out[...] = value
+
+
+def finish(ahead, behind, partial, place, by_core, ties):
+    shape = jax.ShapeDtypeStruct(ahead[0].shape, BF16)
+    return pl.pallas_call(
+        functools.partial(finish_body, len(ties), by_core),
+        in_specs=[SMEM] + [VMEM] * 5 + [ANY] * len(ties),
         out_specs=[VMEM] * 2,
         out_shape=[shape] * 2,
         compiler_params=params(4),
         cost_estimate=QUICK,
         name="finish",
-    )(place, partial, *gots)
+    )(place, partial, *ahead, *behind, *ties)
 
 
 def gate_body(count, dims, place_ref, gain_ref, *refs):
@@ -508,23 +505,25 @@
     at = iter(pieces)
     row = 0
     for _k in range(slots):
-        own = [next(at)[...].astype(F32) for _c in range(chunks)]
-        got = [next(at)[...].astype(F32) for _c in range(chunks)]
-        own = jnp.concatenate(own, axis=1)
-        got = jnp.concatenate(got, axis=1)
-        n = own.shape[0]
-        square = jnp.sum(own * own, axis=-1, keepdims=True) + jnp.sum(got * got, axis=-1, keepdims=True)
-        scale = lax.rsqrt(square * (0.5 / half) + EPS)
-        x_ref[core, row : row + n, :] = (own * scale * own_gain).astype(BF16)
-        x_ref[1 - core, row : row + n, :] = (got * scale * got_gain).astype(BF16)
-        row += n
-
-    per = half * 2 // parts
+        owns = [next(at) for _c in range(chunks)]
+        gots = [next(at) for _c in range(chunks)]
+        for own, got in zip(owns, gots):
+            own, got = own[...].astype(F32), got[...].astype(F32)
+            n = own.shape[0]
+            square = jnp.sum(own * own, axis=-1, keepdims=True) + jnp.sum(got * got, axis=-1, keepdims=True)
+            scale = lax.rsqrt(square * (0.5 / half) + EPS)
+            x_ref[core, row : row + n, :] = (own * scale * own_gain).astype(BF16)
+            x_ref[1 - core, row : row + n, :] = (got * scale * got_gain).astype(BF16)
+            row += n
+
     for j in range(steps):
         gate = up = None
+        at = 0
         for p in range(parts):
-            side, at = divmod(p * per, half)
-            x = x_ref[side, :, at : at + per]
+            per = weights[p].shape[1]
+            side, first = divmod(at, half)
+            at += per
+            x = x_ref[side, :, first : first + per]
             g = jnp.dot(x, weights[p][0, :, j * tile : (j + 1) * tile], preferred_element_type=F32)
             u = jnp.dot(x, weights[p][1, :, j * tile : (j + 1) * tile], preferred_element_type=F32)
             gate = g if gate is None else gate + g
@@ -539,7 +538,7 @@
 
 def gate_up(pieces, slots, chunks, weights, down, gain, place):
     half = gain.shape[0] // 2
-    rows = slots * pieces[0].shape[0]
+    rows = slots * chunks * pieces[0].shape[0]
     parts = len(weights)
     units = weights[0].shape[2]
     return pl.pallas_call(
@@ -582,6 +581,8 @@
     chips = n // 2
     both = [(h, h ^ 1) for h in range(n)]
     ring = [(h, (h + 2) % n) for h in range(n)]
+    ring_back = [(h, (h - 2) % n) for h in range(n)]
+    far = chips // 2
 
     def swap(v):
         return lax.ppermute(v, "hid", both)
@@ -589,37 +590,65 @@
     def onward(v):
         return lax.ppermute(v, "hid", ring)
 
-    def gather(own, fillers=()):
+    def back(v):
+        return lax.ppermute(v, "hid", ring_back)
+
+    def run(fillers, step, value):
+        done = [f(value) for f in fillers[step]] if step < len(fillers) else []
+        return [what for what, _ in done], [token for _, token in done]
+
+    def rotate(own, fillers=()):
         slots = [list(own)]
         here = list(own)
         gave = []
-        fillers = list(fillers)
         for k in range(1, chips):
-            done = [fillers.pop(0)(here[-1])] if fillers else []
+            what, tokens = run(fillers, k - 1, here[-1])
+            gave += what
             here = [onward(v) for v in here]
-            for what, token in done:
-                here = [pass_on(v, token) for v in here]
-                gave.append(what)
+            if tokens:
+                here = [pass_on(v, tokens) for v in here]
             slots.append(here)
-        gave += [f(here[-1])[0] for f in fillers]
         return [(s, [swap(v) for v in s]) for s in slots], gave
 
-    def scatter(partial, count, fillers=(), place=None):
-        rows = partial.shape[0] // chips
-        width = partial.shape[1] // count
-        sums = [partial[rows : 2 * rows, i * width : (i + 1) * width].astype(BF16) for i in range(count)]
+    def gather(own, fillers=()):
+        slots = [None] * chips
+        slots[0] = list(own)
+        ahead, behind = list(own), list(own)
         gave = []
-        fillers = list(fillers)
-        for k in range(2, chips + 1):
-            done = [fillers.pop(0)(sums[-1])] if fillers else []
-            ties = [d[1] for d in done]
-            gave += [d[0] for d in done]
-            sums = [onward(v) for v in sums]
-            if k == chips and place is not None:
-                return finish(sums, partial, place), gave
-            sums = [add_slot(v, partial, k % chips * rows, i * width, ties) for i, v in enumerate(sums)]
-        gave += [f(sums[-1])[0] for f in fillers]
-        return sums, gave
+        for k in range(1, far + 1):
+            what, tokens = run(fillers, k - 1, ahead[0])
+            gave += what
+            ahead[0], behind[1] = onward(ahead[0]), back(behind[1])
+            if k < far:
+                ahead[1], behind[0] = onward(ahead[1]), back(behind[0])
+                ahead[0] = pass_on(ahead[0], [*tokens, ahead[1]])
+                behind[1] = pass_on(behind[1], [*tokens, behind[0]])
+                slots[k], slots[chips - k] = list(ahead), list(behind)
+            else:
+                if tokens:
+                    ahead[0], behind[1] = pass_on(ahead[0], tokens), pass_on(behind[1], tokens)
+                slots[far] = [ahead[0], behind[1]]
+        return [(s, [swap(v) for v in s]) for s in slots], gave
+
+    def scatter(partial, place, by_core, fillers=()):
+        step = partial.shape[0] // (2 * chips)
+        row = lambda slot, i: (2 * (slot % chips) + i) * step
+        first = lambda slot, i: partial[row(slot, i) : row(slot, i) + step].astype(BF16)
+        ahead = [first(far, 0), first(chips - far + 1, 1)]
+        behind = [first(far - 1, 0), first(far, 1)]
+        gave = []
+        for d in range(far - 1, -1, -1):
+            what, ties = run(fillers, far - 1 - d, ahead[0])
+            gave += what
+            ahead[0], behind[1] = onward(ahead[0]), back(behind[1])
+            if d:
+                ahead[1], behind[0] = onward(ahead[1]), back(behind[0])
+                ahead[0] = add_slot(ahead[0], partial, row(chips - d, 0), [*ties, ahead[1]])
+                behind[1] = add_slot(behind[1], partial, row(d, 1), [*ties, behind[0]])
+            if d > 1:
+                ahead[1] = add_slot(ahead[1], partial, row(chips - d + 1, 1), ties)
+                behind[0] = add_slot(behind[0], partial, row(d - 1, 0), ties)
+        return finish(ahead, behind, partial, place, by_core, ties), gave
 
     def per_device(tokens, gain_in, w_qkv, adapt_down, adapt_up, w_out, gain_ff, w_gate_up, w_down,
                    prefix_cache, prefix_owner, group_prefix, lengths):
@@ -653,8 +682,16 @@
         candidates = [cache] + [
             lax.ppermute(cache, "req", [(r, r ^ k) for r in range(n_req)]) for k in range(1, n_req)
         ]
-        slots, given = gather(here, [hold_weights, split_out, cached])
-        (w_t, adapt_down), (w_own, w_away), kv_blocks = given
+        parts, first = [], 0
+        for side in range(2):
+            long = (half // 2 + 255) // 256 * 256
+            for rows in (long, half - long):
+                parts.append(lambda v, first=first, rows=rows: unpair(w_gate_up, first, rows, v))
+                first += rows
+        parts += [lambda v, flip=flip: bring(w_down, place, flip, v) for flip in (True, False)]
+
+        slots, given = rotate(here, [[hold_weights], [split_out] + parts[:EARLY], [cached]])
+        (w_t, adapt_down), (w_own, w_away), *early, kv_blocks = given
         kv_blocks = [
             lax.ppermute(block, "hid", [(h, h ^ (2 * k)) for h in range(n)]) if k else block
             for k, block in enumerate(kv_blocks)
@@ -666,22 +703,22 @@
         heads = attend(pick(1), w_t, adapt_down, adapt_up.T, kv_blocks, acc, lat, place, lengths, chips)
         partial = out_project(heads, swap(heads), w_own, w_got)
 
-        parts = 4
-        work = [lambda v, p=p: unpair(w_gate_up, p, parts, v) for p in range(parts)]
-        work += [lambda v, flip=flip: bring(w_down, place, flip, v) for flip in (True, False)]
-        sums, early = scatter(partial, 2, work[:3])
-        summed, late = gather(sums, work[3:])
-        *w_pairs, down_away, down_own = early + late
+        late = parts[EARLY:]
+        cuts = [0, *CUTS]
+        late = [late[i:j] for i, j in zip(cuts, cuts[1:] + [len(late)])]
+        sums, more = scatter(partial, place, False, late[:2])
+        summed, rest = gather(sums, late[2:])
+        *w_pairs, down_away, down_own = early + more + rest
 
         def first_output(_):
-            attn_own = join(core_rows(summed[0][0], place, 0), core_rows(summed[0][1], place, 0), place)
+            attn_own = join(core_rows(summed[0][0], place), core_rows(summed[0][1], place), place)
             return attn_own, attn_own
 
         pieces = [v for s in summed for v in s[0] + s[1]]
         hidden, away_half = gate_up(pieces, chips, 2, w_pairs, down_away, gain_ff, place)
         got_half = swap(away_half)
         own_half = down_half(hidden, down_own)
-        ends, (attn_own,) = scatter(own_half + got_half.astype(F32), 2, [first_output], place)
+        ends, (attn_own,) = scatter(own_half + got_half.astype(F32), place, True, [[first_output]])
         block_own = join(ends[0], swap(ends[1]), place)
         return attn_own, block_own
 

time: 150 us -> 142 us (0.947)
  waiting for transfers between devices: 61.7 us -> 38.3 us
  starting transfers between devices: 31.3 us -> 46.4 us
    ppermute x24 -> x15, waiting for transfers between devices: 52.7 us -> 23 us  [onward(): return lax.ppermute(v, 'hid', ring)]
    ppermute x0 -> x9, starting transfers between devices: none -> 15.3 us  [back(): return lax.ppermute(v, 'hid', ring_back)]
    ppermute x0 -> x9, waiting for transfers between devices: none -> 5.58 us  [back(): return lax.ppermute(v, 'hid', ring_back)]
    pallas_call x29 -> x22, Pallas kernels: 14.9 us -> 15.4 us  [the longest x4 12.9 us: unpair(): pl.pallas_call(functools.partial(unpair_body, first), in_specs=[HBM, ANY]...]
    ppermute x24 -> x15, starting transfers between devices: 16.9 us -> 16.7 us  [onward(): return lax.ppermute(v, 'hid', ring)]
  transfers between devices with their start and end apart: 51 -> 51, of which waited for: 29 -> 24; matrix products, arithmetic and copies ran while one was open for 0% -> 0% of each run, Pallas kernels for 26% -> 28%
where the time goes in v4:
time: 142 us; the launch traced here: 141 us
  Pallas kernels  52.4 us (37%)
  starting transfers between devices  46.4 us (33%)
  waiting for transfers between devices  38.3 us (27%)
  local copies, waits for them, and re-layouts  2.78 us (2%)
    ppermute x15, waiting for transfers between devices, onward(): return lax.ppermute(v, 'hid', ring)  23 us
    ppermute x15, starting transfers between devices, onward(): return lax.ppermute(v, 'hid', ring)  16.7 us
    ppermute x9, starting transfers between devices, back(): return lax.ppermute(v, 'hid', ring_back)  15.3 us
    pallas_call x4, Pallas kernels, unpair(): pl.pallas_call(functools.partial(unpair_body, first), in_specs=[HBM, ANY]...  12.9 us
    pallas_call x1, Pallas kernels, gate_up(): pl.pallas_call(functools.partial(gate_body, len(pieces), (slots, chunks,...  10.1 us
    pallas_call x2, Pallas kernels, bring(): pl.pallas_call(functools.partial(bring_body, flip), in_specs=[SMEM, HBM,...  6.89 us
    ppermute x3, starting transfers between devices, per_device(): lax.ppermute(block, 'hid', [(h, h ^ 2 * k) for h in range(n)])  5.98 us
    ppermute x9, waiting for transfers between devices, back(): return lax.ppermute(v, 'hid', ring_back)  5.58 us
  transfers between devices with their start and end apart: 51, of which 24 were waited for; matrix products, arithmetic and copies ran while one was open for 0% of the time, Pallas kernels for 28%

profile of v4, /device:TPU:0, one launch (start us, length us, event | category | flops | bytes accessed | tf_op | source)
XLA Modules:
  0.0 141.4 jit_solution(7541097788895950244)
XLA Ops:
  2.7 3.1 %collective-permute-start.15 = (bf16[32,3584]{1,0:T(8,128)(2,1)S(1)}, bf16[32,3584]{1,0:T(8,128)(2,1)S(1)}, u32[]{:S(2)}, u32[]{:S(2)}) collective-permute-start(bf16[32,3584]{1,0:T(8,128)(2,1)S(1)} %get-tuple-element.48.refs_0_), channel_id=1, source_target_pairs={{0,2},{1,3},{2,4},{3,5},{4,6},{5,7},{6,0},{7,1},{8,10},{9,11},{10,... | collective-permute-start | bytes 688136 | tf_op jit(solution)/shard_map/ppermute | solution.py:591
  5.7 1.6 %collective-permute-start.1 = (bf16[32,3584]{1,0:T(8,128)(2,1)S(1)}, bf16[32,3584]{1,0:T(8,128)(2,1)S(1)}, u32[]{:S(2)}, u32[]{:S(2)}) collective-permute-start(bf16[32,3584]{1,0:T(8,128)(2,1)S(1)} %get-tuple-element.36._.refs_0_), channel_id=1, source_target_pairs={{0,2},{1,3},{2,4},{3,5},{4,6},{5,7},{6,0},{7,1},{8,10},{9,11},{10,... | collective-permute-start | bytes 688136 | tf_op jit(solution)/shard_map/ppermute | solution.py:591
  7.3 1.5 %collective-permute-start.6 = (bf16[64,2,1792]{2,1,0:T(2,128)(2,1)}, bf16[64,2,1792]{2,1,0:T(2,128)(2,1)S(1)}, u32[]{:S(2)}, u32[]{:S(2)}) collective-permute-start(bf16[64,2,1792]{2,1,0:T(2,128)(2,1)} %bitcast.9), channel_id=1, source_target_pairs={{0,8},{8,0},{16,24},{24,16},{1,9},{9,1},{17,25},{25,17},{2,10},{10... | collective-permute-start | bytes 1376264 | tf_op jit(solution)/shard_map/ppermute | solution.py:683
  8.8 1.5 %collective-permute-start.7 = (bf16[64,2,1792]{2,1,0:T(2,128)(2,1)}, bf16[64,2,1792]{2,1,0:T(2,128)(2,1)S(1)}, u32[]{:S(2)}, u32[]{:S(2)}) collective-permute-start(bf16[64,2,1792]{2,1,0:T(2,128)(2,1)} %bitcast.10), channel_id=1, source_target_pairs={{0,16},{8,24},{16,0},{24,8},{1,17},{9,25},{17,1},{25,9},{2,18},{10... | collective-permute-start | bytes 1376264 | tf_op jit(solution)/shard_map/ppermute | solution.py:683
  10.9 4.9 %hold.1 = (bf16[672,7168]{1,0:T(8,128)(2,1)S(1)}, bf16[7168,128]{1,0:T(8,128)(2,1)S(1)}, f32[8,128]{1,0:T(8,128)S(1)}) custom-call(s32[3]{0:T(128)S(1)} %pad_add_fusion.place_ref, bf16[672,7168]{1,0:T(8,128)(2,1)} %bitcast.15, bf16[7168,128]{1,0:T(8,128)(2,1)} %down_ref.1, bf16[32,3584]{1,0:T(8,128)(2,1)S(1)} %get-tuple-element.36._.refs_0_), custom_call_target="tpu_custom_call" | custom-call | flops 1 | bytes 1 | tf_op jit(solution)/shard_map/hold/pallas_call | solution.py:106
  15.8 1.6 %collective-permute-start.17 = (bf16[32,3584]{1,0:T(8,128)(2,1)S(1)}, bf16[32,3584]{1,0:T(8,128)(2,1)S(1)}, u32[]{:S(2)}, u32[]{:S(2)}) collective-permute-start(bf16[32,3584]{1,0:T(8,128)(2,1)S(1)} %pass_on.13.refs_2_), channel_id=1, source_target_pairs={{0,2},{1,3},{2,4},{3,5},{4,6},{5,7},{6,0},{7,1},{8,10},{9,11},{10,... | collective-permute-start | bytes 688136 | tf_op jit(solution)/shard_map/ppermute | solution.py:591
  18.4 3.6 %unpair.4 = (bf16[2,1024,1792]{2,1,0:T(8,128)(2,1)S(1)}, f32[8,128]{1,0:T(8,128)S(1)}) custom-call(bf16[3584,2,1792]{2,1,0:T(2,128)(2,1)} %w_ref.11, bf16[32,3584]{1,0:T(8,128)(2,1)S(1)} %pass_on.10._.refs_2_), custom_call_target="tpu_custom_call" | custom-call | flops 1 | bytes 1 | tf_op jit(solution)/shard_map/unpair/pallas_call | solution.py:79
  22.0 1.9 %halves.1 = (bf16[224,1792]{1,0:T(8,128)(2,1)S(1)}, bf16[224,1792]{1,0:T(8,128)(2,1)S(1)}, f32[8,128]{1,0:T(8,128)S(1)}) custom-call(s32[3]{0:T(128)S(1)} %pad_add_fusion.place_ref, bf16[224,3584]{1,0:T(8,128)(2,1)} %w_ref.7, bf16[32,3584]{1,0:T(8,128)(2,1)S(1)} %pass_on.10._.refs_2_), custom_call_target="tpu_custom_call" | custom-call | flops 1 | bytes 1 | tf_op jit(solution)/shard_map/halves/pallas_call | solution.py:237
  23.9 1.5 %collective-permute-done.17._refs_0_ = bf16[32,3584]{1,0:T(8,128)(2,1)S(1)} collective-permute-done((bf16[32,3584]{1,0:T(8,128)(2,1)S(1)}, bf16[32,3584]{1,0:T(8,128)(2,1)S(1)}, u32[]{:S(2)}, u32[]{:S(2)}) %collective-permute-start.17) | collective-permute-done | bytes 229408 | tf_op jit(solution)/shard_map/ppermute | solution.py:591
  25.9 3.6 %collective-permute-done.3._refs_0_ = bf16[32,3584]{1,0:T(8,128)(2,1)S(1)} collective-permute-done((bf16[32,3584]{1,0:T(8,128)(2,1)S(1)}, bf16[32,3584]{1,0:T(8,128)(2,1)S(1)}, u32[]{:S(2)}, u32[]{:S(2)}) %collective-permute-start.3) | collective-permute-done | bytes 229408 | tf_op jit(solution)/shard_map/ppermute | solution.py:591
  30.3 1.2 split_heads.1
  33.5 1.2 collective-permute-start.5
  35.4 1.1 collective-permute-start.11
  36.5 2.3 %collective-permute-start.12 = (bf16[2,2,64,224]{3,2,1,0:T(8,128)(2,1)S(1)}, bf16[2,2,64,224]{3,2,1,0:T(8,128)(2,1)S(1)}, u32[]{:S(2)}, u32[]{:S(2)}) collective-permute-start(bf16[2,2,64,224]{3,2,1,0:T(8,128)(2,1)S(1)} %get-tuple-element.44), channel_id=1, source_target_pairs={{0,4},{1,5},{2,6},{3,7},{4,0},{5,1},{6,2},{7,3},{8,12},{9,13},{10,... | collective-permute-start | bytes 344072 | tf_op jit(solution)/shard_map/ppermute | solution.py:696
  38.8 5.0 %collective-permute-done.5._refs_0_ = bf16[32,3584]{1,0:T(8,128)(2,1)S(1)} collective-permute-done((bf16[32,3584]{1,0:T(8,128)(2,1)S(1)}, bf16[32,3584]{1,0:T(8,128)(2,1)S(1)}, u32[]{:S(2)}, u32[]{:S(2)}) %collective-permute-start.5) | collective-permute-done | bytes 229408 | tf_op jit(solution)/shard_map/ppermute | solution.py:591
  43.9 2.6 %collective-permute-start.13 = (bf16[2,2,64,224]{3,2,1,0:T(8,128)(2,1)S(1)}, bf16[2,2,64,224]{3,2,1,0:T(8,128)(2,1)S(1)}, u32[]{:S(2)}, u32[]{:S(2)}) collective-permute-start(bf16[2,2,64,224]{3,2,1,0:T(8,128)(2,1)S(1)} %get-tuple-element.45), channel_id=1, source_target_pairs={{0,6},{1,7},{2,4},{3,5},{4,2},{5,3},{6,0},{7,1},{8,14},{9,15},{10,... | collective-permute-start | bytes 344072 | tf_op jit(solution)/shard_map/ppermute | solution.py:696
  46.4 2.7 %collective-permute-done.11.refs_10_.refs_9_ = bf16[2,2,64,224]{3,2,1,0:T(8,128)(2,1)S(1)} collective-permute-done((bf16[2,2,64,224]{3,2,1,0:T(8,128)(2,1)S(1)}, bf16[2,2,64,224]{3,2,1,0:T(8,128)(2,1)S(1)}, u32[]{:S(2)}, u32[]{:S(2)}) %collective-permute-start.11) | collective-permute-done | bytes 114720 | tf_op jit(solution)/shard_map/ppermute | solution.py:696
  49.7 2.3 %collective-permute-done.13.refs_12_.refs_11_ = bf16[2,2,64,224]{3,2,1,0:T(8,128)(2,1)S(1)} collective-permute-done((bf16[2,2,64,224]{3,2,1,0:T(8,128)(2,1)S(1)}, bf16[2,2,64,224]{3,2,1,0:T(8,128)(2,1)S(1)}, u32[]{:S(2)}, u32[]{:S(2)}) %collective-permute-start.13) | collective-permute-done | bytes 114720 | tf_op jit(solution)/shard_map/ppermute | solution.py:696
  52.5 2.2 %project.1 = (f32[672,256]{1,0:T(8,128)S(1)}, f32[256,128]{1,0:T(8,128)S(1)}) custom-call(bf16[32,3584]{1,0:T(8,128)(2,1)S(1)} %get-tuple-element.48.refs_0_, bf16[32,3584]{1,0:T(8,128)(2,1)S(1)} %collective-permute-done.14.refs_1_, bf16[32,3584]{1,0:T(8,128)(2,1)S(1)} %pass_on.13.refs_2_, bf16[32,3584]{1,0:T(8,128)(2,1)S(1)} %collective-permute-done.16.refs_3_, ...), custom_call_target="tpu_custom_call" | custom-call | flops 1 | bytes 1 | tf_op jit(solution)/shard_map/project/pallas_call | solution.py:393
  54.7 4.0 %attend.1.a_ref = bf16[256,224]{1,0:T(8,128)(2,1)S(1)} custom-call(s32[3]{0:T(128)S(1)} %pad_add_fusion.place_ref, s32[1,6]{1,0:T(1,128)S(1)} %copy-done.6, bf16[32,3584]{1,0:T(8,128)(2,1)S(1)} %get-tuple-element.36._.refs_0_, bf16[32,3584]{1,0:T(8,128)(2,1)S(1)} %collective-permute-done.refs_1_, bf16[32,3584]{1,0:T(8,128)(2,1)S(1)} %pass_on.10._.refs_2_, ...), custom_call_target="tpu_custom_call" | custom-call | flops 1 | bytes 1 | tf_op jit(solution)/shard_map/attend/pallas_call | solution.py:411
  58.8 1.3 collective-permute-done.21.b_ref
  60.9 1.4 collective-permute-start.26
  62.3 2.3 %collective-permute-start.27 = (bf16[32,1792]{1,0:T(8,128)(2,1)S(1)}, bf16[32,1792]{1,0:T(8,128)(2,1)S(1)}, u32[]{:S(2)}, u32[]{:S(2)}) collective-permute-start(bf16[32,1792]{1,0:T(8,128)(2,1)S(1)} %get-tuple-element.76), channel_id=1, source_target_pairs={{0,6},{1,7},{2,0},{3,1},{4,2},{5,3},{6,4},{7,5},{8,14},{9,15},{10,... | collective-permute-start | bytes 344072 | tf_op jit(solution)/shard_map/ppermute | solution.py:594
  64.6 1.7 %collective-permute-start.24 = (bf16[32,1792]{1,0:T(8,128)(2,1)S(1)}, bf16[32,1792]{1,0:T(8,128)(2,1)S(1)}, u32[]{:S(2)}, u32[]{:S(2)}) collective-permute-start(bf16[32,1792]{1,0:T(8,128)(2,1)S(1)} %get-tuple-element.78), channel_id=1, source_target_pairs={{0,2},{1,3},{2,4},{3,5},{4,6},{5,7},{6,0},{7,1},{8,10},{9,11},{10,... | collective-permute-start | bytes 344072 | tf_op jit(solution)/shard_map/ppermute | solution.py:591
  66.3 2.9 %unpair.5 = (bf16[2,768,1792]{2,1,0:T(8,128)(2,1)S(1)}, f32[8,128]{1,0:T(8,128)S(1)}) custom-call(bf16[3584,2,1792]{2,1,0:T(2,128)(2,1)} %w_ref.11, bf16[32,1792]{1,0:T(8,128)(2,1)S(1)} %get-tuple-element.79._), custom_call_target="tpu_custom_call" | custom-call | flops 1 | bytes 1 | tf_op jit(solution)/shard_map/unpair/pallas_call | solution.py:79
  69.2 1.6 %collective-permute-done.27.got_ref = bf16[32,1792]{1,0:T(8,128)(2,1)S(1)} collective-permute-done((bf16[32,1792]{1,0:T(8,128)(2,1)S(1)}, bf16[32,1792]{1,0:T(8,128)(2,1)S(1)}, u32[]{:S(2)}, u32[]{:S(2)}) %collective-permute-start.27) | collective-permute-done | bytes 114720 | tf_op jit(solution)/shard_map/ppermute | solution.py:594
  70.8 1.7 %collective-permute-start.28 = (bf16[32,1792]{1,0:T(8,128)(2,1)S(1)}, bf16[32,1792]{1,0:T(8,128)(2,1)S(1)}, u32[]{:S(2)}, u32[]{:S(2)}) collective-permute-start(bf16[32,1792]{1,0:T(8,128)(2,1)S(1)} %add_slot.5), channel_id=1, source_target_pairs={{0,6},{1,7},{2,0},{3,1},{4,2},{5,3},{6,4},{7,5},{8,14},{9,15},{10,... | collective-permute-start | bytes 344072 | tf_op jit(solution)/shard_map/ppermute | solution.py:594
  73.7 2.4 %collective-permute-done.24.rest_1_.refs_1_ = bf16[32,1792]{1,0:T(8,128)(2,1)S(1)} collective-permute-done((bf16[32,1792]{1,0:T(8,128)(2,1)S(1)}, bf16[32,1792]{1,0:T(8,128)(2,1)S(1)}, u32[]{:S(2)}, u32[]{:S(2)}) %collective-permute-start.24) | collective-permute-done | bytes 114720 | tf_op jit(solution)/shard_map/ppermute | solution.py:591
  77.1 3.6 %unpair.6 = (bf16[2,1024,1792]{2,1,0:T(8,128)(2,1)S(1)}, f32[8,128]{1,0:T(8,128)S(1)}) custom-call(bf16[3584,2,1792]{2,1,0:T(2,128)(2,1)} %w_ref.11, bf16[32,1792]{1,0:T(8,128)(2,1)S(1)} %add_slot.4._), custom_call_target="tpu_custom_call" | custom-call | flops 1 | bytes 1 | tf_op jit(solution)/shard_map/unpair/pallas_call | solution.py:79
  80.7 2.3 %collective-permute-done.25.refs_0_ = bf16[32,1792]{1,0:T(8,128)(2,1)S(1)} collective-permute-done((bf16[32,1792]{1,0:T(8,128)(2,1)S(1)}, bf16[32,1792]{1,0:T(8,128)(2,1)S(1)}, u32[]{:S(2)}, u32[]{:S(2)}) %collective-permute-start.25) | collective-permute-done | bytes 114720 | tf_op jit(solution)/shard_map/ppermute | solution.py:591
  86.4 1.3 collective-permute-start.32
  87.7 2.9 %unpair.7 = (bf16[2,768,1792]{2,1,0:T(8,128)(2,1)S(1)}, f32[8,128]{1,0:T(8,128)S(1)}) custom-call(bf16[3584,2,1792]{2,1,0:T(2,128)(2,1)} %w_ref.11, bf16[32,1792]{1,0:T(8,128)(2,1)S(1)} %get-tuple-element.55.refs_0_._), custom_call_target="tpu_custom_call" | custom-call | flops 1 | bytes 1 | tf_op jit(solution)/shard_map/unpair/pallas_call | solution.py:79
  90.6 3.5 %bring.2 = (bf16[1792,1792]{1,0:T(8,128)(2,1)S(1)}, f32[8,128]{1,0:T(8,128)S(1)}) custom-call(s32[3]{0:T(128)S(1)} %pad_add_fusion.place_ref, bf16[1792,3584]{1,0:T(8,128)(2,1)} %w_ref.13, bf16[32,1792]{1,0:T(8,128)(2,1)S(1)} %get-tuple-element.55.refs_0_._), custom_call_target="tpu_custom_call" | custom-call | flops 1 | bytes 1 | tf_op jit(solution)/shard_map/bring/pallas_call | solution.py:138
  94.6 2.1 %collective-permute-start.38 = (bf16[32,1792]{1,0:T(8,128)(2,1)S(1)}, bf16[32,1792]{1,0:T(8,128)(2,1)S(1)}, u32[]{:S(2)}, u32[]{:S(2)}) collective-permute-start(bf16[32,1792]{1,0:T(8,128)(2,1)S(1)} %pass_on.18.refs_13_), channel_id=1, source_target_pairs={{0,6},{1,7},{2,0},{3,1},{4,2},{5,3},{6,4},{7,5},{8,14},{9,15},{10,... | collective-permute-start | bytes 344072 | tf_op jit(solution)/shard_map/ppermute | solution.py:594
  97.4 3.4 %bring.3 = (bf16[1792,1792]{1,0:T(8,128)(2,1)S(1)}, f32[8,128]{1,0:T(8,128)S(1)}) custom-call(s32[3]{0:T(128)S(1)} %pad_add_fusion.place_ref, bf16[1792,3584]{1,0:T(8,128)(2,1)} %w_ref.13, bf16[32,1792]{1,0:T(8,128)(2,1)S(1)} %pass_on.16._.refs_4_), custom_call_target="tpu_custom_call" | custom-call | flops 1 | bytes 1 | tf_op jit(solution)/shard_map/bring/pallas_call | solution.py:138
  101.4 2.0 %collective-permute-done.35._refs_0_ = bf16[32,1792]{1,0:T(8,128)(2,1)S(1)} collective-permute-done((bf16[32,1792]{1,0:T(8,128)(2,1)S(1)}, bf16[32,1792]{1,0:T(8,128)(2,1)S(1)}, u32[]{:S(2)}, u32[]{:S(2)}) %collective-permute-start.35) | collective-permute-done | bytes 114720 | tf_op jit(solution)/shard_map/ppermute | solution.py:591
  105.4 10.1 %gate_up.1 = (bf16[256,1792]{1,0:T(8,128)(2,1)S(1)}, bf16[256,1792]{1,0:T(8,128)(2,1)S(1)}) custom-call(s32[3]{0:T(128)S(1)} %pad_add_fusion.place_ref, f32[3584]{0:T(1024)S(1)} %copy-done.5, bf16[32,1792]{1,0:T(8,128)(2,1)S(1)} %get-tuple-element.55.refs_0_._, bf16[32,1792]{1,0:T(8,128)(2,1)S(1)} %get-tuple-element.56.refs_1_, ...), custom_call_target="tpu_custom_call" | custom-call | flops 1 | bytes 1 | tf_op jit(solution)/shard_map/gate_up/pallas_call | solution.py:544
  115.9 1.8 %down_half.1 = f32[256,1792]{1,0:T(8,128)S(1)} custom-call(bf16[256,1792]{1,0:T(8,128)(2,1)S(1)} %get-tuple-element.65.x_ref, bf16[1792,1792]{1,0:T(8,128)(2,1)S(1)} %get-tuple-element.66.w_ref), custom_call_target="tpu_custom_call" | custom-call | flops 1 | bytes 1 | tf_op jit(solution)/shard_map/down_half/pallas_call | solution.py:567
  118.3 1.8 %collective-permute-start.47 = (bf16[32,1792]{1,0:T(8,128)(2,1)S(1)}, bf16[32,1792]{1,0:T(8,128)(2,1)S(1)}, u32[]{:S(2)}, u32[]{:S(2)}) collective-permute-start(bf16[32,1792]{1,0:T(8,128)(2,1)S(1)} %get-tuple-element.73), channel_id=1, source_target_pairs={{0,6},{1,7},{2,0},{3,1},{4,2},{5,3},{6,4},{7,5},{8,14},{9,15},{10,... | collective-permute-start | bytes 344072 | tf_op jit(solution)/shard_map/ppermute | solution.py:594
  120.2 2.0 %collective-permute-start.44 = (bf16[32,1792]{1,0:T(8,128)(2,1)S(1)}, bf16[32,1792]{1,0:T(8,128)(2,1)S(1)}, u32[]{:S(2)}, u32[]{:S(2)}) collective-permute-start(bf16[32,1792]{1,0:T(8,128)(2,1)S(1)} %get-tuple-element.75), channel_id=1, source_target_pairs={{0,2},{1,3},{2,4},{3,5},{4,6},{5,7},{6,0},{7,1},{8,10},{9,11},{10,... | collective-permute-start | bytes 344072 | tf_op jit(solution)/shard_map/ppermute | solution.py:591
  123.5 1.3 join.2.rest_0_
  124.8 1.7 %collective-permute-done.48.got_ref = bf16[32,1792]{1,0:T(8,128)(2,1)S(1)} collective-permute-done((bf16[32,1792]{1,0:T(8,128)(2,1)S(1)}, bf16[32,1792]{1,0:T(8,128)(2,1)S(1)}, u32[]{:S(2)}, u32[]{:S(2)}) %collective-permute-start.48) | collective-permute-done | bytes 114720 | tf_op jit(solution)/shard_map/ppermute | solution.py:594
  127.5 4.0 %collective-permute-start.49 = (bf16[32,1792]{1,0:T(8,128)(2,1)S(1)}, bf16[32,1792]{1,0:T(8,128)(2,1)S(1)}, u32[]{:S(2)}, u32[]{:S(2)}) collective-permute-start(bf16[32,1792]{1,0:T(8,128)(2,1)S(1)} %add_slot.7), channel_id=1, source_target_pairs={{0,6},{1,7},{2,0},{3,1},{4,2},{5,3},{6,4},{7,5},{8,14},{9,15},{10,... | collective-permute-start | bytes 344072 | tf_op jit(solution)/shard_map/ppermute | solution.py:594
  131.5 1.6 %collective-permute-start.46 = (bf16[32,1792]{1,0:T(8,128)(2,1)S(1)}, bf16[32,1792]{1,0:T(8,128)(2,1)S(1)}, u32[]{:S(2)}, u32[]{:S(2)}) collective-permute-start(bf16[32,1792]{1,0:T(8,128)(2,1)S(1)} %add_slot.6), channel_id=1, source_target_pairs={{0,2},{1,3},{2,4},{3,5},{4,6},{5,7},{6,0},{7,1},{8,10},{9,11},{10,... | collective-permute-start | bytes 344072 | tf_op jit(solution)/shard_map/ppermute | solution.py:591
  133.0 1.7 %collective-permute-done.49.refs_3_ = bf16[32,1792]{1,0:T(8,128)(2,1)S(1)} collective-permute-done((bf16[32,1792]{1,0:T(8,128)(2,1)S(1)}, bf16[32,1792]{1,0:T(8,128)(2,1)S(1)}, u32[]{:S(2)}, u32[]{:S(2)}) %collective-permute-start.49) | collective-permute-done | bytes 114720 | tf_op jit(solution)/shard_map/ppermute | solution.py:594
  134.8 3.3 %collective-permute-done.46.refs_0_ = bf16[32,1792]{1,0:T(8,128)(2,1)S(1)} collective-permute-done((bf16[32,1792]{1,0:T(8,128)(2,1)S(1)}, bf16[32,1792]{1,0:T(8,128)(2,1)S(1)}, u32[]{:S(2)}, u32[]{:S(2)}) %collective-permute-start.46) | collective-permute-done | bytes 114720 | tf_op jit(solution)/shard_map/ppermute | solution.py:591
  138.8 1.3 collective-permute-done.50.far_ref
  140.2 1.2 join.3
  (113 shorter events, 22.7 us)
Async XLA Ops:
  2.7 13.1 %collective-permute-start.15 = (bf16[32,3584]{1,0:T(8,128)(2,1)S(1)}, bf16[32,3584]{1,0:T(8,128)(2,1)S(1)}, u32[]{:S(2)}, u32[]{:S(2)}) collective-permute-start(bf16[32,3584]{1,0:T(8,128)(2,1)S(1)} %get-tuple-element.48.refs_0_), channel_id=1, source_target_pairs={{0,2},{1,3},{2,4},{3,5},{4,6},{5,7},{6,0},{7,1},{8,10},{9,11},{10,... | collective-permute-start | bytes 688136 | tf_op jit(solution)/shard_map/ppermute | solution.py:591
  5.7 12.5 %collective-permute-start.1 = (bf16[32,3584]{1,0:T(8,128)(2,1)S(1)}, bf16[32,3584]{1,0:T(8,128)(2,1)S(1)}, u32[]{:S(2)}, u32[]{:S(2)}) collective-permute-start(bf16[32,3584]{1,0:T(8,128)(2,1)S(1)} %get-tuple-element.36._.refs_0_), channel_id=1, source_target_pairs={{0,2},{1,3},{2,4},{3,5},{4,6},{5,7},{6,0},{7,1},{8,10},{9,11},{10,... | collective-permute-start | bytes 688136 | tf_op jit(solution)/shard_map/ppermute | solution.py:591
  7.3 22.2 %collective-permute-start.6 = (bf16[64,2,1792]{2,1,0:T(2,128)(2,1)}, bf16[64,2,1792]{2,1,0:T(2,128)(2,1)S(1)}, u32[]{:S(2)}, u32[]{:S(2)}) collective-permute-start(bf16[64,2,1792]{2,1,0:T(2,128)(2,1)} %bitcast.9), channel_id=1, source_target_pairs={{0,8},{8,0},{16,24},{24,16},{1,9},{9,1},{17,25},{25,17},{2,10},{10... | collective-permute-start | bytes 1376264 | tf_op jit(solution)/shard_map/ppermute | solution.py:683
  8.8 21.5 %collective-permute-start.7 = (bf16[64,2,1792]{2,1,0:T(2,128)(2,1)}, bf16[64,2,1792]{2,1,0:T(2,128)(2,1)S(1)}, u32[]{:S(2)}, u32[]{:S(2)}) collective-permute-start(bf16[64,2,1792]{2,1,0:T(2,128)(2,1)} %bitcast.10), channel_id=1, source_target_pairs={{0,16},{8,24},{16,0},{24,8},{1,17},{9,25},{17,1},{25,9},{2,18},{10... | collective-permute-start | bytes 1376264 | tf_op jit(solution)/shard_map/ppermute | solution.py:683
  10.3 19.9 %collective-permute-start.8 = (bf16[64,2,1792]{2,1,0:T(2,128)(2,1)}, bf16[64,2,1792]{2,1,0:T(2,128)(2,1)S(1)}, u32[]{:S(2)}, u32[]{:S(2)}) collective-permute-start(bf16[64,2,1792]{2,1,0:T(2,128)(2,1)} %bitcast.11), channel_id=1, source_target_pairs={{0,24},{8,16},{16,8},{24,0},{1,25},{9,17},{17,9},{25,1},{2,26},{10... | collective-permute-start | bytes 1376264 | tf_op jit(solution)/shard_map/ppermute | solution.py:683
  15.8 9.6 %collective-permute-start.17 = (bf16[32,3584]{1,0:T(8,128)(2,1)S(1)}, bf16[32,3584]{1,0:T(8,128)(2,1)S(1)}, u32[]{:S(2)}, u32[]{:S(2)}) collective-permute-start(bf16[32,3584]{1,0:T(8,128)(2,1)S(1)} %pass_on.13.refs_2_), channel_id=1, source_target_pairs={{0,2},{1,3},{2,4},{3,5},{4,6},{5,7},{6,0},{7,1},{8,10},{9,11},{10,... | collective-permute-start | bytes 688136 | tf_op jit(solution)/shard_map/ppermute | solution.py:591
  18.3 11.2 %collective-permute-start.3 = (bf16[32,3584]{1,0:T(8,128)(2,1)S(1)}, bf16[32,3584]{1,0:T(8,128)(2,1)S(1)}, u32[]{:S(2)}, u32[]{:S(2)}) collective-permute-start(bf16[32,3584]{1,0:T(8,128)(2,1)S(1)} %pass_on.10._.refs_2_), channel_id=1, source_target_pairs={{0,2},{1,3},{2,4},{3,5},{4,6},{5,7},{6,0},{7,1},{8,10},{9,11},{10,... | collective-permute-start | bytes 688136 | tf_op jit(solution)/shard_map/ppermute | solution.py:591
  25.4 8.1 %collective-permute-start.19 = (bf16[32,3584]{1,0:T(8,128)(2,1)S(1)}, bf16[32,3584]{1,0:T(8,128)(2,1)S(1)}, u32[]{:S(2)}, u32[]{:S(2)}) collective-permute-start(bf16[32,3584]{1,0:T(8,128)(2,1)S(1)} %pass_on.14.refs_4_), channel_id=1, source_target_pairs={{0,2},{1,3},{2,4},{3,5},{4,6},{5,7},{6,0},{7,1},{8,10},{9,11},{10,... | collective-permute-start | bytes 688136 | tf_op jit(solution)/shard_map/ppermute | solution.py:591
  31.5 2.0 %collective-permute-start.9 = (bf16[4,2,64,224]{3,2,1,0:T(8,128)(2,1)S(1)}, bf16[4,2,64,224]{3,2,1,0:T(8,128)(2,1)S(1)}, u32[]{:S(2)}, u32[]{:S(2)}) collective-permute-start(bf16[4,2,64,224]{3,2,1,0:T(8,128)(2,1)S(1)} %get-tuple-element.41), channel_id=1, source_target_pairs={{0,1},{1,0},{2,3},{3,2},{4,5},{5,4},{6,7},{7,6},{8,9},{9,8},{10,11... | collective-permute-start | bytes 688136 | tf_op jit(solution)/shard_map/ppermute | solution.py:588
  31.6 3.7 %collective-permute-start.14 = (bf16[32,3584]{1,0:T(8,128)(2,1)S(1)}, bf16[32,3584]{1,0:T(8,128)(2,1)S(1)}, u32[]{:S(2)}, u32[]{:S(2)}) collective-permute-start(bf16[32,3584]{1,0:T(8,128)(2,1)S(1)} %get-tuple-element.48.refs_0_), channel_id=1, source_target_pairs={{0,1},{1,0},{2,3},{3,2},{4,5},{5,4},{6,7},{7,6},{8,9},{9,8},{10,11... | collective-permute-start | bytes 688136 | tf_op jit(solution)/shard_map/ppermute | solution.py:588
  32.1 26.7 %collective-permute-start.22 = (bf16[224,1792]{1,0:T(8,128)(2,1)S(1)}, bf16[224,1792]{1,0:T(8,128)(2,1)S(1)}, u32[]{:S(2)}, u32[]{:S(2)}) collective-permute-start(bf16[224,1792]{1,0:T(8,128)(2,1)S(1)} %get-tuple-element.52), channel_id=1, source_target_pairs={{0,1},{1,0},{2,3},{3,2},{4,5},{5,4},{6,7},{7,6},{8,9},{9,8},{10,11... | collective-permute-start | bytes 2408456 | tf_op jit(solution)/shard_map/ppermute | solution.py:588
  32.2 3.2 %collective-permute-start.16 = (bf16[32,3584]{1,0:T(8,128)(2,1)S(1)}, bf16[32,3584]{1,0:T(8,128)(2,1)S(1)}, u32[]{:S(2)}, u32[]{:S(2)}) collective-permute-start(bf16[32,3584]{1,0:T(8,128)(2,1)S(1)} %pass_on.13.refs_2_), channel_id=1, source_target_pairs={{0,1},{1,0},{2,3},{3,2},{4,5},{5,4},{6,7},{7,6},{8,9},{9,8},{10,11... | collective-permute-start | bytes 688136 | tf_op jit(solution)/shard_map/ppermute | solution.py:588
  33.5 3.0 %collective-permute-start.18 = (bf16[32,3584]{1,0:T(8,128)(2,1)S(1)}, bf16[32,3584]{1,0:T(8,128)(2,1)S(1)}, u32[]{:S(2)}, u32[]{:S(2)}) collective-permute-start(bf16[32,3584]{1,0:T(8,128)(2,1)S(1)} %pass_on.14.refs_4_), channel_id=1, source_target_pairs={{0,1},{1,0},{2,3},{3,2},{4,5},{5,4},{6,7},{7,6},{8,9},{9,8},{10,11... | collective-permute-start | bytes 688136 | tf_op jit(solution)/shard_map/ppermute | solution.py:588
  33.5 10.3 %collective-permute-start.5 = (bf16[32,3584]{1,0:T(8,128)(2,1)S(1)}, bf16[32,3584]{1,0:T(8,128)(2,1)S(1)}, u32[]{:S(2)}, u32[]{:S(2)}) collective-permute-start(bf16[32,3584]{1,0:T(8,128)(2,1)S(1)} %pass_on.11.refs_4_), channel_id=1, source_target_pairs={{0,2},{1,3},{2,4},{3,5},{4,6},{5,7},{6,0},{7,1},{8,10},{9,11},{10,... | collective-permute-start | bytes 688136 | tf_op jit(solution)/shard_map/ppermute | solution.py:591
  35.3 16.7 %collective-permute-start.20 = (bf16[32,3584]{1,0:T(8,128)(2,1)S(1)}, bf16[32,3584]{1,0:T(8,128)(2,1)S(1)}, u32[]{:S(2)}, u32[]{:S(2)}) collective-permute-start(bf16[32,3584]{1,0:T(8,128)(2,1)S(1)} %pass_on.15.refs_6_), channel_id=1, source_target_pairs={{0,1},{1,0},{2,3},{3,2},{4,5},{5,4},{6,7},{7,6},{8,9},{9,8},{10,11... | collective-permute-start | bytes 688136 | tf_op jit(solution)/shard_map/ppermute | solution.py:588
  35.4 13.8 %collective-permute-start.11 = (bf16[2,2,64,224]{3,2,1,0:T(8,128)(2,1)S(1)}, bf16[2,2,64,224]{3,2,1,0:T(8,128)(2,1)S(1)}, u32[]{:S(2)}, u32[]{:S(2)}) collective-permute-start(bf16[2,2,64,224]{3,2,1,0:T(8,128)(2,1)S(1)} %get-tuple-element.43), channel_id=1, source_target_pairs={{0,2},{1,3},{2,0},{3,1},{4,6},{5,7},{6,4},{7,5},{8,10},{9,11},{10,... | collective-permute-start | bytes 344072 | tf_op jit(solution)/shard_map/ppermute | solution.py:696
  36.5 12.7 %collective-permute-start.12 = (bf16[2,2,64,224]{3,2,1,0:T(8,128)(2,1)S(1)}, bf16[2,2,64,224]{3,2,1,0:T(8,128)(2,1)S(1)}, u32[]{:S(2)}, u32[]{:S(2)}) collective-permute-start(bf16[2,2,64,224]{3,2,1,0:T(8,128)(2,1)S(1)} %get-tuple-element.44), channel_id=1, source_target_pairs={{0,4},{1,5},{2,6},{3,7},{4,0},{5,1},{6,2},{7,3},{8,12},{9,13},{10,... | collective-permute-start | bytes 344072 | tf_op jit(solution)/shard_map/ppermute | solution.py:696
  43.9 8.1 %collective-permute-start.13 = (bf16[2,2,64,224]{3,2,1,0:T(8,128)(2,1)S(1)}, bf16[2,2,64,224]{3,2,1,0:T(8,128)(2,1)S(1)}, u32[]{:S(2)}, u32[]{:S(2)}) collective-permute-start(bf16[2,2,64,224]{3,2,1,0:T(8,128)(2,1)S(1)} %get-tuple-element.45), channel_id=1, source_target_pairs={{0,6},{1,7},{2,4},{3,5},{4,2},{5,3},{6,0},{7,1},{8,14},{9,15},{10,... | collective-permute-start | bytes 344072 | tf_op jit(solution)/shard_map/ppermute | solution.py:696
  49.2 5.5 %collective-permute-start = (bf16[32,3584]{1,0:T(8,128)(2,1)S(1)}, bf16[32,3584]{1,0:T(8,128)(2,1)S(1)}, u32[]{:S(2)}, u32[]{:S(2)}) collective-permute-start(bf16[32,3584]{1,0:T(8,128)(2,1)S(1)} %get-tuple-element.36._.refs_0_), channel_id=1, source_target_pairs={{0,1},{1,0},{2,3},{3,2},{4,5},{5,4},{6,7},{7,6},{8,9},{9,8},{10,11... | collective-permute-start | bytes 688136 | tf_op jit(solution)/shard_map/ppermute | solution.py:588
  49.2 5.5 %collective-permute-start.2 = (bf16[32,3584]{1,0:T(8,128)(2,1)S(1)}, bf16[32,3584]{1,0:T(8,128)(2,1)S(1)}, u32[]{:S(2)}, u32[]{:S(2)}) collective-permute-start(bf16[32,3584]{1,0:T(8,128)(2,1)S(1)} %pass_on.10._.refs_2_), channel_id=1, source_target_pairs={{0,1},{1,0},{2,3},{3,2},{4,5},{5,4},{6,7},{7,6},{8,9},{9,8},{10,11... | collective-permute-start | bytes 688136 | tf_op jit(solution)/shard_map/ppermute | solution.py:588
  52.0 2.7 %collective-permute-start.4 = (bf16[32,3584]{1,0:T(8,128)(2,1)S(1)}, bf16[32,3584]{1,0:T(8,128)(2,1)S(1)}, u32[]{:S(2)}, u32[]{:S(2)}) collective-permute-start(bf16[32,3584]{1,0:T(8,128)(2,1)S(1)} %pass_on.11.refs_4_), channel_id=1, source_target_pairs={{0,1},{1,0},{2,3},{3,2},{4,5},{5,4},{6,7},{7,6},{8,9},{9,8},{10,11... | collective-permute-start | bytes 688136 | tf_op jit(solution)/shard_map/ppermute | solution.py:588
  52.0 2.7 %collective-permute-start.10 = (bf16[32,3584]{1,0:T(8,128)(2,1)S(1)}, bf16[32,3584]{1,0:T(8,128)(2,1)S(1)}, u32[]{:S(2)}, u32[]{:S(2)}) collective-permute-start(bf16[32,3584]{1,0:T(8,128)(2,1)S(1)} %pass_on.12.refs_6_), channel_id=1, source_target_pairs={{0,1},{1,0},{2,3},{3,2},{4,5},{5,4},{6,7},{7,6},{8,9},{9,8},{10,11... | collective-permute-start | bytes 688136 | tf_op jit(solution)/shard_map/ppermute | solution.py:588
  58.7 1.4 collective-permute-start.21
  60.9 8.3 %collective-permute-start.26 = (bf16[32,1792]{1,0:T(8,128)(2,1)S(1)}, bf16[32,1792]{1,0:T(8,128)(2,1)S(1)}, u32[]{:S(2)}, u32[]{:S(2)}) collective-permute-start(bf16[32,1792]{1,0:T(8,128)(2,1)S(1)} %get-tuple-element.77), channel_id=1, source_target_pairs={{0,6},{1,7},{2,0},{3,1},{4,2},{5,3},{6,4},{7,5},{8,14},{9,15},{10,... | collective-permute-start | bytes 344072 | tf_op jit(solution)/shard_map/ppermute | solution.py:594
  62.3 8.5 %collective-permute-start.27 = (bf16[32,1792]{1,0:T(8,128)(2,1)S(1)}, bf16[32,1792]{1,0:T(8,128)(2,1)S(1)}, u32[]{:S(2)}, u32[]{:S(2)}) collective-permute-start(bf16[32,1792]{1,0:T(8,128)(2,1)S(1)} %get-tuple-element.76), channel_id=1, source_target_pairs={{0,6},{1,7},{2,0},{3,1},{4,2},{5,3},{6,4},{7,5},{8,14},{9,15},{10,... | collective-permute-start | bytes 344072 | tf_op jit(solution)/shard_map/ppermute | solution.py:594
  64.6 9.1 %collective-permute-start.23 = (bf16[32,1792]{1,0:T(8,128)(2,1)S(1)}, bf16[32,1792]{1,0:T(8,128)(2,1)S(1)}, u32[]{:S(2)}, u32[]{:S(2)}) collective-permute-start(bf16[32,1792]{1,0:T(8,128)(2,1)S(1)} %get-tuple-element.79._), channel_id=1, source_target_pairs={{0,2},{1,3},{2,4},{3,5},{4,6},{5,7},{6,0},{7,1},{8,10},{9,11},{10,... | collective-permute-start | bytes 344072 | tf_op jit(solution)/shard_map/ppermute | solution.py:591
  64.6 11.5 %collective-permute-start.24 = (bf16[32,1792]{1,0:T(8,128)(2,1)S(1)}, bf16[32,1792]{1,0:T(8,128)(2,1)S(1)}, u32[]{:S(2)}, u32[]{:S(2)}) collective-permute-start(bf16[32,1792]{1,0:T(8,128)(2,1)S(1)} %get-tuple-element.78), channel_id=1, source_target_pairs={{0,2},{1,3},{2,4},{3,5},{4,6},{5,7},{6,0},{7,1},{8,10},{9,11},{10,... | collective-permute-start | bytes 344072 | tf_op jit(solution)/shard_map/ppermute | solution.py:591
  70.8 9.9 %collective-permute-start.28 = (bf16[32,1792]{1,0:T(8,128)(2,1)S(1)}, bf16[32,1792]{1,0:T(8,128)(2,1)S(1)}, u32[]{:S(2)}, u32[]{:S(2)}) collective-permute-start(bf16[32,1792]{1,0:T(8,128)(2,1)S(1)} %add_slot.5), channel_id=1, source_target_pairs={{0,6},{1,7},{2,0},{3,1},{4,2},{5,3},{6,4},{7,5},{8,14},{9,15},{10,... | collective-permute-start | bytes 344072 | tf_op jit(solution)/shard_map/ppermute | solution.py:594
  76.1 6.9 %collective-permute-start.25 = (bf16[32,1792]{1,0:T(8,128)(2,1)S(1)}, bf16[32,1792]{1,0:T(8,128)(2,1)S(1)}, u32[]{:S(2)}, u32[]{:S(2)}) collective-permute-start(bf16[32,1792]{1,0:T(8,128)(2,1)S(1)} %add_slot.4._), channel_id=1, source_target_pairs={{0,2},{1,3},{2,4},{3,5},{4,6},{5,7},{6,0},{7,1},{8,10},{9,11},{10,... | collective-permute-start | bytes 344072 | tf_op jit(solution)/shard_map/ppermute | solution.py:591
  83.6 10.5 %collective-permute-start.36 = (bf16[32,1792]{1,0:T(8,128)(2,1)S(1)}, bf16[32,1792]{1,0:T(8,128)(2,1)S(1)}, u32[]{:S(2)}, u32[]{:S(2)}) collective-permute-start(bf16[32,1792]{1,0:T(8,128)(2,1)S(1)} %get-tuple-element.56.refs_1_), channel_id=1, source_target_pairs={{0,6},{1,7},{2,0},{3,1},{4,2},{5,3},{6,4},{7,5},{8,14},{9,15},{10,... | collective-permute-start | bytes 344072 | tf_op jit(solution)/shard_map/ppermute | solution.py:594
  84.4 10.2 %collective-permute-start.37 = (bf16[32,1792]{1,0:T(8,128)(2,1)S(1)}, bf16[32,1792]{1,0:T(8,128)(2,1)S(1)}, u32[]{:S(2)}, u32[]{:S(2)}) collective-permute-start(bf16[32,1792]{1,0:T(8,128)(2,1)S(1)} %get-tuple-element.55.refs_0_._), channel_id=1, source_target_pairs={{0,6},{1,7},{2,0},{3,1},{4,2},{5,3},{6,4},{7,5},{8,14},{9,15},{10,... | collective-permute-start | bytes 344072 | tf_op jit(solution)/shard_map/ppermute | solution.py:594
  85.5 11.2 %collective-permute-start.31 = (bf16[32,1792]{1,0:T(8,128)(2,1)S(1)}, bf16[32,1792]{1,0:T(8,128)(2,1)S(1)}, u32[]{:S(2)}, u32[]{:S(2)}) collective-permute-start(bf16[32,1792]{1,0:T(8,128)(2,1)S(1)} %get-tuple-element.55.refs_0_._), channel_id=1, source_target_pairs={{0,2},{1,3},{2,4},{3,5},{4,6},{5,7},{6,0},{7,1},{8,10},{9,11},{10,... | collective-permute-start | bytes 344072 | tf_op jit(solution)/shard_map/ppermute | solution.py:591
  86.4 10.3 %collective-permute-start.32 = (bf16[32,1792]{1,0:T(8,128)(2,1)S(1)}, bf16[32,1792]{1,0:T(8,128)(2,1)S(1)}, u32[]{:S(2)}, u32[]{:S(2)}) collective-permute-start(bf16[32,1792]{1,0:T(8,128)(2,1)S(1)} %get-tuple-element.56.refs_1_), channel_id=1, source_target_pairs={{0,2},{1,3},{2,4},{3,5},{4,6},{5,7},{6,0},{7,1},{8,10},{9,11},{10,... | collective-permute-start | bytes 344072 | tf_op jit(solution)/shard_map/ppermute | solution.py:591
  94.6 6.3 %collective-permute-start.38 = (bf16[32,1792]{1,0:T(8,128)(2,1)S(1)}, bf16[32,1792]{1,0:T(8,128)(2,1)S(1)}, u32[]{:S(2)}, u32[]{:S(2)}) collective-permute-start(bf16[32,1792]{1,0:T(8,128)(2,1)S(1)} %pass_on.18.refs_13_), channel_id=1, source_target_pairs={{0,6},{1,7},{2,0},{3,1},{4,2},{5,3},{6,4},{7,5},{8,14},{9,15},{10,... | collective-permute-start | bytes 344072 | tf_op jit(solution)/shard_map/ppermute | solution.py:594
  96.7 6.6 %collective-permute-start.35 = (bf16[32,1792]{1,0:T(8,128)(2,1)S(1)}, bf16[32,1792]{1,0:T(8,128)(2,1)S(1)}, u32[]{:S(2)}, u32[]{:S(2)}) collective-permute-start(bf16[32,1792]{1,0:T(8,128)(2,1)S(1)} %pass_on.16._.refs_4_), channel_id=1, source_target_pairs={{0,2},{1,3},{2,4},{3,5},{4,6},{5,7},{6,0},{7,1},{8,10},{9,11},{10,... | collective-permute-start | bytes 344072 | tf_op jit(solution)/shard_map/ppermute | solution.py:591
  96.8 6.6 %collective-permute-start.29 = (bf16[32,1792]{1,0:T(8,128)(2,1)S(1)}, bf16[32,1792]{1,0:T(8,128)(2,1)S(1)}, u32[]{:S(2)}, u32[]{:S(2)}) collective-permute-start(bf16[32,1792]{1,0:T(8,128)(2,1)S(1)} %get-tuple-element.55.refs_0_._), channel_id=1, source_target_pairs={{0,1},{1,0},{2,3},{3,2},{4,5},{5,4},{6,7},{7,6},{8,9},{9,8},{10,11... | collective-permute-start | bytes 344072 | tf_op jit(solution)/shard_map/ppermute | solution.py:588
  96.9 7.0 %collective-permute-start.30 = (bf16[32,1792]{1,0:T(8,128)(2,1)S(1)}, bf16[32,1792]{1,0:T(8,128)(2,1)S(1)}, u32[]{:S(2)}, u32[]{:S(2)}) collective-permute-start(bf16[32,1792]{1,0:T(8,128)(2,1)S(1)} %get-tuple-element.56.refs_1_), channel_id=1, source_target_pairs={{0,1},{1,0},{2,3},{3,2},{4,5},{5,4},{6,7},{7,6},{8,9},{9,8},{10,11... | collective-permute-start | bytes 344072 | tf_op jit(solution)/shard_map/ppermute | solution.py:588
  97.4 6.6 %collective-permute-start.42 = (bf16[32,1792]{1,0:T(8,128)(2,1)S(1)}, bf16[32,1792]{1,0:T(8,128)(2,1)S(1)}, u32[]{:S(2)}, u32[]{:S(2)}) collective-permute-start(bf16[32,1792]{1,0:T(8,128)(2,1)S(1)} %pass_on.18.refs_13_), channel_id=1, source_target_pairs={{0,1},{1,0},{2,3},{3,2},{4,5},{5,4},{6,7},{7,6},{8,9},{9,8},{10,11... | collective-permute-start | bytes 344072 | tf_op jit(solution)/shard_map/ppermute | solution.py:588
  100.9 3.5 %collective-permute-start.33 = (bf16[32,1792]{1,0:T(8,128)(2,1)S(1)}, bf16[32,1792]{1,0:T(8,128)(2,1)S(1)}, u32[]{:S(2)}, u32[]{:S(2)}) collective-permute-start(bf16[32,1792]{1,0:T(8,128)(2,1)S(1)} %pass_on.16._.refs_4_), channel_id=1, source_target_pairs={{0,1},{1,0},{2,3},{3,2},{4,5},{5,4},{6,7},{7,6},{8,9},{9,8},{10,11... | collective-permute-start | bytes 344072 | tf_op jit(solution)/shard_map/ppermute | solution.py:588
  103.4 1.5 %collective-permute-start.41 = (bf16[32,1792]{1,0:T(8,128)(2,1)S(1)}, bf16[32,1792]{1,0:T(8,128)(2,1)S(1)}, u32[]{:S(2)}, u32[]{:S(2)}) collective-permute-start(bf16[32,1792]{1,0:T(8,128)(2,1)S(1)} %collective-permute-done.37._refs_3_.refs_12_), channel_id=1, source_target_pairs={{0,1},{1,0},{2,3},{3,2},{4,5},{5,4},{6,7},{7,6},{8,9},{9,8},{10,11... | collective-permute-start | bytes 344072 | tf_op jit(solution)/shard_map/ppermute | solution.py:588
  103.9 1.4 %collective-permute-start.39 = (bf16[32,1792]{1,0:T(8,128)(2,1)S(1)}, bf16[32,1792]{1,0:T(8,128)(2,1)S(1)}, u32[]{:S(2)}, u32[]{:S(2)}) collective-permute-start(bf16[32,1792]{1,0:T(8,128)(2,1)S(1)} %pass_on.17.refs_8_), channel_id=1, source_target_pairs={{0,1},{1,0},{2,3},{3,2},{4,5},{5,4},{6,7},{7,6},{8,9},{9,8},{10,11... | collective-permute-start | bytes 344072 | tf_op jit(solution)/shard_map/ppermute | solution.py:588
  115.5 2.5 %collective-permute-start.43 = (bf16[256,1792]{1,0:T(8,128)(2,1)S(1)}, bf16[256,1792]{1,0:T(8,128)(2,1)S(1)}, u32[]{:S(2)}, u32[]{:S(2)}) collective-permute-start(bf16[256,1792]{1,0:T(8,128)(2,1)S(1)} %get-tuple-element.67), channel_id=1, source_target_pairs={{0,1},{1,0},{2,3},{3,2},{4,5},{5,4},{6,7},{7,6},{8,9},{9,8},{10,11... | collective-permute-start | bytes 2752520 | tf_op jit(solution)/shard_map/ppermute | solution.py:588
  118.3 6.5 %collective-permute-start.47 = (bf16[32,1792]{1,0:T(8,128)(2,1)S(1)}, bf16[32,1792]{1,0:T(8,128)(2,1)S(1)}, u32[]{:S(2)}, u32[]{:S(2)}) collective-permute-start(bf16[32,1792]{1,0:T(8,128)(2,1)S(1)} %get-tuple-element.73), channel_id=1, source_target_pairs={{0,6},{1,7},{2,0},{3,1},{4,2},{5,3},{6,4},{7,5},{8,14},{9,15},{10,... | collective-permute-start | bytes 344072 | tf_op jit(solution)/shard_map/ppermute | solution.py:594
  120.1 6.4 %collective-permute-start.48 = (bf16[32,1792]{1,0:T(8,128)(2,1)S(1)}, bf16[32,1792]{1,0:T(8,128)(2,1)S(1)}, u32[]{:S(2)}, u32[]{:S(2)}) collective-permute-start(bf16[32,1792]{1,0:T(8,128)(2,1)S(1)} %get-tuple-element.72), channel_id=1, source_target_pairs={{0,6},{1,7},{2,0},{3,1},{4,2},{5,3},{6,4},{7,5},{8,14},{9,15},{10,... | collective-permute-start | bytes 344072 | tf_op jit(solution)/shard_map/ppermute | solution.py:594
  120.2 11.2 %collective-permute-start.44 = (bf16[32,1792]{1,0:T(8,128)(2,1)S(1)}, bf16[32,1792]{1,0:T(8,128)(2,1)S(1)}, u32[]{:S(2)}, u32[]{:S(2)}) collective-permute-start(bf16[32,1792]{1,0:T(8,128)(2,1)S(1)} %get-tuple-element.75), channel_id=1, source_target_pairs={{0,2},{1,3},{2,4},{3,5},{4,6},{5,7},{6,0},{7,1},{8,10},{9,11},{10,... | collective-permute-start | bytes 344072 | tf_op jit(solution)/shard_map/ppermute | solution.py:591
  122.2 9.3 %collective-permute-start.45 = (bf16[32,1792]{1,0:T(8,128)(2,1)S(1)}, bf16[32,1792]{1,0:T(8,128)(2,1)S(1)}, u32[]{:S(2)}, u32[]{:S(2)}) collective-permute-start(bf16[32,1792]{1,0:T(8,128)(2,1)S(1)} %get-tuple-element.74), channel_id=1, source_target_pairs={{0,2},{1,3},{2,4},{3,5},{4,6},{5,7},{6,0},{7,1},{8,10},{9,11},{10,... | collective-permute-start | bytes 344072 | tf_op jit(solution)/shard_map/ppermute | solution.py:591
  127.5 7.3 %collective-permute-start.49 = (bf16[32,1792]{1,0:T(8,128)(2,1)S(1)}, bf16[32,1792]{1,0:T(8,128)(2,1)S(1)}, u32[]{:S(2)}, u32[]{:S(2)}) collective-permute-start(bf16[32,1792]{1,0:T(8,128)(2,1)S(1)} %add_slot.7), channel_id=1, source_target_pairs={{0,6},{1,7},{2,0},{3,1},{4,2},{5,3},{6,4},{7,5},{8,14},{9,15},{10,... | collective-permute-start | bytes 344072 | tf_op jit(solution)/shard_map/ppermute | solution.py:594
  131.5 6.6 %collective-permute-start.46 = (bf16[32,1792]{1,0:T(8,128)(2,1)S(1)}, bf16[32,1792]{1,0:T(8,128)(2,1)S(1)}, u32[]{:S(2)}, u32[]{:S(2)}) collective-permute-start(bf16[32,1792]{1,0:T(8,128)(2,1)S(1)} %add_slot.6), channel_id=1, source_target_pairs={{0,2},{1,3},{2,4},{3,5},{4,6},{5,7},{6,0},{7,1},{8,10},{9,11},{10,... | collective-permute-start | bytes 344072 | tf_op jit(solution)/shard_map/ppermute | solution.py:591
  (12 other events, 55.8 us)

commit v5 on v4

--- a/solution.py
+++ b/solution.py
@@ -9,7 +9,7 @@
 
 HD = 224
 EPS = 1e-05
-EARLY = 1
+EARLY, EARLY_2 = 1, 1
 CUTS = (1, 2, 4)
 F32 = jnp.float32
 BF16 = jnp.bfloat16
@@ -36,10 +36,19 @@
     return 256 if width % 256 == 0 else width
 
 
-def norm_body(tok_ref, gain_ref, *outs):
-    t = tok_ref[...].astype(F32)
+def norm_body(tok_ref, gain_ref, *refs):
+    *outs, tok, gain, sems = refs
+    copies = [
+        pltpu.make_async_copy(tok_ref, tok, sems.at[0]),
+        pltpu.make_async_copy(gain_ref, gain, sems.at[1]),
+    ]
+    for c in copies:
+        c.start()
+    for c in copies:
+        c.wait()
+    t = tok[...].astype(F32)
     scale = lax.rsqrt(jnp.mean(t * t, axis=-1, keepdims=True) + EPS)
-    normed = (t * scale * gain_ref[...]).astype(BF16)
+    normed = (t * scale * gain[...]).astype(BF16)
     width = t.shape[1] // len(outs)
     for i, out in enumerate(outs):
         out[...] = normed[:, i * width : (i + 1) * width]
@@ -49,13 +58,18 @@
     rows, width = tokens.shape
     return pl.pallas_call(
         norm_body,
-        in_specs=[VMEM, VMEM],
+        in_specs=[HBM, HBM],
         out_specs=[VMEM] * count,
         out_shape=[jax.ShapeDtypeStruct((rows, width // count), BF16)] * count,
-        compiler_params=params(16),
+        scratch_shapes=[
+            pltpu.VMEM((rows, width), BF16),
+            pltpu.VMEM((1, width), F32),
+            pltpu.SemaphoreType.DMA((2,)),
+        ],
+        compiler_params=params(8),
         cost_estimate=QUICK,
         name="norm_rows",
-    )(tokens, gain)
+    )(pltpu.with_memory_space_constraint(tokens, pltpu.HBM), pltpu.with_memory_space_constraint(gain, pltpu.HBM))
 
 
 def unpair_body(first, w_ref, _, out_ref, token_ref, buf, sems):
@@ -147,6 +161,24 @@
     )(place, pltpu.with_memory_space_constraint(w_down, pltpu.HBM), after)
 
 
+def stack_body(*refs):
+    out_ref = refs[-1]
+    for i, ref in enumerate(refs[:-1]):
+        out_ref[i] = ref[...]
+
+
+def stack(values):
+    return pl.pallas_call(
+        stack_body,
+        in_specs=[VMEM] * len(values),
+        out_specs=VMEM,
+        out_shape=jax.ShapeDtypeStruct((len(values), *values[0].shape), BF16),
+        compiler_params=params(4),
+        cost_estimate=QUICK,
+        name="stack",
+    )(*values)
+
+
 def pass_body(*_refs):
     pass
 
@@ -169,28 +201,29 @@
     mine_ref, other_ref = refs[-2:]
     core, req = place_ref[1], place_ref[2]
     away = owner_ref[group_ref[req]] ^ req
-    chips = mine_ref.shape[0]
-    cols = mine_ref.shape[3]
+    chips, two, cols, _ = mine_ref.shape
     chosen = candidates[0][...]
     for k in range(1, count):
         chosen = jnp.where(away == k, candidates[k][...], chosen)
-    chosen = jnp.swapaxes(chosen, 0, 1)
-    for c in range(chips):
-        even = chosen[:, :, 2 * c * cols : (2 * c + 1) * cols]
-        odd = chosen[:, :, (2 * c + 1) * cols : (2 * c + 2) * cols]
-        mine_ref[c] = jnp.where(core == 0, even, odd)
-        other_ref[c] = jnp.where(core == 0, odd, even)
+    chosen = jnp.swapaxes(chosen, 0, 1).astype(F32)
+    for kind in range(two):
+        turned = chosen[kind].T.astype(BF16)
+        for c in range(chips):
+            even = turned[2 * c * cols : (2 * c + 1) * cols]
+            odd = turned[(2 * c + 1) * cols : (2 * c + 2) * cols]
+            mine_ref[c, kind] = jnp.where(core == 0, even, odd)
+            other_ref[c, kind] = jnp.where(core == 0, odd, even)
 
 
 def split_heads(candidates, place, owner, group, chips, ties):
     positions, two, width = candidates[0].shape
-    shape = jax.ShapeDtypeStruct((chips, two, positions, width // (2 * chips)), BF16)
+    shape = jax.ShapeDtypeStruct((chips, two, width // (2 * chips), positions), BF16)
     return pl.pallas_call(
         functools.partial(split_body, len(candidates)),
         in_specs=[SMEM] * 3 + [VMEM] * len(candidates) + [ANY] * len(ties),
         out_specs=[VMEM] * 2,
         out_shape=[shape] * 2,
-        compiler_params=params(16),
+        compiler_params=params(2 + candidates[0].size * 24 // 2**20),
         cost_estimate=QUICK,
         name="split_heads",
     )(place, owner, group, *candidates, *ties)
@@ -199,13 +232,13 @@
 def pack_body(place_ref, mine_ref, got_ref, *outs):
     chip = place_ref[0]
     for k, out in enumerate(outs):
-        out[0] = mine_ref[chip ^ k]
-        out[1] = got_ref[chip ^ k]
+        for kind in range(out.shape[0]):
+            out[kind] = jnp.concatenate([mine_ref[chip ^ k, kind], got_ref[chip ^ k, kind]], axis=1)
 
 
 def pack_blocks(mine, got, place):
     chips = mine.shape[0]
-    shape = jax.ShapeDtypeStruct((2, *mine.shape[1:]), BF16)
+    shape = jax.ShapeDtypeStruct((*mine.shape[1:3], 2 * mine.shape[3]), BF16)
     return pl.pallas_call(
         pack_body,
         in_specs=[SMEM, VMEM, VMEM],
@@ -292,8 +325,9 @@
 def project_part(pieces, part, w_ref, down_ref, rows_ref, acc_ref, lat_ref, acc, lat):
     at = 0
     for piece in pieces:
-        rows_ref[at : at + piece.shape[0], :] = piece[...]
-        at += piece.shape[0]
+        n = piece.shape[-2]
+        rows_ref[at : at + n, :] = piece[part] if len(piece.shape) == 3 else piece[...]
+        at += n
     width = rows_ref.shape[1]
     kb = width // 4
     for s in range(4):
@@ -328,8 +362,8 @@
     chip, core = place_ref[0], place_ref[1]
     keys_t = acc_ref[cols : 2 * cols, :].astype(BF16)
     vals_t = acc_ref[2 * cols :, :].astype(BF16)
-    cached_k = jnp.concatenate([kv[s, 0] for kv in kv_refs for s in range(2)], axis=0)
-    cached_v = jnp.concatenate([kv[s, 1] for kv in kv_refs for s in range(2)], axis=0)
+    cached_k = jnp.concatenate([kv[0] for kv in kv_refs], axis=1)
+    cached_v = jnp.concatenate([kv[1] for kv in kv_refs], axis=1)
     up = up_ref[...]
     scale = HD ** (-0.5)
     pair = 2 * tok_dev
@@ -362,14 +396,14 @@
         q = q.astype(BF16)
         q_spot = spots(r0 + lax.broadcasted_iota(jnp.int32, (1, block), 1))
         allowed = jnp.logical_and(requests(q_spot) == key_req, key_spot <= q_spot)
-        pre = jnp.dot(cached_k, q, preferred_element_type=F32) * scale
+        pre = lax.dot_general(cached_k, q, TN, preferred_element_type=F32) * scale
         suf = lax.dot_general(keys_t, q, TN, preferred_element_type=F32) * scale
         suf = jnp.where(allowed, suf, -jnp.inf)
         top = jnp.maximum(jnp.max(pre, axis=0, keepdims=True), jnp.max(suf, axis=0, keepdims=True))
         pre = jnp.exp(pre - top)
         suf = jnp.exp(suf - top)
         total = jnp.sum(pre, axis=0, keepdims=True) + jnp.sum(suf, axis=0, keepdims=True)
-        weighted = lax.dot_general(cached_v, pre.astype(BF16), TN, preferred_element_type=F32) + jnp.dot(
+        weighted = jnp.dot(cached_v, pre.astype(BF16), preferred_element_type=F32) + jnp.dot(
             vals_t, suf.astype(BF16), preferred_element_type=F32
         )
         heads = (weighted / total).T.astype(BF16)
@@ -387,7 +421,7 @@
 
 
 def project(pieces, w_t, down, ties):
-    rows = sum(p.shape[0] for p in pieces)
+    rows = sum(p.shape[-2] for p in pieces)
     width = pieces[0].shape[1]
     cols3, rank = w_t.shape[0], down.shape[1]
     return pl.pallas_call(
@@ -403,7 +437,7 @@
 
 
 def attend(pieces, w_t, down, up_t, kv_blocks, acc, lat, place, lengths, chips):
-    rows = sum(p.shape[0] for p in pieces)
+    rows = sum(p.shape[-2] for p in pieces)
     width = pieces[0].shape[1]
     cols3, rank = w_t.shape[0], down.shape[1]
     cols = cols3 // 3
@@ -418,7 +452,7 @@
             pltpu.VMEM((cols3, rows), F32),
             pltpu.VMEM((rows, rank), F32),
         ],
-        compiler_params=params(10 + rows * width * 5 // 2**20),
+        compiler_params=params(6 + rows * width * 5 // 2**20),
         cost_estimate=QUICK,
         name="attend",
     )(place, lengths, *pieces, *kv_blocks, w_t, down, up_t, acc, lat)
@@ -595,7 +629,8 @@
 
     def run(fillers, step, value):
         done = [f(value) for f in fillers[step]] if step < len(fillers) else []
-        return [what for what, _ in done], [token for _, token in done]
+        tokens = [t for _, token in done for t in (token if isinstance(token, list) else [token])]
+        return [what for what, _ in done], tokens
 
     def rotate(own, fillers=()):
         slots = [list(own)]
@@ -604,6 +639,8 @@
         for k in range(1, chips):
             what, tokens = run(fillers, k - 1, here[-1])
             gave += what
+            if k == chips - 1:
+                here = [stack(here)]
             here = [onward(v) for v in here]
             if tokens:
                 here = [pass_on(v, tokens) for v in here]
@@ -676,7 +713,12 @@
         def cached(v):
             mine, other = split_heads(candidates, place, prefix_owner, group_prefix, chips, [v])
             blocks = pack_blocks(mine, swap(other), place)
-            return blocks, blocks[0]
+            got = [
+                lax.ppermute(block, "hid", [(h, h ^ (2 * k)) for h in range(n)])
+                for k, block in enumerate(blocks)
+                if k
+            ]
+            return [blocks[0], *got], got
 
         cache = prefix_cache[0]
         candidates = [cache] + [
@@ -690,20 +732,16 @@
                 first += rows
         parts += [lambda v, flip=flip: bring(w_down, place, flip, v) for flip in (True, False)]
 
-        slots, given = rotate(here, [[hold_weights], [split_out] + parts[:EARLY], [cached]])
+        slots, given = rotate(here, [[hold_weights], [split_out] + parts[:EARLY], parts[EARLY:EARLY_2] + [cached]])
         (w_t, adapt_down), (w_own, w_away), *early, kv_blocks = given
-        kv_blocks = [
-            lax.ppermute(block, "hid", [(h, h ^ (2 * k)) for h in range(n)]) if k else block
-            for k, block in enumerate(kv_blocks)
-        ]
         w_got = swap(w_away)
 
-        pick = lambda i: [v for s in slots for v in (s[0][i], s[1][i])]
-        acc, lat = project(pick(0), w_t, adapt_down, kv_blocks[1:])
+        pick = lambda i: [v for near, far_side in slots for v in (near[min(i, len(near) - 1)], far_side[min(i, len(far_side) - 1)])]
+        acc, lat = project(pick(0), w_t, adapt_down, ())
         heads = attend(pick(1), w_t, adapt_down, adapt_up.T, kv_blocks, acc, lat, place, lengths, chips)
         partial = out_project(heads, swap(heads), w_own, w_got)
 
-        late = parts[EARLY:]
+        late = parts[EARLY_2:]
         cuts = [0, *CUTS]
         late = [late[i:j] for i, j in zip(cuts, cuts[1:] + [len(late)])]
         sums, more = scatter(partial, place, False, late[:2])

time: 142 us -> 140 us (0.986)
  starting transfers between devices: 46.4 us -> 43.4 us
  waiting for transfers between devices: 38.3 us -> 40.4 us
  local copies, waits for them, and re-layouts: 2.78 us -> 1.03 us
    ppermute x15 -> x14, waiting for transfers between devices: 23 us -> 16.5 us  [onward(): return lax.ppermute(v, 'hid', ring)]
    ppermute x3, waiting for transfers between devices: 5.02 us -> 11.1 us  [cached(): lax.ppermute(block, 'hid', [(h, h ^ 2 * k) for h in range(n)])]
    ppermute x21 -> x20, waiting for transfers between devices: 3.93 us -> 6.38 us  [swap(): return lax.ppermute(v, 'hid', both)]
    unnamed x18 -> x14, local copies, waits for them, and re-layouts: 2.72 us -> 0.96 us
    ppermute x15 -> x14, starting transfers between devices: 16.7 us -> 15.1 us  [onward(): return lax.ppermute(v, 'hid', ring)]
    ppermute x3, starting transfers between devices: 5.98 us -> 4.45 us  [cached(): lax.ppermute(block, 'hid', [(h, h ^ 2 * k) for h in range(n)])]
    ppermute x21 -> x20, starting transfers between devices: 4.92 us -> 5.2 us  [swap(): return lax.ppermute(v, 'hid', both)]
  transfers between devices with their start and end apart: 51 -> 49, of which waited for: 24 -> 25; matrix products, arithmetic and copies ran while one was open for 0% -> 0% of each run, Pallas kernels for 28% -> 28%
where the time goes in v5:
time: 140 us
  Pallas kernels  53.5 us (38%)
  starting transfers between devices  43.4 us (31%)
  waiting for transfers between devices  40.4 us (29%)
    ppermute x14, waiting for transfers between devices, onward(): return lax.ppermute(v, 'hid', ring)  16.5 us
    ppermute x9, starting transfers between devices, back(): return lax.ppermute(v, 'hid', ring_back)  15.2 us
    ppermute x14, starting transfers between devices, onward(): return lax.ppermute(v, 'hid', ring)  15.1 us
    pallas_call x4, Pallas kernels, unpair(): pl.pallas_call(functools.partial(unpair_body, first), in_specs=[HBM, ANY]...  12.9 us
    ppermute x3, waiting for transfers between devices, cached(): lax.ppermute(block, 'hid', [(h, h ^ 2 * k) for h in range(n)])  11.1 us
    pallas_call x1, Pallas kernels, gate_up(): pl.pallas_call(functools.partial(gate_body, len(pieces), (slots, chunks,...  10.1 us
    pallas_call x2, Pallas kernels, bring(): pl.pallas_call(functools.partial(bring_body, flip), in_specs=[SMEM, HBM,...  6.89 us
    ppermute x20, waiting for transfers between devices, swap(): return lax.ppermute(v, 'hid', both)  6.38 us
  transfers between devices with their start and end apart: 49, of which 25 were waited for; matrix products, arithmetic and copies ran while one was open for 0% of the time, Pallas kernels for 28%

profile of v5, /device:TPU:0, one launch (start us, length us, event | category | flops | bytes accessed | tf_op | source)
XLA Modules:
  0.0 139.7 jit_solution(4156827271894145443)
XLA Ops:
  0.6 1.3 norm_rows.1
  1.9 3.1 %collective-permute-start.1 = (bf16[32,3584]{1,0:T(8,128)(2,1)S(1)}, bf16[32,3584]{1,0:T(8,128)(2,1)S(1)}, u32[]{:S(2)}, u32[]{:S(2)}) collective-permute-start(bf16[32,3584]{1,0:T(8,128)(2,1)S(1)} %get-tuple-element.36._.refs_0_), channel_id=1, source_target_pairs={{0,2},{1,3},{2,4},{3,5},{4,6},{5,7},{6,0},{7,1},{8,10},{9,11},{10,... | collective-permute-start | bytes 688136 | tf_op jit(solution)/shard_map/ppermute | solution.py:625
  5.0 1.6 %collective-permute-start.5 = (bf16[32,3584]{1,0:T(8,128)(2,1)S(1)}, bf16[32,3584]{1,0:T(8,128)(2,1)S(1)}, u32[]{:S(2)}, u32[]{:S(2)}) collective-permute-start(bf16[32,3584]{1,0:T(8,128)(2,1)S(1)} %get-tuple-element.40.refs_0_), channel_id=1, source_target_pairs={{0,2},{1,3},{2,4},{3,5},{4,6},{5,7},{6,0},{7,1},{8,10},{9,11},{10,... | collective-permute-start | bytes 688136 | tf_op jit(solution)/shard_map/ppermute | solution.py:625
  6.6 2.4 %collective-permute-start.10 = (bf16[64,2,1792]{2,1,0:T(2,128)(2,1)}, bf16[64,2,1792]{2,1,0:T(2,128)(2,1)S(1)}, u32[]{:S(2)}, u32[]{:S(2)}) collective-permute-start(bf16[64,2,1792]{2,1,0:T(2,128)(2,1)} %bitcast.9), channel_id=1, source_target_pairs={{0,24},{8,16},{16,8},{24,0},{1,25},{9,17},{17,9},{25,1},{2,26},{10... | collective-permute-start | bytes 1376264 | tf_op jit(solution)/shard_map/ppermute | solution.py:725
  10.2 4.9 %hold.1 = (bf16[672,7168]{1,0:T(8,128)(2,1)S(1)}, bf16[7168,128]{1,0:T(8,128)(2,1)S(1)}, f32[8,128]{1,0:T(8,128)S(1)}) custom-call(s32[3]{0:T(128)S(1)} %pad_add_fusion.place_ref, bf16[672,7168]{1,0:T(8,128)(2,1)} %bitcast.14, bf16[7168,128]{1,0:T(8,128)(2,1)} %down_ref.1, bf16[32,3584]{1,0:T(8,128)(2,1)S(1)} %get-tuple-element.36._.refs_0_), custom_call_target="tpu_custom_call" | custom-call | flops 1 | bytes 1 | tf_op jit(solution)/shard_map/hold/pallas_call | solution.py:120
  15.1 1.6 %collective-permute-start.3 = (bf16[32,3584]{1,0:T(8,128)(2,1)S(1)}, bf16[32,3584]{1,0:T(8,128)(2,1)S(1)}, u32[]{:S(2)}, u32[]{:S(2)}) collective-permute-start(bf16[32,3584]{1,0:T(8,128)(2,1)S(1)} %pass_on.9._.refs_2_), channel_id=1, source_target_pairs={{0,2},{1,3},{2,4},{3,5},{4,6},{5,7},{6,0},{7,1},{8,10},{9,11},{10,... | collective-permute-start | bytes 688136 | tf_op jit(solution)/shard_map/ppermute | solution.py:625
  17.6 3.6 %unpair.4 = (bf16[2,1024,1792]{2,1,0:T(8,128)(2,1)S(1)}, f32[8,128]{1,0:T(8,128)S(1)}) custom-call(bf16[3584,2,1792]{2,1,0:T(2,128)(2,1)} %w_ref.11, bf16[32,3584]{1,0:T(8,128)(2,1)S(1)} %pass_on.9._.refs_2_), custom_call_target="tpu_custom_call" | custom-call | flops 1 | bytes 1 | tf_op jit(solution)/shard_map/unpair/pallas_call | solution.py:93
  21.2 1.9 %halves.1 = (bf16[224,1792]{1,0:T(8,128)(2,1)S(1)}, bf16[224,1792]{1,0:T(8,128)(2,1)S(1)}, f32[8,128]{1,0:T(8,128)S(1)}) custom-call(s32[3]{0:T(128)S(1)} %pad_add_fusion.place_ref, bf16[224,3584]{1,0:T(8,128)(2,1)} %w_ref.7, bf16[32,3584]{1,0:T(8,128)(2,1)S(1)} %pass_on.9._.refs_2_), custom_call_target="tpu_custom_call" | custom-call | flops 1 | bytes 1 | tf_op jit(solution)/shard_map/halves/pallas_call | solution.py:270
  23.2 1.5 %collective-permute-done.3._refs_0_ = bf16[32,3584]{1,0:T(8,128)(2,1)S(1)} collective-permute-done((bf16[32,3584]{1,0:T(8,128)(2,1)S(1)}, bf16[32,3584]{1,0:T(8,128)(2,1)S(1)}, u32[]{:S(2)}, u32[]{:S(2)}) %collective-permute-start.3) | collective-permute-done | bytes 229408 | tf_op jit(solution)/shard_map/ppermute | solution.py:625
  24.7 3.2 %collective-permute-done.6._refs_0_ = bf16[32,3584]{1,0:T(8,128)(2,1)S(1)} collective-permute-done((bf16[32,3584]{1,0:T(8,128)(2,1)S(1)}, bf16[32,3584]{1,0:T(8,128)(2,1)S(1)}, u32[]{:S(2)}, u32[]{:S(2)}) %collective-permute-start.6) | collective-permute-done | bytes 229408 | tf_op jit(solution)/shard_map/ppermute | solution.py:625
  28.0 1.3 collective-permute-done.8.refs_1_
  31.0 1.3 collective-permute-done.11.got_ref
  33.0 1.6 %collective-permute-start.12 = (bf16[2,224,128]{2,1,0:T(8,128)(2,1)S(1)}, bf16[2,224,128]{2,1,0:T(8,128)(2,1)S(1)}, u32[]{:S(2)}, u32[]{:S(2)}) collective-permute-start(bf16[2,224,128]{2,1,0:T(8,128)(2,1)S(1)} %get-tuple-element.43), channel_id=1, source_target_pairs={{0,2},{1,3},{2,0},{3,1},{4,6},{5,7},{6,4},{7,5},{8,10},{9,11},{10,... | collective-permute-start | bytes 344072 | tf_op jit(solution)/shard_map/ppermute | solution.py:717
  34.7 1.5 %collective-permute-start.13 = (bf16[2,224,128]{2,1,0:T(8,128)(2,1)S(1)}, bf16[2,224,128]{2,1,0:T(8,128)(2,1)S(1)}, u32[]{:S(2)}, u32[]{:S(2)}) collective-permute-start(bf16[2,224,128]{2,1,0:T(8,128)(2,1)S(1)} %get-tuple-element.44), channel_id=1, source_target_pairs={{0,4},{1,5},{2,6},{3,7},{4,0},{5,1},{6,2},{7,3},{8,12},{9,13},{10,... | collective-permute-start | bytes 344072 | tf_op jit(solution)/shard_map/ppermute | solution.py:717
  36.1 1.3 collective-permute-start.14
  37.5 9.0 %collective-permute-done.12._refs_1_.refs_9_ = bf16[2,224,128]{2,1,0:T(8,128)(2,1)S(1)} collective-permute-done((bf16[2,224,128]{2,1,0:T(8,128)(2,1)S(1)}, bf16[2,224,128]{2,1,0:T(8,128)(2,1)S(1)}, u32[]{:S(2)}, u32[]{:S(2)}) %collective-permute-start.12) | collective-permute-done | bytes 114720 | tf_op jit(solution)/shard_map/ppermute | solution.py:717
  46.4 2.1 %collective-permute-done.13._refs_2_.refs_10_ = bf16[2,224,128]{2,1,0:T(8,128)(2,1)S(1)} collective-permute-done((bf16[2,224,128]{2,1,0:T(8,128)(2,1)S(1)}, bf16[2,224,128]{2,1,0:T(8,128)(2,1)S(1)}, u32[]{:S(2)}, u32[]{:S(2)}) %collective-permute-start.13) | collective-permute-done | bytes 114720 | tf_op jit(solution)/shard_map/ppermute | solution.py:717
  51.6 2.1 %project.1 = (f32[672,256]{1,0:T(8,128)S(1)}, f32[256,128]{1,0:T(8,128)S(1)}) custom-call(bf16[32,3584]{1,0:T(8,128)(2,1)S(1)} %get-tuple-element.40.refs_0_, bf16[32,3584]{1,0:T(8,128)(2,1)S(1)} %collective-permute-done.16.refs_1_, bf16[32,3584]{1,0:T(8,128)(2,1)S(1)} %pass_on.11.refs_2_, bf16[32,3584]{1,0:T(8,128)(2,1)S(1)} %collective-permute-done.17.refs_3_, ...), custom_call_target="tpu_custom_call" | custom-call | flops 1 | bytes 1 | tf_op jit(solution)/shard_map/project/pallas_call | solution.py:427
  53.8 4.0 %attend.1.a_ref = bf16[256,224]{1,0:T(8,128)(2,1)S(1)} custom-call(s32[3]{0:T(128)S(1)} %pad_add_fusion.place_ref, s32[1,6]{1,0:T(1,128)S(1)} %copy-done.4, bf16[32,3584]{1,0:T(8,128)(2,1)S(1)} %get-tuple-element.36._.refs_0_, bf16[32,3584]{1,0:T(8,128)(2,1)S(1)} %collective-permute-done.refs_1_, bf16[32,3584]{1,0:T(8,128)(2,1)S(1)} %pass_on.9._.refs_2_, ...), custom_call_target="tpu_custom_call" | custom-call | flops 1 | bytes 1 | tf_op jit(solution)/shard_map/attend/pallas_call | solution.py:445
  60.1 2.8 %collective-permute-start.25 = (bf16[32,1792]{1,0:T(8,128)(2,1)S(1)}, bf16[32,1792]{1,0:T(8,128)(2,1)S(1)}, u32[]{:S(2)}, u32[]{:S(2)}) collective-permute-start(bf16[32,1792]{1,0:T(8,128)(2,1)S(1)} %get-tuple-element.76), channel_id=1, source_target_pairs={{0,6},{1,7},{2,0},{3,1},{4,2},{5,3},{6,4},{7,5},{8,14},{9,15},{10,... | collective-permute-start | bytes 344072 | tf_op jit(solution)/shard_map/ppermute | solution.py:628
  62.9 1.6 %collective-permute-start.22 = (bf16[32,1792]{1,0:T(8,128)(2,1)S(1)}, bf16[32,1792]{1,0:T(8,128)(2,1)S(1)}, u32[]{:S(2)}, u32[]{:S(2)}) collective-permute-start(bf16[32,1792]{1,0:T(8,128)(2,1)S(1)} %get-tuple-element.78), channel_id=1, source_target_pairs={{0,2},{1,3},{2,4},{3,5},{4,6},{5,7},{6,0},{7,1},{8,10},{9,11},{10,... | collective-permute-start | bytes 344072 | tf_op jit(solution)/shard_map/ppermute | solution.py:625
  64.6 2.9 %unpair.5 = (bf16[2,768,1792]{2,1,0:T(8,128)(2,1)S(1)}, f32[8,128]{1,0:T(8,128)S(1)}) custom-call(bf16[3584,2,1792]{2,1,0:T(2,128)(2,1)} %w_ref.11, bf16[32,1792]{1,0:T(8,128)(2,1)S(1)} %get-tuple-element.79._), custom_call_target="tpu_custom_call" | custom-call | flops 1 | bytes 1 | tf_op jit(solution)/shard_map/unpair/pallas_call | solution.py:93
  67.5 1.6 %collective-permute-done.25.got_ref = bf16[32,1792]{1,0:T(8,128)(2,1)S(1)} collective-permute-done((bf16[32,1792]{1,0:T(8,128)(2,1)S(1)}, bf16[32,1792]{1,0:T(8,128)(2,1)S(1)}, u32[]{:S(2)}, u32[]{:S(2)}) %collective-permute-start.25) | collective-permute-done | bytes 114720 | tf_op jit(solution)/shard_map/ppermute | solution.py:628
  69.1 1.7 %collective-permute-start.26 = (bf16[32,1792]{1,0:T(8,128)(2,1)S(1)}, bf16[32,1792]{1,0:T(8,128)(2,1)S(1)}, u32[]{:S(2)}, u32[]{:S(2)}) collective-permute-start(bf16[32,1792]{1,0:T(8,128)(2,1)S(1)} %add_slot.5), channel_id=1, source_target_pairs={{0,6},{1,7},{2,0},{3,1},{4,2},{5,3},{6,4},{7,5},{8,14},{9,15},{10,... | collective-permute-start | bytes 344072 | tf_op jit(solution)/shard_map/ppermute | solution.py:628
  70.8 1.1 collective-permute-done.21.got_ref
  72.0 2.4 %collective-permute-done.22.rest_1_.refs_1_ = bf16[32,1792]{1,0:T(8,128)(2,1)S(1)} collective-permute-done((bf16[32,1792]{1,0:T(8,128)(2,1)S(1)}, bf16[32,1792]{1,0:T(8,128)(2,1)S(1)}, u32[]{:S(2)}, u32[]{:S(2)}) %collective-permute-start.22) | collective-permute-done | bytes 114720 | tf_op jit(solution)/shard_map/ppermute | solution.py:625
  74.4 1.2 collective-permute-start.23
  75.6 3.6 %unpair.6 = (bf16[2,1024,1792]{2,1,0:T(8,128)(2,1)S(1)}, f32[8,128]{1,0:T(8,128)S(1)}) custom-call(bf16[3584,2,1792]{2,1,0:T(2,128)(2,1)} %w_ref.11, bf16[32,1792]{1,0:T(8,128)(2,1)S(1)} %add_slot.4._), custom_call_target="tpu_custom_call" | custom-call | flops 1 | bytes 1 | tf_op jit(solution)/shard_map/unpair/pallas_call | solution.py:93
  79.2 2.1 %collective-permute-done.23.refs_0_ = bf16[32,1792]{1,0:T(8,128)(2,1)S(1)} collective-permute-done((bf16[32,1792]{1,0:T(8,128)(2,1)S(1)}, bf16[32,1792]{1,0:T(8,128)(2,1)S(1)}, u32[]{:S(2)}, u32[]{:S(2)}) %collective-permute-start.23) | collective-permute-done | bytes 114720 | tf_op jit(solution)/shard_map/ppermute | solution.py:625
  82.7 1.2 collective-permute-start.35
  84.7 1.3 collective-permute-start.30
  86.0 2.9 %unpair.7 = (bf16[2,768,1792]{2,1,0:T(8,128)(2,1)S(1)}, f32[8,128]{1,0:T(8,128)S(1)}) custom-call(bf16[3584,2,1792]{2,1,0:T(2,128)(2,1)} %w_ref.11, bf16[32,1792]{1,0:T(8,128)(2,1)S(1)} %get-tuple-element.55.refs_0_._), custom_call_target="tpu_custom_call" | custom-call | flops 1 | bytes 1 | tf_op jit(solution)/shard_map/unpair/pallas_call | solution.py:93
  88.9 3.5 %bring.2 = (bf16[1792,1792]{1,0:T(8,128)(2,1)S(1)}, f32[8,128]{1,0:T(8,128)S(1)}) custom-call(s32[3]{0:T(128)S(1)} %pad_add_fusion.place_ref, bf16[1792,3584]{1,0:T(8,128)(2,1)} %w_ref.13, bf16[32,1792]{1,0:T(8,128)(2,1)S(1)} %get-tuple-element.55.refs_0_._), custom_call_target="tpu_custom_call" | custom-call | flops 1 | bytes 1 | tf_op jit(solution)/shard_map/bring/pallas_call | solution.py:152
  92.4 2.6 %collective-permute-start.36 = (bf16[32,1792]{1,0:T(8,128)(2,1)S(1)}, bf16[32,1792]{1,0:T(8,128)(2,1)S(1)}, u32[]{:S(2)}, u32[]{:S(2)}) collective-permute-start(bf16[32,1792]{1,0:T(8,128)(2,1)S(1)} %pass_on.16.refs_13_), channel_id=1, source_target_pairs={{0,6},{1,7},{2,0},{3,1},{4,2},{5,3},{6,4},{7,5},{8,14},{9,15},{10,... | collective-permute-start | bytes 344072 | tf_op jit(solution)/shard_map/ppermute | solution.py:628
  95.7 3.4 %bring.3 = (bf16[1792,1792]{1,0:T(8,128)(2,1)S(1)}, f32[8,128]{1,0:T(8,128)S(1)}) custom-call(s32[3]{0:T(128)S(1)} %pad_add_fusion.place_ref, bf16[1792,3584]{1,0:T(8,128)(2,1)} %w_ref.13, bf16[32,1792]{1,0:T(8,128)(2,1)S(1)} %pass_on.14._.refs_4_), custom_call_target="tpu_custom_call" | custom-call | flops 1 | bytes 1 | tf_op jit(solution)/shard_map/bring/pallas_call | solution.py:152
  99.7 2.0 %collective-permute-done.33._refs_0_ = bf16[32,1792]{1,0:T(8,128)(2,1)S(1)} collective-permute-done((bf16[32,1792]{1,0:T(8,128)(2,1)S(1)}, bf16[32,1792]{1,0:T(8,128)(2,1)S(1)}, u32[]{:S(2)}, u32[]{:S(2)}) %collective-permute-start.33) | collective-permute-done | bytes 114720 | tf_op jit(solution)/shard_map/ppermute | solution.py:625
  103.7 10.1 %gate_up.1 = (bf16[256,1792]{1,0:T(8,128)(2,1)S(1)}, bf16[256,1792]{1,0:T(8,128)(2,1)S(1)}) custom-call(s32[3]{0:T(128)S(1)} %pad_add_fusion.place_ref, f32[3584]{0:T(1024)S(1)} %copy-done.3, bf16[32,1792]{1,0:T(8,128)(2,1)S(1)} %get-tuple-element.55.refs_0_._, bf16[32,1792]{1,0:T(8,128)(2,1)S(1)} %get-tuple-element.56.refs_1_, ...), custom_call_target="tpu_custom_call" | custom-call | flops 1 | bytes 1 | tf_op jit(solution)/shard_map/gate_up/pallas_call | solution.py:578
  114.2 1.8 %down_half.1 = f32[256,1792]{1,0:T(8,128)S(1)} custom-call(bf16[256,1792]{1,0:T(8,128)(2,1)S(1)} %get-tuple-element.65.x_ref, bf16[1792,1792]{1,0:T(8,128)(2,1)S(1)} %get-tuple-element.66.w_ref), custom_call_target="tpu_custom_call" | custom-call | flops 1 | bytes 1 | tf_op jit(solution)/shard_map/down_half/pallas_call | solution.py:601
  116.6 1.9 %collective-permute-start.45 = (bf16[32,1792]{1,0:T(8,128)(2,1)S(1)}, bf16[32,1792]{1,0:T(8,128)(2,1)S(1)}, u32[]{:S(2)}, u32[]{:S(2)}) collective-permute-start(bf16[32,1792]{1,0:T(8,128)(2,1)S(1)} %get-tuple-element.73), channel_id=1, source_target_pairs={{0,6},{1,7},{2,0},{3,1},{4,2},{5,3},{6,4},{7,5},{8,14},{9,15},{10,... | collective-permute-start | bytes 344072 | tf_op jit(solution)/shard_map/ppermute | solution.py:628
  118.5 2.0 %collective-permute-start.42 = (bf16[32,1792]{1,0:T(8,128)(2,1)S(1)}, bf16[32,1792]{1,0:T(8,128)(2,1)S(1)}, u32[]{:S(2)}, u32[]{:S(2)}) collective-permute-start(bf16[32,1792]{1,0:T(8,128)(2,1)S(1)} %get-tuple-element.75), channel_id=1, source_target_pairs={{0,2},{1,3},{2,4},{3,5},{4,6},{5,7},{6,0},{7,1},{8,10},{9,11},{10,... | collective-permute-start | bytes 344072 | tf_op jit(solution)/shard_map/ppermute | solution.py:625
  121.8 1.3 join.2.rest_0_
  123.1 1.7 %collective-permute-done.46.got_ref = bf16[32,1792]{1,0:T(8,128)(2,1)S(1)} collective-permute-done((bf16[32,1792]{1,0:T(8,128)(2,1)S(1)}, bf16[32,1792]{1,0:T(8,128)(2,1)S(1)}, u32[]{:S(2)}, u32[]{:S(2)}) %collective-permute-start.46) | collective-permute-done | bytes 114720 | tf_op jit(solution)/shard_map/ppermute | solution.py:628
  125.8 4.0 %collective-permute-start.47 = (bf16[32,1792]{1,0:T(8,128)(2,1)S(1)}, bf16[32,1792]{1,0:T(8,128)(2,1)S(1)}, u32[]{:S(2)}, u32[]{:S(2)}) collective-permute-start(bf16[32,1792]{1,0:T(8,128)(2,1)S(1)} %add_slot.7), channel_id=1, source_target_pairs={{0,6},{1,7},{2,0},{3,1},{4,2},{5,3},{6,4},{7,5},{8,14},{9,15},{10,... | collective-permute-start | bytes 344072 | tf_op jit(solution)/shard_map/ppermute | solution.py:628
  129.8 1.6 %collective-permute-start.44 = (bf16[32,1792]{1,0:T(8,128)(2,1)S(1)}, bf16[32,1792]{1,0:T(8,128)(2,1)S(1)}, u32[]{:S(2)}, u32[]{:S(2)}) collective-permute-start(bf16[32,1792]{1,0:T(8,128)(2,1)S(1)} %add_slot.6), channel_id=1, source_target_pairs={{0,2},{1,3},{2,4},{3,5},{4,6},{5,7},{6,0},{7,1},{8,10},{9,11},{10,... | collective-permute-start | bytes 344072 | tf_op jit(solution)/shard_map/ppermute | solution.py:625
  131.3 1.7 %collective-permute-done.47.refs_3_ = bf16[32,1792]{1,0:T(8,128)(2,1)S(1)} collective-permute-done((bf16[32,1792]{1,0:T(8,128)(2,1)S(1)}, bf16[32,1792]{1,0:T(8,128)(2,1)S(1)}, u32[]{:S(2)}, u32[]{:S(2)}) %collective-permute-start.47) | collective-permute-done | bytes 114720 | tf_op jit(solution)/shard_map/ppermute | solution.py:628
  133.1 3.3 %collective-permute-done.44.refs_0_ = bf16[32,1792]{1,0:T(8,128)(2,1)S(1)} collective-permute-done((bf16[32,1792]{1,0:T(8,128)(2,1)S(1)}, bf16[32,1792]{1,0:T(8,128)(2,1)S(1)}, u32[]{:S(2)}, u32[]{:S(2)}) %collective-permute-start.44) | collective-permute-done | bytes 114720 | tf_op jit(solution)/shard_map/ppermute | solution.py:625
  137.1 1.3 collective-permute-done.48.far_ref
  138.5 1.2 join.3
  (105 shorter events, 19.3 us)
Async XLA Ops:
  1.9 13.1 %collective-permute-start.1 = (bf16[32,3584]{1,0:T(8,128)(2,1)S(1)}, bf16[32,3584]{1,0:T(8,128)(2,1)S(1)}, u32[]{:S(2)}, u32[]{:S(2)}) collective-permute-start(bf16[32,3584]{1,0:T(8,128)(2,1)S(1)} %get-tuple-element.36._.refs_0_), channel_id=1, source_target_pairs={{0,2},{1,3},{2,4},{3,5},{4,6},{5,7},{6,0},{7,1},{8,10},{9,11},{10,... | collective-permute-start | bytes 688136 | tf_op jit(solution)/shard_map/ppermute | solution.py:625
  5.0 12.5 %collective-permute-start.5 = (bf16[32,3584]{1,0:T(8,128)(2,1)S(1)}, bf16[32,3584]{1,0:T(8,128)(2,1)S(1)}, u32[]{:S(2)}, u32[]{:S(2)}) collective-permute-start(bf16[32,3584]{1,0:T(8,128)(2,1)S(1)} %get-tuple-element.40.refs_0_), channel_id=1, source_target_pairs={{0,2},{1,3},{2,4},{3,5},{4,6},{5,7},{6,0},{7,1},{8,10},{9,11},{10,... | collective-permute-start | bytes 688136 | tf_op jit(solution)/shard_map/ppermute | solution.py:625
  6.6 21.4 %collective-permute-start.10 = (bf16[64,2,1792]{2,1,0:T(2,128)(2,1)}, bf16[64,2,1792]{2,1,0:T(2,128)(2,1)S(1)}, u32[]{:S(2)}, u32[]{:S(2)}) collective-permute-start(bf16[64,2,1792]{2,1,0:T(2,128)(2,1)} %bitcast.9), channel_id=1, source_target_pairs={{0,24},{8,16},{16,8},{24,0},{1,25},{9,17},{17,9},{25,1},{2,26},{10... | collective-permute-start | bytes 1376264 | tf_op jit(solution)/shard_map/ppermute | solution.py:725
  9.0 20.3 %collective-permute-start.8 = (bf16[64,2,1792]{2,1,0:T(2,128)(2,1)}, bf16[64,2,1792]{2,1,0:T(2,128)(2,1)S(1)}, u32[]{:S(2)}, u32[]{:S(2)}) collective-permute-start(bf16[64,2,1792]{2,1,0:T(2,128)(2,1)} %bitcast.10), channel_id=1, source_target_pairs={{0,8},{8,0},{16,24},{24,16},{1,9},{9,1},{17,25},{25,17},{2,10},{10... | collective-permute-start | bytes 1376264 | tf_op jit(solution)/shard_map/ppermute | solution.py:725
  9.6 19.8 %collective-permute-start.9 = (bf16[64,2,1792]{2,1,0:T(2,128)(2,1)}, bf16[64,2,1792]{2,1,0:T(2,128)(2,1)S(1)}, u32[]{:S(2)}, u32[]{:S(2)}) collective-permute-start(bf16[64,2,1792]{2,1,0:T(2,128)(2,1)} %bitcast.11), channel_id=1, source_target_pairs={{0,16},{8,24},{16,0},{24,8},{1,17},{9,25},{17,1},{25,9},{2,18},{10... | collective-permute-start | bytes 1376264 | tf_op jit(solution)/shard_map/ppermute | solution.py:725
  15.1 9.6 %collective-permute-start.3 = (bf16[32,3584]{1,0:T(8,128)(2,1)S(1)}, bf16[32,3584]{1,0:T(8,128)(2,1)S(1)}, u32[]{:S(2)}, u32[]{:S(2)}) collective-permute-start(bf16[32,3584]{1,0:T(8,128)(2,1)S(1)} %pass_on.9._.refs_2_), channel_id=1, source_target_pairs={{0,2},{1,3},{2,4},{3,5},{4,6},{5,7},{6,0},{7,1},{8,10},{9,11},{10,... | collective-permute-start | bytes 688136 | tf_op jit(solution)/shard_map/ppermute | solution.py:625
  17.6 10.3 %collective-permute-start.6 = (bf16[32,3584]{1,0:T(8,128)(2,1)S(1)}, bf16[32,3584]{1,0:T(8,128)(2,1)S(1)}, u32[]{:S(2)}, u32[]{:S(2)}) collective-permute-start(bf16[32,3584]{1,0:T(8,128)(2,1)S(1)} %pass_on.11.refs_2_), channel_id=1, source_target_pairs={{0,2},{1,3},{2,4},{3,5},{4,6},{5,7},{6,0},{7,1},{8,10},{9,11},{10,... | collective-permute-start | bytes 688136 | tf_op jit(solution)/shard_map/ppermute | solution.py:625
  27.9 20.6 %collective-permute-start.7 = (bf16[2,32,3584]{2,1,0:T(8,128)(2,1)S(1)}, bf16[2,32,3584]{2,1,0:T(8,128)(2,1)S(1)}, u32[]{:S(2)}, u32[]{:S(2)}) collective-permute-start(bf16[2,32,3584]{2,1,0:T(8,128)(2,1)S(1)} %stack.17), channel_id=1, source_target_pairs={{0,2},{1,3},{2,4},{3,5},{4,6},{5,7},{6,0},{7,1},{8,10},{9,11},{10,... | collective-permute-start | bytes 1376264 | tf_op jit(solution)/shard_map/ppermute | solution.py:625
  30.4 1.9 %collective-permute-start.11 = (bf16[4,2,224,64]{3,2,1,0:T(8,128)(2,1)S(1)}, bf16[4,2,224,64]{3,2,1,0:T(8,128)(2,1)S(1)}, u32[]{:S(2)}, u32[]{:S(2)}) collective-permute-start(bf16[4,2,224,64]{3,2,1,0:T(8,128)(2,1)S(1)} %get-tuple-element.42), channel_id=1, source_target_pairs={{0,1},{1,0},{2,3},{3,2},{4,5},{5,4},{6,7},{7,6},{8,9},{9,8},{10,11... | collective-permute-start | bytes 688136 | tf_op jit(solution)/shard_map/ppermute | solution.py:622
  30.5 27.7 %collective-permute-start.20 = (bf16[224,1792]{1,0:T(8,128)(2,1)S(1)}, bf16[224,1792]{1,0:T(8,128)(2,1)S(1)}, u32[]{:S(2)}, u32[]{:S(2)}) collective-permute-start(bf16[224,1792]{1,0:T(8,128)(2,1)S(1)} %get-tuple-element.52), channel_id=1, source_target_pairs={{0,1},{1,0},{2,3},{3,2},{4,5},{5,4},{6,7},{7,6},{8,9},{9,8},{10,11... | collective-permute-start | bytes 2408456 | tf_op jit(solution)/shard_map/ppermute | solution.py:622
  33.0 13.4 %collective-permute-start.12 = (bf16[2,224,128]{2,1,0:T(8,128)(2,1)S(1)}, bf16[2,224,128]{2,1,0:T(8,128)(2,1)S(1)}, u32[]{:S(2)}, u32[]{:S(2)}) collective-permute-start(bf16[2,224,128]{2,1,0:T(8,128)(2,1)S(1)} %get-tuple-element.43), channel_id=1, source_target_pairs={{0,2},{1,3},{2,0},{3,1},{4,6},{5,7},{6,4},{7,5},{8,10},{9,11},{10,... | collective-permute-start | bytes 344072 | tf_op jit(solution)/shard_map/ppermute | solution.py:717
  34.7 13.9 %collective-permute-start.13 = (bf16[2,224,128]{2,1,0:T(8,128)(2,1)S(1)}, bf16[2,224,128]{2,1,0:T(8,128)(2,1)S(1)}, u32[]{:S(2)}, u32[]{:S(2)}) collective-permute-start(bf16[2,224,128]{2,1,0:T(8,128)(2,1)S(1)} %get-tuple-element.44), channel_id=1, source_target_pairs={{0,4},{1,5},{2,6},{3,7},{4,0},{5,1},{6,2},{7,3},{8,12},{9,13},{10,... | collective-permute-start | bytes 344072 | tf_op jit(solution)/shard_map/ppermute | solution.py:717
  36.1 12.4 %collective-permute-start.14 = (bf16[2,224,128]{2,1,0:T(8,128)(2,1)S(1)}, bf16[2,224,128]{2,1,0:T(8,128)(2,1)S(1)}, u32[]{:S(2)}, u32[]{:S(2)}) collective-permute-start(bf16[2,224,128]{2,1,0:T(8,128)(2,1)S(1)} %get-tuple-element.45), channel_id=1, source_target_pairs={{0,6},{1,7},{2,4},{3,5},{4,2},{5,3},{6,0},{7,1},{8,14},{9,15},{10,... | collective-permute-start | bytes 344072 | tf_op jit(solution)/shard_map/ppermute | solution.py:717
  48.6 3.1 %collective-permute-start.15 = (bf16[2,32,3584]{2,1,0:T(8,128)(2,1)S(1)}, bf16[2,32,3584]{2,1,0:T(8,128)(2,1)S(1)}, u32[]{:S(2)}, u32[]{:S(2)}) collective-permute-start(bf16[2,32,3584]{2,1,0:T(8,128)(2,1)S(1)} %pass_on.13.refs_6_), channel_id=1, source_target_pairs={{0,1},{1,0},{2,3},{3,2},{4,5},{5,4},{6,7},{7,6},{8,9},{9,8},{10,11... | collective-permute-start | bytes 1376264 | tf_op jit(solution)/shard_map/ppermute | solution.py:622
  48.6 2.1 %collective-permute-start.16 = (bf16[32,3584]{1,0:T(8,128)(2,1)S(1)}, bf16[32,3584]{1,0:T(8,128)(2,1)S(1)}, u32[]{:S(2)}, u32[]{:S(2)}) collective-permute-start(bf16[32,3584]{1,0:T(8,128)(2,1)S(1)} %get-tuple-element.40.refs_0_), channel_id=1, source_target_pairs={{0,1},{1,0},{2,3},{3,2},{4,5},{5,4},{6,7},{7,6},{8,9},{9,8},{10,11... | collective-permute-start | bytes 688136 | tf_op jit(solution)/shard_map/ppermute | solution.py:622
  49.1 2.0 %collective-permute-start.17 = (bf16[32,3584]{1,0:T(8,128)(2,1)S(1)}, bf16[32,3584]{1,0:T(8,128)(2,1)S(1)}, u32[]{:S(2)}, u32[]{:S(2)}) collective-permute-start(bf16[32,3584]{1,0:T(8,128)(2,1)S(1)} %pass_on.11.refs_2_), channel_id=1, source_target_pairs={{0,1},{1,0},{2,3},{3,2},{4,5},{5,4},{6,7},{7,6},{8,9},{9,8},{10,11... | collective-permute-start | bytes 688136 | tf_op jit(solution)/shard_map/ppermute | solution.py:622
  49.2 2.2 %collective-permute-start.18 = (bf16[32,3584]{1,0:T(8,128)(2,1)S(1)}, bf16[32,3584]{1,0:T(8,128)(2,1)S(1)}, u32[]{:S(2)}, u32[]{:S(2)}) collective-permute-start(bf16[32,3584]{1,0:T(8,128)(2,1)S(1)} %pass_on.12.refs_0_.refs_4_), channel_id=1, source_target_pairs={{0,1},{1,0},{2,3},{3,2},{4,5},{5,4},{6,7},{7,6},{8,9},{9,8},{10,11... | collective-permute-start | bytes 688136 | tf_op jit(solution)/shard_map/ppermute | solution.py:622
  50.8 3.0 %collective-permute-start = (bf16[32,3584]{1,0:T(8,128)(2,1)S(1)}, bf16[32,3584]{1,0:T(8,128)(2,1)S(1)}, u32[]{:S(2)}, u32[]{:S(2)}) collective-permute-start(bf16[32,3584]{1,0:T(8,128)(2,1)S(1)} %get-tuple-element.36._.refs_0_), channel_id=1, source_target_pairs={{0,1},{1,0},{2,3},{3,2},{4,5},{5,4},{6,7},{7,6},{8,9},{9,8},{10,11... | collective-permute-start | bytes 688136 | tf_op jit(solution)/shard_map/ppermute | solution.py:622
  51.1 2.7 %collective-permute-start.2 = (bf16[32,3584]{1,0:T(8,128)(2,1)S(1)}, bf16[32,3584]{1,0:T(8,128)(2,1)S(1)}, u32[]{:S(2)}, u32[]{:S(2)}) collective-permute-start(bf16[32,3584]{1,0:T(8,128)(2,1)S(1)} %pass_on.9._.refs_2_), channel_id=1, source_target_pairs={{0,1},{1,0},{2,3},{3,2},{4,5},{5,4},{6,7},{7,6},{8,9},{9,8},{10,11... | collective-permute-start | bytes 688136 | tf_op jit(solution)/shard_map/ppermute | solution.py:622
  51.4 2.4 %collective-permute-start.4 = (bf16[32,3584]{1,0:T(8,128)(2,1)S(1)}, bf16[32,3584]{1,0:T(8,128)(2,1)S(1)}, u32[]{:S(2)}, u32[]{:S(2)}) collective-permute-start(bf16[32,3584]{1,0:T(8,128)(2,1)S(1)} %pass_on.10.refs_1_.refs_4_), channel_id=1, source_target_pairs={{0,1},{1,0},{2,3},{3,2},{4,5},{5,4},{6,7},{7,6},{8,9},{9,8},{10,11... | collective-permute-start | bytes 688136 | tf_op jit(solution)/shard_map/ppermute | solution.py:622
  57.8 1.4 %collective-permute-start.19 = (bf16[256,224]{1,0:T(8,128)(2,1)S(1)}, bf16[256,224]{1,0:T(8,128)(2,1)S(1)}, u32[]{:S(2)}, u32[]{:S(2)}) collective-permute-start(bf16[256,224]{1,0:T(8,128)(2,1)S(1)} %attend.1.a_ref), channel_id=1, source_target_pairs={{0,1},{1,0},{2,3},{3,2},{4,5},{5,4},{6,7},{7,6},{8,9},{9,8},{10,11... | collective-permute-start | bytes 344072 | tf_op jit(solution)/shard_map/ppermute | solution.py:622
  60.0 7.5 %collective-permute-start.24 = (bf16[32,1792]{1,0:T(8,128)(2,1)S(1)}, bf16[32,1792]{1,0:T(8,128)(2,1)S(1)}, u32[]{:S(2)}, u32[]{:S(2)}) collective-permute-start(bf16[32,1792]{1,0:T(8,128)(2,1)S(1)} %get-tuple-element.77), channel_id=1, source_target_pairs={{0,6},{1,7},{2,0},{3,1},{4,2},{5,3},{6,4},{7,5},{8,14},{9,15},{10,... | collective-permute-start | bytes 344072 | tf_op jit(solution)/shard_map/ppermute | solution.py:628
  60.1 9.0 %collective-permute-start.25 = (bf16[32,1792]{1,0:T(8,128)(2,1)S(1)}, bf16[32,1792]{1,0:T(8,128)(2,1)S(1)}, u32[]{:S(2)}, u32[]{:S(2)}) collective-permute-start(bf16[32,1792]{1,0:T(8,128)(2,1)S(1)} %get-tuple-element.76), channel_id=1, source_target_pairs={{0,6},{1,7},{2,0},{3,1},{4,2},{5,3},{6,4},{7,5},{8,14},{9,15},{10,... | collective-permute-start | bytes 344072 | tf_op jit(solution)/shard_map/ppermute | solution.py:628
  62.9 9.1 %collective-permute-start.21 = (bf16[32,1792]{1,0:T(8,128)(2,1)S(1)}, bf16[32,1792]{1,0:T(8,128)(2,1)S(1)}, u32[]{:S(2)}, u32[]{:S(2)}) collective-permute-start(bf16[32,1792]{1,0:T(8,128)(2,1)S(1)} %get-tuple-element.79._), channel_id=1, source_target_pairs={{0,2},{1,3},{2,4},{3,5},{4,6},{5,7},{6,0},{7,1},{8,10},{9,11},{10,... | collective-permute-start | bytes 344072 | tf_op jit(solution)/shard_map/ppermute | solution.py:625
  62.9 11.5 %collective-permute-start.22 = (bf16[32,1792]{1,0:T(8,128)(2,1)S(1)}, bf16[32,1792]{1,0:T(8,128)(2,1)S(1)}, u32[]{:S(2)}, u32[]{:S(2)}) collective-permute-start(bf16[32,1792]{1,0:T(8,128)(2,1)S(1)} %get-tuple-element.78), channel_id=1, source_target_pairs={{0,2},{1,3},{2,4},{3,5},{4,6},{5,7},{6,0},{7,1},{8,10},{9,11},{10,... | collective-permute-start | bytes 344072 | tf_op jit(solution)/shard_map/ppermute | solution.py:625
  69.1 10.0 %collective-permute-start.26 = (bf16[32,1792]{1,0:T(8,128)(2,1)S(1)}, bf16[32,1792]{1,0:T(8,128)(2,1)S(1)}, u32[]{:S(2)}, u32[]{:S(2)}) collective-permute-start(bf16[32,1792]{1,0:T(8,128)(2,1)S(1)} %add_slot.5), channel_id=1, source_target_pairs={{0,6},{1,7},{2,0},{3,1},{4,2},{5,3},{6,4},{7,5},{8,14},{9,15},{10,... | collective-permute-start | bytes 344072 | tf_op jit(solution)/shard_map/ppermute | solution.py:628
  74.4 6.9 %collective-permute-start.23 = (bf16[32,1792]{1,0:T(8,128)(2,1)S(1)}, bf16[32,1792]{1,0:T(8,128)(2,1)S(1)}, u32[]{:S(2)}, u32[]{:S(2)}) collective-permute-start(bf16[32,1792]{1,0:T(8,128)(2,1)S(1)} %add_slot.4._), channel_id=1, source_target_pairs={{0,2},{1,3},{2,4},{3,5},{4,6},{5,7},{6,0},{7,1},{8,10},{9,11},{10,... | collective-permute-start | bytes 344072 | tf_op jit(solution)/shard_map/ppermute | solution.py:625
  81.9 10.5 %collective-permute-start.34 = (bf16[32,1792]{1,0:T(8,128)(2,1)S(1)}, bf16[32,1792]{1,0:T(8,128)(2,1)S(1)}, u32[]{:S(2)}, u32[]{:S(2)}) collective-permute-start(bf16[32,1792]{1,0:T(8,128)(2,1)S(1)} %get-tuple-element.56.refs_1_), channel_id=1, source_target_pairs={{0,6},{1,7},{2,0},{3,1},{4,2},{5,3},{6,4},{7,5},{8,14},{9,15},{10,... | collective-permute-start | bytes 344072 | tf_op jit(solution)/shard_map/ppermute | solution.py:628
  82.7 9.7 %collective-permute-start.35 = (bf16[32,1792]{1,0:T(8,128)(2,1)S(1)}, bf16[32,1792]{1,0:T(8,128)(2,1)S(1)}, u32[]{:S(2)}, u32[]{:S(2)}) collective-permute-start(bf16[32,1792]{1,0:T(8,128)(2,1)S(1)} %get-tuple-element.55.refs_0_._), channel_id=1, source_target_pairs={{0,6},{1,7},{2,0},{3,1},{4,2},{5,3},{6,4},{7,5},{8,14},{9,15},{10,... | collective-permute-start | bytes 344072 | tf_op jit(solution)/shard_map/ppermute | solution.py:628
  83.9 11.1 %collective-permute-start.29 = (bf16[32,1792]{1,0:T(8,128)(2,1)S(1)}, bf16[32,1792]{1,0:T(8,128)(2,1)S(1)}, u32[]{:S(2)}, u32[]{:S(2)}) collective-permute-start(bf16[32,1792]{1,0:T(8,128)(2,1)S(1)} %get-tuple-element.55.refs_0_._), channel_id=1, source_target_pairs={{0,2},{1,3},{2,4},{3,5},{4,6},{5,7},{6,0},{7,1},{8,10},{9,11},{10,... | collective-permute-start | bytes 344072 | tf_op jit(solution)/shard_map/ppermute | solution.py:625
  84.7 10.3 %collective-permute-start.30 = (bf16[32,1792]{1,0:T(8,128)(2,1)S(1)}, bf16[32,1792]{1,0:T(8,128)(2,1)S(1)}, u32[]{:S(2)}, u32[]{:S(2)}) collective-permute-start(bf16[32,1792]{1,0:T(8,128)(2,1)S(1)} %get-tuple-element.56.refs_1_), channel_id=1, source_target_pairs={{0,2},{1,3},{2,4},{3,5},{4,6},{5,7},{6,0},{7,1},{8,10},{9,11},{10,... | collective-permute-start | bytes 344072 | tf_op jit(solution)/shard_map/ppermute | solution.py:625
  92.4 6.8 %collective-permute-start.36 = (bf16[32,1792]{1,0:T(8,128)(2,1)S(1)}, bf16[32,1792]{1,0:T(8,128)(2,1)S(1)}, u32[]{:S(2)}, u32[]{:S(2)}) collective-permute-start(bf16[32,1792]{1,0:T(8,128)(2,1)S(1)} %pass_on.16.refs_13_), channel_id=1, source_target_pairs={{0,6},{1,7},{2,0},{3,1},{4,2},{5,3},{6,4},{7,5},{8,14},{9,15},{10,... | collective-permute-start | bytes 344072 | tf_op jit(solution)/shard_map/ppermute | solution.py:628
  95.0 6.6 %collective-permute-start.33 = (bf16[32,1792]{1,0:T(8,128)(2,1)S(1)}, bf16[32,1792]{1,0:T(8,128)(2,1)S(1)}, u32[]{:S(2)}, u32[]{:S(2)}) collective-permute-start(bf16[32,1792]{1,0:T(8,128)(2,1)S(1)} %pass_on.14._.refs_4_), channel_id=1, source_target_pairs={{0,2},{1,3},{2,4},{3,5},{4,6},{5,7},{6,0},{7,1},{8,10},{9,11},{10,... | collective-permute-start | bytes 344072 | tf_op jit(solution)/shard_map/ppermute | solution.py:625
  95.1 6.6 %collective-permute-start.27 = (bf16[32,1792]{1,0:T(8,128)(2,1)S(1)}, bf16[32,1792]{1,0:T(8,128)(2,1)S(1)}, u32[]{:S(2)}, u32[]{:S(2)}) collective-permute-start(bf16[32,1792]{1,0:T(8,128)(2,1)S(1)} %get-tuple-element.55.refs_0_._), channel_id=1, source_target_pairs={{0,1},{1,0},{2,3},{3,2},{4,5},{5,4},{6,7},{7,6},{8,9},{9,8},{10,11... | collective-permute-start | bytes 344072 | tf_op jit(solution)/shard_map/ppermute | solution.py:622
  95.2 7.0 %collective-permute-start.28 = (bf16[32,1792]{1,0:T(8,128)(2,1)S(1)}, bf16[32,1792]{1,0:T(8,128)(2,1)S(1)}, u32[]{:S(2)}, u32[]{:S(2)}) collective-permute-start(bf16[32,1792]{1,0:T(8,128)(2,1)S(1)} %get-tuple-element.56.refs_1_), channel_id=1, source_target_pairs={{0,1},{1,0},{2,3},{3,2},{4,5},{5,4},{6,7},{7,6},{8,9},{9,8},{10,11... | collective-permute-start | bytes 344072 | tf_op jit(solution)/shard_map/ppermute | solution.py:622
  95.7 6.6 %collective-permute-start.40 = (bf16[32,1792]{1,0:T(8,128)(2,1)S(1)}, bf16[32,1792]{1,0:T(8,128)(2,1)S(1)}, u32[]{:S(2)}, u32[]{:S(2)}) collective-permute-start(bf16[32,1792]{1,0:T(8,128)(2,1)S(1)} %pass_on.16.refs_13_), channel_id=1, source_target_pairs={{0,1},{1,0},{2,3},{3,2},{4,5},{5,4},{6,7},{7,6},{8,9},{9,8},{10,11... | collective-permute-start | bytes 344072 | tf_op jit(solution)/shard_map/ppermute | solution.py:622
  99.2 3.5 %collective-permute-start.31 = (bf16[32,1792]{1,0:T(8,128)(2,1)S(1)}, bf16[32,1792]{1,0:T(8,128)(2,1)S(1)}, u32[]{:S(2)}, u32[]{:S(2)}) collective-permute-start(bf16[32,1792]{1,0:T(8,128)(2,1)S(1)} %pass_on.14._.refs_4_), channel_id=1, source_target_pairs={{0,1},{1,0},{2,3},{3,2},{4,5},{5,4},{6,7},{7,6},{8,9},{9,8},{10,11... | collective-permute-start | bytes 344072 | tf_op jit(solution)/shard_map/ppermute | solution.py:622
  101.7 1.5 %collective-permute-start.39 = (bf16[32,1792]{1,0:T(8,128)(2,1)S(1)}, bf16[32,1792]{1,0:T(8,128)(2,1)S(1)}, u32[]{:S(2)}, u32[]{:S(2)}) collective-permute-start(bf16[32,1792]{1,0:T(8,128)(2,1)S(1)} %collective-permute-done.35._refs_3_.refs_12_), channel_id=1, source_target_pairs={{0,1},{1,0},{2,3},{3,2},{4,5},{5,4},{6,7},{7,6},{8,9},{9,8},{10,11... | collective-permute-start | bytes 344072 | tf_op jit(solution)/shard_map/ppermute | solution.py:622
  102.2 1.3 collective-permute-start.38
  102.2 1.4 %collective-permute-start.37 = (bf16[32,1792]{1,0:T(8,128)(2,1)S(1)}, bf16[32,1792]{1,0:T(8,128)(2,1)S(1)}, u32[]{:S(2)}, u32[]{:S(2)}) collective-permute-start(bf16[32,1792]{1,0:T(8,128)(2,1)S(1)} %pass_on.15.refs_8_), channel_id=1, source_target_pairs={{0,1},{1,0},{2,3},{3,2},{4,5},{5,4},{6,7},{7,6},{8,9},{9,8},{10,11... | collective-permute-start | bytes 344072 | tf_op jit(solution)/shard_map/ppermute | solution.py:622
  113.8 2.5 %collective-permute-start.41 = (bf16[256,1792]{1,0:T(8,128)(2,1)S(1)}, bf16[256,1792]{1,0:T(8,128)(2,1)S(1)}, u32[]{:S(2)}, u32[]{:S(2)}) collective-permute-start(bf16[256,1792]{1,0:T(8,128)(2,1)S(1)} %get-tuple-element.67), channel_id=1, source_target_pairs={{0,1},{1,0},{2,3},{3,2},{4,5},{5,4},{6,7},{7,6},{8,9},{9,8},{10,11... | collective-permute-start | bytes 2752520 | tf_op jit(solution)/shard_map/ppermute | solution.py:622
  116.6 6.5 %collective-permute-start.45 = (bf16[32,1792]{1,0:T(8,128)(2,1)S(1)}, bf16[32,1792]{1,0:T(8,128)(2,1)S(1)}, u32[]{:S(2)}, u32[]{:S(2)}) collective-permute-start(bf16[32,1792]{1,0:T(8,128)(2,1)S(1)} %get-tuple-element.73), channel_id=1, source_target_pairs={{0,6},{1,7},{2,0},{3,1},{4,2},{5,3},{6,4},{7,5},{8,14},{9,15},{10,... | collective-permute-start | bytes 344072 | tf_op jit(solution)/shard_map/ppermute | solution.py:628
  118.4 6.3 %collective-permute-start.46 = (bf16[32,1792]{1,0:T(8,128)(2,1)S(1)}, bf16[32,1792]{1,0:T(8,128)(2,1)S(1)}, u32[]{:S(2)}, u32[]{:S(2)}) collective-permute-start(bf16[32,1792]{1,0:T(8,128)(2,1)S(1)} %get-tuple-element.72), channel_id=1, source_target_pairs={{0,6},{1,7},{2,0},{3,1},{4,2},{5,3},{6,4},{7,5},{8,14},{9,15},{10,... | collective-permute-start | bytes 344072 | tf_op jit(solution)/shard_map/ppermute | solution.py:628
  118.5 11.2 %collective-permute-start.42 = (bf16[32,1792]{1,0:T(8,128)(2,1)S(1)}, bf16[32,1792]{1,0:T(8,128)(2,1)S(1)}, u32[]{:S(2)}, u32[]{:S(2)}) collective-permute-start(bf16[32,1792]{1,0:T(8,128)(2,1)S(1)} %get-tuple-element.75), channel_id=1, source_target_pairs={{0,2},{1,3},{2,4},{3,5},{4,6},{5,7},{6,0},{7,1},{8,10},{9,11},{10,... | collective-permute-start | bytes 344072 | tf_op jit(solution)/shard_map/ppermute | solution.py:625
  120.5 9.3 %collective-permute-start.43 = (bf16[32,1792]{1,0:T(8,128)(2,1)S(1)}, bf16[32,1792]{1,0:T(8,128)(2,1)S(1)}, u32[]{:S(2)}, u32[]{:S(2)}) collective-permute-start(bf16[32,1792]{1,0:T(8,128)(2,1)S(1)} %get-tuple-element.74), channel_id=1, source_target_pairs={{0,2},{1,3},{2,4},{3,5},{4,6},{5,7},{6,0},{7,1},{8,10},{9,11},{10,... | collective-permute-start | bytes 344072 | tf_op jit(solution)/shard_map/ppermute | solution.py:625
  125.8 7.3 %collective-permute-start.47 = (bf16[32,1792]{1,0:T(8,128)(2,1)S(1)}, bf16[32,1792]{1,0:T(8,128)(2,1)S(1)}, u32[]{:S(2)}, u32[]{:S(2)}) collective-permute-start(bf16[32,1792]{1,0:T(8,128)(2,1)S(1)} %add_slot.7), channel_id=1, source_target_pairs={{0,6},{1,7},{2,0},{3,1},{4,2},{5,3},{6,4},{7,5},{8,14},{9,15},{10,... | collective-permute-start | bytes 344072 | tf_op jit(solution)/shard_map/ppermute | solution.py:628
  129.8 6.6 %collective-permute-start.44 = (bf16[32,1792]{1,0:T(8,128)(2,1)S(1)}, bf16[32,1792]{1,0:T(8,128)(2,1)S(1)}, u32[]{:S(2)}, u32[]{:S(2)}) collective-permute-start(bf16[32,1792]{1,0:T(8,128)(2,1)S(1)} %add_slot.6), channel_id=1, source_target_pairs={{0,2},{1,3},{2,4},{3,5},{4,6},{5,7},{6,0},{7,1},{8,10},{9,11},{10,... | collective-permute-start | bytes 344072 | tf_op jit(solution)/shard_map/ppermute | solution.py:625
  137.1 1.4 collective-permute-start.48
  (8 other events, 50.7 us)
